TPU v7x, 512 devices: a whole 4x8x8 slice. The times are simulated.
512 devices in a mesh: pages: 16 (over z, core), expert: 32 (over y, x).
Axes of the slice: x: 4, y: 8, z: 8, core: 2. Of those that a mesh axis runs over, the one named last changes fastest.
Arguments:
- queries: bfloat16 [247808, 576], P(('pages', 'expert')), may hold values from -6 to 6
- keys: bfloat16 [247808, 576], P(('pages', 'expert')), may hold values from -6 to 6
- values: bfloat16 [247808, 576], P(('pages', 'expert')), may hold values from -6 to 6
- resid: bfloat16 [247808, 576], P(('pages', 'expert')), may hold values from -6 to 6
- w_out: bfloat16 [576, 576], replicated, may hold values from -0.25 to 0.25
- w_merge: bfloat16 [2304, 1280], P(None, 'expert'), may hold values from -0.125 to 0.125
- rms_gain: float32 [1280], replicated, may hold values from 0.25 to 1.75
- w_gate: bfloat16 [32, 1280, 704], P('expert', 'pages'), may hold values from -0.15625 to 0.15625
- w_up: bfloat16 [32, 1280, 704], P('expert', 'pages'), may hold values from -0.15625 to 0.15625
- w_down: bfloat16 [32, 704, 1280], P('expert', None, 'pages'), may hold values from -0.21875 to 0.21875
- tile_count: int32 [16, 8], P('pages'), may hold values from 1 to 4, 20 in all within a row
- routes: int32 [61952, 6], P(('pages', 'expert')), may hold values from 0 to 31, all different within a row; in each aligned block of 121 rows (0 to 120, 121 to 241, ...) at most 30 rows name the same one
- route_weight: float32 [61952, 6], P(('pages', 'expert')), may hold values from 0.2 to 1
Outputs:
- layer_out: bfloat16 [61952, 1280], P(('pages', 'expert'))
Inputs may be any that keep to these rules, and one draw needn't show every extreme that they name: `tile_count`: each page has 1 to 4 tiles; a group's counts sum to 20. `routes`: A token names 6 different experts; within the 121 rows of one tile no expert is named more than 30 times, and in some tile's rows one expert is named exactly 30 times.
All inputs are finite; a program needn't handle non-finite values.
Results may differ from a plain program's by a relative error of at most 0.014.
Values may be sent and summed in bfloat16 or wider, within the bound.
No kernel may reach another device: no remote copies, remote signals or barrier semaphores. Data moves between devices by JAX's collectives and lax.ppermute only.
A program may use at most 128 MiB of HBM per device.

v0:
```python
import jax
import jax.numpy as jnp
from jax import lax
from jax.sharding import PartitionSpec as P

HEADS = 8
TS = 22
EXPERTS = 32
TOPK = 6
CAP = 30
MAXT = 4


def tile_attention(queries, keys, values, resid, w_out):
    patches = queries.shape[0]
    head_size = queries.shape[1] // HEADS
    q_heads = queries.reshape(patches, HEADS, head_size)
    k_heads = keys.reshape(patches, HEADS, head_size)
    v_heads = values.reshape(patches, HEADS, head_size)
    scores = jnp.einsum(
        "qhd,khd->hqk", q_heads, k_heads, preferred_element_type=jnp.float32
    ) * head_size ** (-0.5)
    top = jnp.max(scores, axis=-1, keepdims=True)
    weights = jnp.exp(scores - top)
    probs = (weights / jnp.sum(weights, axis=-1, keepdims=True)).astype(jnp.bfloat16)
    attended = jnp.einsum(
        "hqk,khd->qhd", probs, v_heads, preferred_element_type=jnp.float32
    ).astype(jnp.bfloat16)
    update = jnp.dot(attended.reshape(patches, -1), w_out, preferred_element_type=jnp.float32)
    return (resid.astype(jnp.float32) + update).astype(jnp.bfloat16)


def space_to_depth(vis):
    half = TS // 2
    width = vis.shape[1]
    grid = vis.reshape(half, 2, half, 2, width).transpose(0, 2, 1, 3, 4)
    return grid.reshape(half * half, 4 * width)


def slot_targets(route_block):
    flat = route_block.reshape(-1)
    onehot = (flat[:, None] == jnp.arange(EXPERTS, dtype=jnp.int32)[None, :]).astype(jnp.int32)
    before = jnp.cumsum(onehot, axis=0) - onehot
    return flat * CAP + jnp.sum(before * onehot, axis=1)


def local(
    queries,
    keys,
    values,
    resid,
    w_out,
    w_merge,
    rms_gain,
    w_gate,
    w_up,
    w_down,
    tile_count,
    routes,
    route_weight,
):
    position = lax.axis_index("expert")
    page = position // MAXT
    count = lax.dynamic_index_in_dim(tile_count[0], page, keepdims=False)
    live = position % MAXT < count
    vis = tile_attention(queries, keys, values, resid, w_out)
    merged = jnp.where(live, space_to_depth(vis), jnp.zeros((), jnp.bfloat16))
    product = jnp.dot(
        merged,
        lax.all_gather(w_merge, "expert", axis=1, tiled=True),
        preferred_element_type=jnp.float32,
    )
    stream = jax.nn.gelu(product, approximate=False).astype(jnp.bfloat16)
    wide = stream.astype(jnp.float32)
    normed = (
        wide * lax.rsqrt(jnp.mean(wide * wide, axis=-1, keepdims=True) + 1e-06) * rms_gain
    ).astype(jnp.bfloat16)
    tokens = normed.shape[0]
    target = slot_targets(routes)
    table = (jnp.arange(EXPERTS * CAP, dtype=jnp.int32)[:, None] == target[None, :]).astype(
        jnp.float32
    )
    table = jnp.sum(table.reshape(EXPERTS * CAP, tokens, TOPK), axis=2).astype(jnp.bfloat16)
    send = jnp.dot(table, normed, preferred_element_type=jnp.float32).astype(jnp.bfloat16)
    send = send.reshape(EXPERTS, CAP, normed.shape[1])
    received = lax.all_to_all(send, "expert", split_axis=0, concat_axis=1, tiled=True)
    gate_part = jnp.einsum(
        "erd,edh->erh",
        received,
        lax.all_gather(w_gate, "pages", axis=1, tiled=True),
        preferred_element_type=jnp.float32,
    )
    up_part = jnp.einsum(
        "erd,edh->erh",
        received,
        lax.all_gather(w_up, "pages", axis=1, tiled=True),
        preferred_element_type=jnp.float32,
    )
    act = (jax.nn.silu(gate_part) * up_part).astype(jnp.bfloat16)
    outcome = jnp.einsum(
        "erh,ehd->erd",
        act,
        lax.all_gather(w_down, "pages", axis=2, tiled=True),
        preferred_element_type=jnp.float32,
    ).astype(jnp.bfloat16)
    back = lax.all_to_all(outcome, "expert", split_axis=1, concat_axis=0, tiled=True)
    picked = back.reshape(EXPERTS * CAP, -1)[target].reshape(tokens, TOPK, -1)
    total = wide + jnp.sum(route_weight[:, :, None] * picked.astype(jnp.float32), axis=1)
    return total.astype(jnp.bfloat16)


def solution(mesh):
    return jax.shard_map(
        local,
        mesh=mesh,
        in_specs=(
            P(("pages", "expert"), None),
            P(("pages", "expert"), None),
            P(("pages", "expert"), None),
            P(("pages", "expert"), None),
            P(),
            P(None, "expert"),
            P(),
            P("expert", "pages", None),
            P("expert", "pages", None),
            P("expert", None, "pages"),
            P("pages", None),
            P(("pages", "expert"), None),
            P(("pages", "expert"), None),
        ),
        out_specs=P(("pages", "expert"), None),
        check_vma=False,
    )
```

profile of v0, /device:TPU:1, one launch (start us, length us, event | category | flops | bytes accessed | tf_op | source)
XLA Modules:
  0.0 364.3 jit_solution(10380909858349089428)
XLA Ops:
  6.5 0.7 all-gather.5.cloned.1.call-update
  7.3 0.0 all-gather.9.cloned.1.call-start
  7.3 0.7 all-gather.9.cloned.1.call-update
  8.0 0.0 all-gather.11.cloned.1.call-start
  8.1 0.7 all-gather.11.cloned.1.call-update
  8.8 1.2 constant_dynamic-slice_fusion
  10.7 7.2 %fusion.46 = (f32[8,484]{1,0:T(8,128)S(1)}, f32[8,484,484]{1,2,0:T(8,128)}) fusion(bf16[484,8,72]{0,2,1:T(8,128)(2,1)} %bitcast.60, bf16[484,8,72]{0,2,1:T(8,128)(2,1)} %bitcast.61), kind=kOutput, calls=%fused_computation.74 | convolution fusion | flops 275485536 | bytes 8626816 | tf_op jit(solution)/shard_map/sub | solution.py:24
  17.8 4.1 %fusion.15 = bf16[8,484,72]{1,2,0:T(8,128)(2,1)S(1)} fusion(bf16[484,8,72]{0,2,1:T(8,128)(2,1)S(1)} %bitcast.62, f32[8,484,484]{1,2,0:T(8,128)} %get-tuple-element.10, f32[8,484]{1,0:T(8,128)S(1)} %get-tuple-element.9), kind=kOutput, calls=%fused_computation.23 | convolution fusion | flops 273889792 | bytes 8626816 | tf_op jit(solution)/shard_map/hqk,khd->qhd/dot_general | solution.py:26
  22.0 0.7 fusion.16
  22.7 0.3 copy.44
  23.0 0.8 select_n.47
  23.8 0.4 copy.45
  24.3 1.1 select_n.49
  25.4 0.1 copy.47
  25.5 0.1 eq.39
  25.7 1.7 reduce-window.6
  27.4 0.3 slice_reduce_fusion
  27.7 0.1 bitcast_bitcast_fusion
  27.9 0.1 reduce_sum.51
  28.0 0.1 copy.51
  28.1 0.4 convert_reduce_fusion
  28.5 78.0 %all-gather.5.cloned.1.call-done = bf16[2304,1280]{0,1:T(8,128)(2,1)} async-done(((bf16[2304,40]{0,1:T(8,128)(2,1)}), bf16[2304,1280]{0,1:T(8,128)(2,1)}) %all-gather.5.cloned.1.call-update) | async-done | bytes 5898256 | tf_op jit(solution)/shard_map/all_gather | solution.py:70
  106.6 5.9 %fusion.24 = (f32[121]{0:T(128)S(1)}, bf16[121,1280]{1,0:T(8,128)(2,1)S(1)}) fusion(bf16[121,2304]{1,0:T(8,128)(2,1)S(1)} %select_n.49, bf16[2304,1280]{0,1:T(8,128)(2,1)} %all-gather.5.cloned.1.call-done), kind=kOutput, calls=%fused_computation.33 | convolution fusion | flops 724218752 | bytes 6766052 | tf_op jit(solution)/shard_map/dot_general | solution.py:68
  112.5 0.9 convolution_convert_fusion.1
  113.4 2.3 reshape.142
  115.6 6.4 %all-to-all-start = ((bf16[32,30,1280]{2,1,0:T(8,128)(2,1)}), bf16[32,30,1280]{2,1,0:T(8,128)(2,1)S(1)}, u32[]{:S(2)}, u32[]{:S(2)}) async-start(bf16[32,30,1280]{2,1,0:T(8,128)(2,1)} %reshape.142), calls=%async_computation | async-start | bytes 5242880 | tf_op jit(solution)/shard_map/all_to_all | solution.py:86
  122.0 0.2 all-gather.7.cloned.1.call-start
  122.2 0.3 all-gather.7.cloned.1.call-update
  122.6 58.4 %all-to-all-done = bf16[32,30,1280]{2,1,0:T(8,128)(2,1)S(1)} async-done(((bf16[32,30,1280]{2,1,0:T(8,128)(2,1)}), bf16[32,30,1280]{2,1,0:T(8,128)(2,1)S(1)}, u32[]{:S(2)}, u32[]{:S(2)}) %all-to-all-start) | async-done | bytes 2457632 | tf_op jit(solution)/shard_map/all_to_all | solution.py:86
  181.0 2.2 reshape.143
  183.2 6.0 %fusion.8 = f32[960,704]{0,1:T(8,128)} fusion(bf16[960,1280]{1,0:T(8,128)(2,1)} %reshape.143, bf16[1,1280,704]{2,1,0:T(8,128)(2,1)} %all-gather.9.cloned.1.call-done), kind=kOutput, calls=%fused_computation.17 | convolution fusion | flops 1730150400 | bytes 6963200 | tf_op jit(solution)/shard_map/erd,edh->erh/dot_general | solution.py:93
  189.1 5.5 %all-gather.11.cloned.1.call-done = bf16[1,704,1280]{1,2,0:T(8,128)(2,1)} async-done(((bf16[1,704,80]{1,2,0:T(8,128)(2,1)}), bf16[1,704,1280]{1,2,0:T(8,128)(2,1)}) %all-gather.11.cloned.1.call-update) | async-done | bytes 1802256 | tf_op jit(solution)/shard_map/all_gather | solution.py:103
  194.6 42.8 %all-gather.7.cloned.1.call-done = bf16[1,1280,704]{2,1,0:T(8,128)(2,1)} async-done(((bf16[1,80,704]{2,1,0:T(8,128)(2,1)}), bf16[1,1280,704]{2,1,0:T(8,128)(2,1)}) %all-gather.7.cloned.1.call-update) | async-done | bytes 1802256 | tf_op jit(solution)/shard_map/all_gather | solution.py:90
  237.4 8.2 %fusion.6 = bf16[1,960,1280]{2,1,0:T(8,128)(2,1)S(1)} fusion(bf16[1,704,1280]{1,2,0:T(8,128)(2,1)} %all-gather.11.cloned.1.call-done, f32[960,704]{0,1:T(8,128)} %fusion.8, bf16[960,1280]{1,0:T(8,128)(2,1)} %reshape.143, bf16[1,1280,704]{2,1,0:T(8,128)(2,1)} %all-gather.7.cloned.1.call-done), kind=kOutput, calls=%fused_computation.11 | convolution fusion | flops 3465584640 | bytes 11223040 | tf_op jit(solution)/shard_map/erh,ehd->erd/dot_general | solution.py:100
  245.6 6.0 %copy.62 = bf16[1,960,1280]{2,0,1:T(2,128)(2,1)} copy(bf16[1,960,1280]{2,1,0:T(8,128)(2,1)S(1)} %fusion.6) | data formatting | bytes 4915200 | tf_op jit(solution)/shard_map/convert_element_type | solution.py:105
  251.6 0.5 broadcast.93
  252.1 15.6 %reduce.4 = bf16[960,1280]{1,0:T(8,128)(2,1)S(1)} reduce(bf16[960,1,1280]{2,1,0:T(2,128)(2,1)} %bitcast.57, bf16[]{:T(256)} %broadcast.93), dimensions={1}, to_apply=%bitcast.53.reduce_sub_computation | reduce | bytes 4915202
  267.6 2.2 reshape.160
  269.9 9.4 %all-to-all-start.1 = ((bf16[32,2,19200]{2,1,0:T(2,128)(2,1)}), bf16[32,2,19200]{2,1,0:T(2,128)(2,1)S(1)}, u32[]{:S(2)}, u32[]{:S(2)}) async-start(bf16[32,2,19200]{2,1,0:T(2,128)(2,1)} %reshape.160), calls=%async_computation.1 | async-start | bytes 4915200 | tf_op jit(solution)/shard_map/all_to_all | solution.py:106
  279.3 0.1 mul.98
  279.4 0.1 copy.46
  279.6 55.6 %all-to-all-done.1 = bf16[32,2,19200]{2,1,0:T(2,128)(2,1)S(1)} async-done(((bf16[32,2,19200]{2,1,0:T(2,128)(2,1)}), bf16[32,2,19200]{2,1,0:T(2,128)(2,1)S(1)}, u32[]{:S(2)}, u32[]{:S(2)}) %all-to-all-start.1) | async-done | bytes 2457632 | tf_op jit(solution)/shard_map/all_to_all | solution.py:106
  335.2 6.9 %reshape.161 = bf16[960,1,1280]{2,1,0:T(2,128)(2,1)} reshape(bf16[32,2,19200]{2,1,0:T(2,128)(2,1)S(1)} %all-to-all-done.1) | data formatting | bytes 4915200
  342.0 2.8 copy.61
  344.8 3.7 %gather_fusion = bf16[726,1280]{1,0:T(8,128)(2,1)} fusion(bf16[960,1280]{1,0:T(8,128)(2,1)S(1)} %bitcast.55, s32[1024]{0:T(1024)S(1)} %pad_clamp_fusion), kind=kCustom, calls=%fused_computation | custom fusion | bytes 3720024 | tf_op jit(solution)/shard_map/gather | solution.py:107
  348.5 4.4 %reshape.149 = f32[121,6,1280]{2,1,0:T(8,128)} reshape(bf16[726,1280]{1,0:T(8,128)(2,1)} %gather_fusion) | data formatting | bytes 5575680 | tf_op jit(solution)/shard_map/convert_element_type | solution.py:108
  352.9 4.0 %multiply_reduce_fusion.1 = f32[121,1280]{1,0:T(8,128)S(1)} fusion(f32[121,6,1280]{2,1,0:T(8,128)} %reshape.149, f32[121,6]{1,0:T(8,128)S(1)} %copy.46), kind=kLoop, calls=%fused_computation.6 | loop fusion | flops 1703680 | bytes 4339544 | tf_op jit(solution)/shard_map/reduce_sum | solution.py:108
  356.9 0.8 fusion.27
  (28 shorter events, 0.2 us)
Async XLA Ops:
  6.5 15.5 %copy-start = (bf16[576,576]{1,0:T(8,128)(2,1)S(1)}, bf16[576,576]{1,0:T(8,128)(2,1)}, u32[]{:S(2)}) copy-start(bf16[576,576]{1,0:T(8,128)(2,1)} %param.17) | copy-start | bytes 1990660
  6.5 100.0 %all-gather.5.cloned.1.call-start = ((), (), s32[]{:S(2)}) async-start(), calls=%async_computation.2 | async-start | bytes 6082560 | tf_op jit(solution)/shard_map/all_gather | solution.py:70
  7.3 175.9 %all-gather.9.cloned.1.call-start = ((), (), s32[]{:S(2)}) async-start(), calls=%async_computation.4 | async-start | bytes 2088960 | tf_op jit(solution)/shard_map/all_gather | solution.py:96
  8.0 186.6 %all-gather.11.cloned.1.call-start = ((), (), s32[]{:S(2)}) async-start(), calls=%async_computation.5 | async-start | bytes 2088960 | tf_op jit(solution)/shard_map/all_gather | solution.py:103
  10.7 7.2 %copy-start.7 = (bf16[484,576]{0,1:T(8,128)(2,1)S(1)}, bf16[484,576]{0,1:T(8,128)(2,1)}, u32[]{:S(2)}) copy-start(bf16[484,576]{0,1:T(8,128)(2,1)} %param.15) | copy-start | bytes 1672708
  17.8 4.2 %copy-start.8 = (bf16[484,576]{0,1:T(8,128)(2,1)S(1)}, bf16[484,576]{0,1:T(8,128)(2,1)}, u32[]{:S(2)}) copy-start(bf16[484,576]{0,1:T(8,128)(2,1)} %param.16) | copy-start | bytes 1672708
  22.7 2.7 copy-start.5
  28.5 84.0 %copy-start.4 = (f32[1280]{0:T(1024)S(1)}, f32[1280]{0:T(1024)}, u32[]{:S(2)}) copy-start(f32[1280]{0:T(1024)} %param.19) | copy-start | bytes 15364
  112.5 3.2 copy-start.2
  115.6 65.3 %all-to-all-start = ((bf16[32,30,1280]{2,1,0:T(8,128)(2,1)}), bf16[32,30,1280]{2,1,0:T(8,128)(2,1)S(1)}, u32[]{:S(2)}, u32[]{:S(2)}) async-start(bf16[32,30,1280]{2,1,0:T(8,128)(2,1)} %reshape.142), calls=%async_computation | async-start | bytes 5242880 | tf_op jit(solution)/shard_map/all_to_all | solution.py:86
  122.0 115.4 %all-gather.7.cloned.1.call-start = ((), (), s32[]{:S(2)}) async-start(), calls=%async_computation.3 | async-start | bytes 2088960 | tf_op jit(solution)/shard_map/all_gather | solution.py:90
  269.9 9.5 %copy-start.6 = (f32[121,6]{0,1:T(8,128)S(1)}, f32[121,6]{0,1:T(8,128)}, u32[]{:S(2)}) copy-start(f32[121,6]{0,1:T(8,128)} %param.25) | copy-start | bytes 8716
  269.9 65.3 %all-to-all-start.1 = ((bf16[32,2,19200]{2,1,0:T(2,128)(2,1)}), bf16[32,2,19200]{2,1,0:T(2,128)(2,1)S(1)}, u32[]{:S(2)}, u32[]{:S(2)}) async-start(bf16[32,2,19200]{2,1,0:T(2,128)(2,1)} %reshape.160), calls=%async_computation.1 | async-start | bytes 4915200 | tf_op jit(solution)/shard_map/all_to_all | solution.py:106
  348.5 9.2 %copy-start.1 = (bf16[576,576]{1,0:T(8,128)(2,1)S(1)}, bf16[576,576]{1,0:T(8,128)(2,1)}, u32[]{:S(2)}) copy-start(bf16[576,576]{1,0:T(8,128)(2,1)} %param.17) | copy-start | bytes 1990660
  352.9 4.0 %copy-start.3 = (bf16[121,1280]{1,0:T(8,128)(2,1)S(1)}, bf16[121,1280]{1,0:T(8,128)(2,1)}, u32[]{:S(2)}) copy-start(bf16[121,1280]{1,0:T(8,128)(2,1)} %copy-done.2) | copy-start | bytes 929284
Sparse Core Ops, SparseCore 0:
  10.5 95.9 all-gather.4
  108.7 42.6 all-gather.8
  153.6 40.9 all-gather.10
  196.6 40.8 all-gather.6
where the time goes:
time: 366 us; the launch traced here: 364 us
  waiting for transfers between devices  243 us (66%)
  local copies, waits for them, and re-layouts  35.8 us (10%)
  matrix products  32.9 us (9%)
  other arithmetic  22.8 us (6%)
  starting transfers between devices  16.1 us (4%)
  between operations  14.1 us (4%)
    all_gather x1, waiting for transfers between devices, local(): lax.all_gather(w_merge, 'expert', axis=1, tiled=True)  78 us
    all_to_all x1, waiting for transfers between devices, local(): lax.all_to_all(send, 'expert', split_axis=0, concat_axis=1, tiled=True)  58.4 us
    all_to_all x1, waiting for transfers between devices, local(): lax.all_to_all(outcome, 'expert', split_axis=1, concat_axis=0, tiled=True)  55.6 us
    all_gather x1, waiting for transfers between devices, local(): lax.all_gather(w_gate, 'pages', axis=1, tiled=True)  42.8 us
    unnamed x1, other arithmetic  15.6 us
    unnamed x24, local copies, waits for them, and re-layouts  12.7 us
    all_to_all x1, starting transfers between devices, local(): lax.all_to_all(outcome, 'expert', split_axis=1, concat_axis=0, tiled=True)  9.39 us
    dot_general x1, matrix products, local(): jnp.einsum('erh,ehd->erd', act, lax.all_gather(w_down, 'pages', axis=2, t...  8.16 us
  transfers between devices with their start and end apart: 6, of which 5 were waited for; matrix products, arithmetic and copies ran while one was open for 10% of the time, Pallas kernels for 0%

commit v1 on v0

v1 whole, which is shorter than its diff:
```python
import functools
import jax
import jax.numpy as jnp
from jax import lax
from jax.experimental import pallas as pl
from jax.experimental.pallas import tpu as pltpu
from jax.sharding import Mesh
from jax.sharding import PartitionSpec as P

HEADS = 8
TS = 22
EXPERTS = 32
TOPK = 6
MAXT = 4
SLOT = 32
TPAD = 128


def tile_attention(queries, keys, values, resid, w_out):
    patches = queries.shape[0]
    head_size = queries.shape[1] // HEADS
    q_heads = queries.reshape(patches, HEADS, head_size)
    k_heads = keys.reshape(patches, HEADS, head_size)
    v_heads = values.reshape(patches, HEADS, head_size)
    scores = jnp.einsum(
        "qhd,khd->hqk", q_heads, k_heads, preferred_element_type=jnp.float32
    ) * head_size ** (-0.5)
    top = jnp.max(scores, axis=-1, keepdims=True)
    weights = jnp.exp(scores - top)
    probs = (weights / jnp.sum(weights, axis=-1, keepdims=True)).astype(jnp.bfloat16)
    attended = jnp.einsum(
        "hqk,khd->qhd", probs, v_heads, preferred_element_type=jnp.float32
    ).astype(jnp.bfloat16)
    update = jnp.dot(attended.reshape(patches, -1), w_out, preferred_element_type=jnp.float32)
    return (resid.astype(jnp.float32) + update).astype(jnp.bfloat16)


def space_to_depth(vis):
    half = TS // 2
    width = vis.shape[1]
    grid = vis.reshape(half, 2, half, 2, width).transpose(0, 2, 1, 3, 4)
    return grid.reshape(half * half, 4 * width)


def slot_tables(routes, route_weight):
    tokens = routes.shape[0]
    routes = jnp.pad(routes, ((0, TPAD - tokens), (0, 0)), constant_values=-1)
    route_weight = jnp.pad(route_weight, ((0, TPAD - tokens), (0, 0)))
    hit = routes.T[:, None, :] == jnp.arange(EXPERTS, dtype=jnp.int32)[None, :, None]
    member = jnp.any(hit, axis=0)
    weight = jnp.sum(jnp.where(hit, route_weight.T[:, None, :], 0.0), axis=0)
    earlier = jnp.triu(jnp.ones((TPAD, TPAD), jnp.bfloat16), 1)
    before = jnp.dot(
        member.astype(jnp.bfloat16), earlier, preferred_element_type=jnp.float32
    ).astype(jnp.int32)
    place = jnp.where(member, before, -1)
    table = place[:, None, :] == jnp.arange(SLOT, dtype=jnp.int32)[None, :, None]
    high = weight.astype(jnp.bfloat16)
    low = (weight - high.astype(jnp.float32)).astype(jnp.bfloat16)
    zero = jnp.zeros((), jnp.bfloat16)
    rows = EXPERTS * SLOT
    return (
        table.astype(jnp.bfloat16).reshape(rows, TPAD),
        jnp.where(table, high[:, None, :], zero).reshape(rows, TPAD),
        jnp.where(table, low[:, None, :], zero).reshape(rows, TPAD),
    )


def merge_body(merged_ref, weight_ref, table_ref, stream_ref, send_ref):
    half = weight_ref.shape[2]
    dims = (((1,), (1,)), ((), ()))
    product = lax.dot_general(
        merged_ref[:, :half], weight_ref[0], dims, preferred_element_type=jnp.float32
    ) + lax.dot_general(
        merged_ref[:, half:], weight_ref[1], dims, preferred_element_type=jnp.float32
    )
    gelu = 0.5 * product * (1.0 + lax.erf(product * (0.5**0.5)))
    stream = gelu.astype(jnp.bfloat16)
    stream_ref[...] = stream
    rows = jnp.dot(table_ref[...], stream, preferred_element_type=jnp.float32)
    send_ref[...] = rows.astype(jnp.bfloat16).reshape(send_ref.shape)


def merge_dispatch(merged, weight, table):
    width = weight.shape[1]
    block = 256
    return pl.pallas_call(
        merge_body,
        grid=(width // block,),
        in_specs=[
            pl.BlockSpec(merged.shape, lambda i: (0, 0)),
            pl.BlockSpec((2, block, weight.shape[2]), lambda i: (0, i, 0)),
            pl.BlockSpec(table.shape, lambda i: (0, 0)),
        ],
        out_specs=[
            pl.BlockSpec((TPAD, block), lambda i: (0, i)),
            pl.BlockSpec((EXPERTS, SLOT, block), lambda i: (0, 0, i)),
        ],
        out_shape=[
            jax.ShapeDtypeStruct((TPAD, width), jnp.bfloat16),
            jax.ShapeDtypeStruct((EXPERTS, SLOT, width), jnp.bfloat16),
        ],
        compiler_params=pltpu.CompilerParams(vmem_limit_bytes=40 << 20),
        cost_estimate=pl.CostEstimate(
            flops=2 * TPAD * width * (merged.shape[1] + EXPERTS * SLOT),
            bytes_accessed=10 << 20,
            transcendentals=TPAD * width,
        ),
        name="merge_dispatch",
    )(merged, weight, table)


def expert_body(hidden, rows_ref, gain_ref, weight_ref, out_ref):
    wide = rows_ref[...].astype(jnp.float32)
    scale = lax.rsqrt(jnp.mean(wide * wide, axis=-1, keepdims=True) + 1e-06)
    normed = (wide * scale * gain_ref[...]).astype(jnp.bfloat16)
    both = jnp.dot(normed, weight_ref[:, : 2 * hidden], preferred_element_type=jnp.float32)
    gate = both[:, :hidden]
    up = both[:, hidden:]
    act = (gate / (1.0 + jnp.exp(-gate)) * up).astype(jnp.bfloat16)
    out_ref[...] = lax.dot_general(
        act,
        weight_ref[:, 2 * hidden :],
        (((1,), (1,)), ((), ())),
        preferred_element_type=jnp.float32,
    ).astype(jnp.bfloat16)


def expert_ffn(rows, gain, weight):
    count, width = rows.shape
    hidden = weight.shape[1] // 3
    block = 256
    return pl.pallas_call(
        functools.partial(expert_body, hidden),
        grid=(count // block,),
        in_specs=[
            pl.BlockSpec((block, width), lambda i: (i, 0)),
            pl.BlockSpec((1, width), lambda i: (0, 0)),
            pl.BlockSpec(weight.shape, lambda i: (0, 0)),
        ],
        out_specs=pl.BlockSpec((block, width), lambda i: (i, 0)),
        out_shape=jax.ShapeDtypeStruct((count, width), jnp.bfloat16),
        compiler_params=pltpu.CompilerParams(vmem_limit_bytes=48 << 20),
        cost_estimate=pl.CostEstimate(
            flops=6 * count * width * hidden,
            bytes_accessed=11 << 20,
            transcendentals=count * hidden,
        ),
        name="expert_ffn",
    )(rows, gain, weight)


def combine_body(stream_ref, high_ref, low_ref, back_ref, out_ref):
    dims = (((0,), (0,)), ((), ()))
    back = back_ref[...]
    total = lax.dot_general(
        high_ref[...], back, dims, preferred_element_type=jnp.float32
    ) + lax.dot_general(low_ref[...], back, dims, preferred_element_type=jnp.float32)
    total = total + stream_ref[...].astype(jnp.float32)
    out_ref[...] = total[: out_ref.shape[0]].astype(jnp.bfloat16)


def combine(stream, high, low, back, tokens):
    width = stream.shape[1]
    block = 256
    whole = lambda i: (0, 0)
    column = lambda i: (0, i)
    return pl.pallas_call(
        combine_body,
        grid=(width // block,),
        in_specs=[
            pl.BlockSpec((TPAD, block), column),
            pl.BlockSpec(high.shape, whole),
            pl.BlockSpec(low.shape, whole),
            pl.BlockSpec((back.shape[0], block), column),
        ],
        out_specs=pl.BlockSpec((tokens, block), column),
        out_shape=jax.ShapeDtypeStruct((tokens, width), jnp.bfloat16),
        compiler_params=pltpu.CompilerParams(vmem_limit_bytes=40 << 20),
        cost_estimate=pl.CostEstimate(
            flops=4 * TPAD * width * back.shape[0],
            bytes_accessed=4 << 20,
            transcendentals=0,
        ),
        name="combine",
    )(stream, high, low, back)


def local(
    queries,
    keys,
    values,
    resid,
    w_out,
    w_merge,
    rms_gain,
    w_gate,
    w_up,
    w_down,
    tile_count,
    routes,
    route_weight,
):
    tokens = routes.shape[0]
    position = lax.axis_index("y") * lax.axis_size("x") + lax.axis_index("x")
    page = position // MAXT
    count = lax.dynamic_index_in_dim(tile_count[0], page, keepdims=False)
    live = position % MAXT < count

    half = w_merge.shape[0] // 2
    piece = lax.dynamic_slice_in_dim(w_merge.T, lax.axis_index("core") * half, half, 1)
    piece = lax.all_gather(piece, "x", axis=0, tiled=True)
    merger = lax.all_gather(piece, ("core", "y"), axis=0, tiled=True)
    merger = merger.reshape(2, -1, half)

    mine = jnp.concatenate([w_gate[0], w_up[0], w_down[0].T], axis=1)
    mine, merger = lax.optimization_barrier((mine, merger))
    experts = lax.all_gather(mine, ("z", "core"), axis=0, tiled=True)

    table, high, low = slot_tables(routes, route_weight)
    vis = tile_attention(queries, keys, values, resid, w_out)
    merged = jnp.where(live, space_to_depth(vis), jnp.zeros((), jnp.bfloat16))
    merged = jnp.pad(merged, ((0, TPAD - tokens), (0, 0)))
    stream, send = merge_dispatch(merged, merger, table)
    received = lax.all_to_all(send, ("y", "x"), split_axis=0, concat_axis=0)
    width = stream.shape[1]
    outcome = expert_ffn(received.reshape(-1, width), rms_gain[None, :], experts)
    back = lax.all_to_all(
        outcome.reshape(EXPERTS, SLOT, width), ("y", "x"), split_axis=0, concat_axis=0
    )
    return combine(stream, high, low, back.reshape(-1, width), tokens)


def solution(mesh):
    inner = Mesh(mesh.devices.reshape(8, 2, 8, 4), ("z", "core", "y", "x"))
    pages = ("z", "core")
    expert = ("y", "x")
    rows = P(("z", "core", "y", "x"), None)
    return jax.shard_map(
        local,
        mesh=inner,
        in_specs=(
            rows,
            rows,
            rows,
            rows,
            P(),
            P(None, expert),
            P(),
            P(expert, pages, None),
            P(expert, pages, None),
            P(expert, None, pages),
            P(pages, None),
            rows,
            rows,
        ),
        out_specs=rows,
        check_vma=False,
    )
```

time: 366 us -> 263 us (0.72)
  waiting for transfers between devices: 243 us -> 171 us
  other arithmetic: 22.8 us -> 1.27 us
  matrix products: 32.9 us -> 12 us
  Pallas kernels: 0 us -> 19.6 us
  local copies, waits for them, and re-layouts: 35.8 us -> 16.2 us
  blocking collectives: 0 us -> 11.5 us
    all_gather x4 -> x2, waiting for transfers between devices: 126 us -> 53.4 us  [the longest x1 53.4 us: local(): merger = lax.all_gather(piece, ('core', 'y'), axis=0, tiled=True)]
    dot_general x4 -> x1, matrix products: 20.9 us -> 0.13 us  [slot_tables(): jnp.dot(member.astype(jnp.bfloat16), earlier, preferred_element_type=jnp....]
    pallas_call x0 -> x3, Pallas kernels: none -> 19.6 us  [the longest x1 10.7 us: expert_ffn(): pl.pallas_call(functools.partial(expert_body, hidden), grid=(count // blo...]
    unnamed x1 -> x0, other arithmetic: 15.6 us -> none
    all_gather x0 -> x1, blocking collectives: none -> 11.5 us  [local(): piece = lax.all_gather(piece, 'x', axis=0, tiled=True)]
    convert_element_type x2 -> x0, local copies, waits for them, and re-layouts: 10.4 us -> none  [the longest x1 5.99 us: local(): outcome = jnp.einsum('erh,ehd->erd', act, lax.all_gather(w_down, 'pages',...]
    reduce_sum x3 -> x1, other arithmetic: 4.48 us -> 0.02 us  [slot_tables(): weight = jnp.sum(jnp.where(hit, route_weight.T[:, None, :], 0.0), axis=0)]
    all_to_all x2, waiting for transfers between devices: 114 us -> 118 us  [the longest x1 59.4 us: local(): received = lax.all_to_all(send, ('y', 'x'), split_axis=0, concat_axis=0)]
  transfers between devices with their start and end apart: 6 -> 4, of which waited for: 5 -> 3; matrix products, arithmetic and copies ran while one was open for 10% -> 7% of each run, Pallas kernels for 0% -> 2%
where the time goes in v1:
time: 263 us; the launch traced here: 261 us
  waiting for transfers between devices  171 us (65%)
  Pallas kernels  19.6 us (7%)
  local copies, waits for them, and re-layouts  16.2 us (6%)
  starting transfers between devices  14.7 us (6%)
  between operations  14.3 us (5%)
  matrix products  12 us (5%)
  blocking collectives  11.5 us (4%)
    all_to_all x1, waiting for transfers between devices, local(): received = lax.all_to_all(send, ('y', 'x'), split_axis=0, concat_axis=0)  59.4 us
    all_to_all x1, waiting for transfers between devices, local(): lax.all_to_all(outcome.reshape(EXPERTS, SLOT, width), ('y', 'x'), split_a...  58.2 us
    all_gather x1, waiting for transfers between devices, local(): merger = lax.all_gather(piece, ('core', 'y'), axis=0, tiled=True)  53.4 us
    all_gather x1, blocking collectives, local(): piece = lax.all_gather(piece, 'x', axis=0, tiled=True)  11.5 us
    pallas_call x1, Pallas kernels, expert_ffn(): pl.pallas_call(functools.partial(expert_body, hidden), grid=(count // blo...  10.7 us
    unnamed x26, local copies, waits for them, and re-layouts  9.27 us
    all_to_all x1, starting transfers between devices, local(): lax.all_to_all(outcome.reshape(EXPERTS, SLOT, width), ('y', 'x'), split_a...  7.74 us
    sub x1, matrix products, tile_attention(): weights = jnp.exp(scores - top)  7.08 us
  transfers between devices with their start and end apart: 4, of which 3 were waited for; matrix products, arithmetic and copies ran while one was open for 7% of the time, Pallas kernels for 2%

profile of v1, /device:TPU:1, one launch (start us, length us, event | category | flops | bytes accessed | tf_op | source)
XLA Modules:
  0.0 260.7 jit_solution(1710067147626564094)
XLA Ops:
  6.5 0.0 copy-start
  6.5 0.0 copy-start.11
  6.5 0.0 all-gather.3.cloned.1.call-start
  6.5 1.0 dynamic-slice_bitcast_fusion
  7.5 11.5 %all_gather.9 = bf16[160,1152]{1,0:T(8,128)(2,1)} all-gather(bf16[40,1152]{1,0:T(8,128)(2,1)S(1)} %dynamic-slice_bitcast_fusion), channel_id=1, replica_groups=mesh['z'=8,'core'=2,'y'=8,'x'=4] {'x'}, dimensions={0}, use_global_device_ids=true | all-gather | bytes 460800 | tf_op jit(solution)/shard_map/all_gather | solution.py:212
  19.0 0.0 all-gather.3.cloned.1.call-update
  19.1 0.0 all-gather.5.cloned.1.call-start
  19.1 1.9 concatenate.3
  21.0 53.4 %all-gather.3.cloned.1.call-done = bf16[2560,1152]{1,0:T(8,128)(2,1)} async-done(((bf16[160,1152]{1,0:T(8,128)(2,1)}), bf16[2560,1152]{1,0:T(8,128)(2,1)}) %all-gather.3.cloned.1.call-update) | async-done | bytes 5898256 | tf_op jit(solution)/shard_map/all_gather | solution.py:213
  74.4 0.0 all-gather.5.cloned.1.call-update
  74.5 1.2 constant_dynamic-slice_fusion
  76.4 7.1 %fusion.23 = (f32[8,484]{1,0:T(8,128)S(1)}, f32[8,484,484]{1,2,0:T(8,128)}) fusion(bf16[484,8,72]{0,2,1:T(8,128)(2,1)} %bitcast.51, bf16[484,8,72]{0,2,1:T(8,128)(2,1)} %bitcast.52), kind=kOutput, calls=%fused_computation.33 | convolution fusion | flops 275485536 | bytes 8626816 | tf_op jit(solution)/shard_map/sub | solution.py:29
  83.5 0.0 copy-done.11
  83.5 0.0 copy-start.12
  83.5 4.1 %fusion.7 = bf16[8,484,72]{1,2,0:T(8,128)(2,1)S(1)} fusion(bf16[484,8,72]{0,2,1:T(8,128)(2,1)S(1)} %bitcast.53, f32[8,484,484]{1,2,0:T(8,128)} %get-tuple-element.18, f32[8,484]{1,0:T(8,128)S(1)} %get-tuple-element.17), kind=kOutput, calls=%fused_computation.9 | convolution fusion | flops 273889792 | bytes 8626816 | tf_op jit(solution)/shard_map/hqk,khd->qhd/dot_general | solution.py:31
  87.6 0.0 copy-start.9
  87.6 0.0 copy-done
  87.6 0.0 copy-done.12
  87.7 0.7 fusion.8
  88.3 0.3 copy.20
  88.7 0.8 select_n.61
  89.5 0.0 copy-start.8
  89.5 0.4 copy.21
  89.9 1.1 select_n.63
  91.0 0.1 eq.43
  91.2 0.0 copy-done.9
  91.2 0.1 fusion.9
  91.3 0.2 fusion.14.table_ref
  91.6 0.0 copy-start.1
  91.6 2.7 %copy-done.1 = bf16[2560,1152]{1,0:T(8,128)(2,1)S(1)} copy-done((bf16[2560,1152]{1,0:T(8,128)(2,1)S(1)}, bf16[2560,1152]{1,0:T(8,128)(2,1)}, u32[]{:S(2)}) %copy-start.1) | copy-done | bytes 5898264
  94.2 5.8 %merge_dispatch.1 = (bf16[128,1280]{1,0:T(8,128)(2,1)S(1)}, bf16[32,32,1280]{2,1,0:T(8,128)(2,1)S(1)}) custom-call(bf16[128,2304]{1,0:T(8,128)(2,1)S(1)} %pad.12.merged_ref, bf16[2,1280,1152]{2,1,0:T(8,128)(2,1)S(1)} %bitcast.44, bf16[1024,128]{1,0:T(8,128)(2,1)S(1)} %fusion.14.table_ref), custom_call_target="tpu_custom_call" | custom-call | flops 1090519040 | bytes 10485760 | tf_op jit(solution)/shard_map/merge_dispatch/pallas_call | solution.py:87
  100.1 0.0 copy-start.3
  100.1 1.5 copy-done.3
  101.6 0.7 copy-done.6
  102.3 6.9 %all-to-all-start = ((bf16[32,32,1280]{2,1,0:T(8,128)(2,1)}), bf16[32,32,1280]{2,1,0:T(8,128)(2,1)S(1)}, u32[]{:S(2)}, u32[]{:S(2)}) async-start(bf16[32,32,1280]{2,1,0:T(8,128)(2,1)} %copy-done.3), calls=%async_computation | async-start | bytes 5242880 | tf_op jit(solution)/shard_map/all_to_all | solution.py:225
  109.2 0.0 copy-done.8
  109.2 59.4 %all-to-all-done = bf16[32,32,1280]{2,1,0:T(8,128)(2,1)S(1)} async-done(((bf16[32,32,1280]{2,1,0:T(8,128)(2,1)}), bf16[32,32,1280]{2,1,0:T(8,128)(2,1)S(1)}, u32[]{:S(2)}, u32[]{:S(2)}) %all-to-all-start) | async-done | bytes 2621472 | tf_op jit(solution)/shard_map/all_to_all | solution.py:225
  168.6 10.7 %expert_ffn.1 = bf16[1024,1280]{1,0:T(8,128)(2,1)S(1)} custom-call(bf16[1024,1280]{1,0:T(8,128)(2,1)S(1)} %bitcast.46, f32[1,1280]{1,0:T(1,128)S(1)} %broadcast_in_dim.72.gain_ref, bf16[1280,2112]{1,0:T(8,128)(2,1)} %all-gather.5.cloned.1.call-done.weight_ref), custom_call_target="tpu_custom_call" | custom-call | flops 5536481280 | bytes 11534336 | tf_op jit(solution)/shard_map/expert_ffn/pallas_call | solution.py:133
  179.3 0.0 copy-start.2
  179.3 1.5 copy-done.2
  180.8 7.7 %all-to-all-start.1 = ((bf16[32,32,1280]{2,1,0:T(8,128)(2,1)}), bf16[32,32,1280]{2,1,0:T(8,128)(2,1)S(1)}, u32[]{:S(2)}, u32[]{:S(2)}) async-start(bf16[32,32,1280]{2,1,0:T(8,128)(2,1)} %bitcast.45), calls=%async_computation.1 | async-start | bytes 5242880 | tf_op jit(solution)/shard_map/all_to_all | solution.py:228
  188.6 0.0 copy-done.10
  188.6 1.0 fusion.12
  189.7 58.2 %all-to-all-done.1 = bf16[32,32,1280]{2,1,0:T(8,128)(2,1)S(1)} async-done(((bf16[32,32,1280]{2,1,0:T(8,128)(2,1)}), bf16[32,32,1280]{2,1,0:T(8,128)(2,1)S(1)}, u32[]{:S(2)}, u32[]{:S(2)}) %all-to-all-start.1) | async-done | bytes 2621472 | tf_op jit(solution)/shard_map/all_to_all | solution.py:228
  247.9 0.9 copy-done.4
  248.8 0.9 copy-done.5
  249.8 1.0 copy-done.7
  250.8 3.1 %combine.1 = bf16[121,1280]{1,0:T(8,128)(2,1)} custom-call(bf16[128,1280]{1,0:T(8,128)(2,1)S(1)} %copy-done.7, bf16[1024,128]{1,0:T(8,128)(2,1)S(1)} %copy-done.5, bf16[1024,128]{1,0:T(8,128)(2,1)S(1)} %copy-done.4, bf16[1024,1280]{1,0:T(8,128)(2,1)S(1)} %bitcast.43), custom_call_target="tpu_custom_call" | custom-call | flops 671088640 | bytes 4194304 | tf_op jit(solution)/shard_map/combine/pallas_call | solution.py:168
  (14 shorter events, 0.1 us)
Async XLA Ops:
  6.5 81.1 %copy-start = (bf16[576,576]{1,0:T(8,128)(2,1)S(1)}, bf16[576,576]{1,0:T(8,128)(2,1)}, u32[]{:S(2)}) copy-start(bf16[576,576]{1,0:T(8,128)(2,1)} %param.17) | copy-start | bytes 1990660
  6.5 76.9 %copy-start.11 = (bf16[484,576]{0,1:T(8,128)(2,1)S(1)}, bf16[484,576]{0,1:T(8,128)(2,1)}, u32[]{:S(2)}) copy-start(bf16[484,576]{0,1:T(8,128)(2,1)} %param.15) | copy-start | bytes 1672708
  6.5 67.9 %all-gather.3.cloned.1.call-start = ((), (), s32[]{:S(2)}) async-start(), calls=%async_computation.2 | async-start | bytes 6266880 | tf_op jit(solution)/shard_map/all_gather | solution.py:213
  19.1 149.6 %all-gather.5.cloned.1.call-start = ((), (), s32[]{:S(2)}) async-start(), calls=%async_computation.3 | async-start | bytes 5918720 | tf_op jit(solution)/shard_map/all_gather | solution.py:218
  83.5 4.2 %copy-start.12 = (bf16[484,576]{0,1:T(8,128)(2,1)S(1)}, bf16[484,576]{0,1:T(8,128)(2,1)}, u32[]{:S(2)}) copy-start(bf16[484,576]{0,1:T(8,128)(2,1)} %param.16) | copy-start | bytes 1672708
  87.6 3.5 %copy-start.9 = (s32[121,6]{0,1:T(8,128)S(1)}, s32[121,6]{0,1:T(8,128)}, u32[]{:S(2)}) copy-start(s32[121,6]{0,1:T(8,128)} %param.24) | copy-start | bytes 8716
  89.5 19.7 %copy-start.8 = (f32[1280]{0:T(1024)S(1)}, f32[1280]{0:T(1024)}, u32[]{:S(2)}) copy-start(f32[1280]{0:T(1024)} %param.19) | copy-start | bytes 15364
  91.6 2.7 %copy-start.1 = (bf16[2560,1152]{1,0:T(8,128)(2,1)S(1)}, bf16[2560,1152]{1,0:T(8,128)(2,1)}, u32[]{:S(2)}) copy-start(bf16[2560,1152]{1,0:T(8,128)(2,1)} %all-gather.3.cloned.1.call-done) | copy-start | bytes 17694724
  100.1 1.5 copy-start.3
  101.6 0.7 copy-start.6
  102.3 66.3 %all-to-all-start = ((bf16[32,32,1280]{2,1,0:T(8,128)(2,1)}), bf16[32,32,1280]{2,1,0:T(8,128)(2,1)S(1)}, u32[]{:S(2)}, u32[]{:S(2)}) async-start(bf16[32,32,1280]{2,1,0:T(8,128)(2,1)} %copy-done.3), calls=%async_computation | async-start | bytes 5242880 | tf_op jit(solution)/shard_map/all_to_all | solution.py:225
  168.6 19.9 %copy-start.10 = (f32[121,6]{0,1:T(8,128)S(1)}, f32[121,6]{0,1:T(8,128)}, u32[]{:S(2)}) copy-start(f32[121,6]{0,1:T(8,128)} %param.25) | copy-start | bytes 8716
  179.3 1.5 copy-start.2
  180.8 67.1 %all-to-all-start.1 = ((bf16[32,32,1280]{2,1,0:T(8,128)(2,1)}), bf16[32,32,1280]{2,1,0:T(8,128)(2,1)S(1)}, u32[]{:S(2)}, u32[]{:S(2)}) async-start(bf16[32,32,1280]{2,1,0:T(8,128)(2,1)} %bitcast.45), calls=%async_computation.1 | async-start | bytes 5242880 | tf_op jit(solution)/shard_map/all_to_all | solution.py:228
  247.9 1.0 copy-start.4
  248.8 0.9 copy-start.5
  249.8 1.0 copy-start.7
Sparse Core Ops, SparseCore 0:
  19.2 55.2 all-gather.2
  76.6 46.4 all-gather.4

commit v2 on v1

--- a/solution.py
+++ b/solution.py
@@ -100,7 +100,7 @@
             jax.ShapeDtypeStruct((TPAD, width), jnp.bfloat16),
             jax.ShapeDtypeStruct((EXPERTS, SLOT, width), jnp.bfloat16),
         ],
-        compiler_params=pltpu.CompilerParams(vmem_limit_bytes=40 << 20),
+        compiler_params=pltpu.CompilerParams(vmem_limit_bytes=60 << 20),
         cost_estimate=pl.CostEstimate(
             flops=2 * TPAD * width * (merged.shape[1] + EXPERTS * SLOT),
             bytes_accessed=10 << 20,
@@ -111,19 +111,23 @@
 
 
 def expert_body(hidden, rows_ref, gain_ref, weight_ref, out_ref):
-    wide = rows_ref[...].astype(jnp.float32)
-    scale = lax.rsqrt(jnp.mean(wide * wide, axis=-1, keepdims=True) + 1e-06)
-    normed = (wide * scale * gain_ref[...]).astype(jnp.bfloat16)
-    both = jnp.dot(normed, weight_ref[:, : 2 * hidden], preferred_element_type=jnp.float32)
-    gate = both[:, :hidden]
-    up = both[:, hidden:]
-    act = (gate / (1.0 + jnp.exp(-gate)) * up).astype(jnp.bfloat16)
-    out_ref[...] = lax.dot_general(
-        act,
-        weight_ref[:, 2 * hidden :],
-        (((1,), (1,)), ((), ())),
-        preferred_element_type=jnp.float32,
-    ).astype(jnp.bfloat16)
+    gain = gain_ref[...]
+    part = rows_ref.shape[0] // 2
+    for i in range(2):
+        span = pl.ds(i * part, part)
+        wide = rows_ref[span].astype(jnp.float32)
+        scale = lax.rsqrt(jnp.mean(wide * wide, axis=-1, keepdims=True) + 1e-06)
+        normed = (wide * scale * gain).astype(jnp.bfloat16)
+        both = jnp.dot(normed, weight_ref[:, : 2 * hidden], preferred_element_type=jnp.float32)
+        gate = both[:, :hidden]
+        up = both[:, hidden:]
+        act = (gate / (1.0 + jnp.exp(-gate)) * up).astype(jnp.bfloat16)
+        out_ref[span] = lax.dot_general(
+            act,
+            weight_ref[:, 2 * hidden :],
+            (((1,), (1,)), ((), ())),
+            preferred_element_type=jnp.float32,
+        ).astype(jnp.bfloat16)
 
 
 def expert_ffn(rows, gain, weight):
@@ -140,7 +144,7 @@
         ],
         out_specs=pl.BlockSpec((block, width), lambda i: (i, 0)),
         out_shape=jax.ShapeDtypeStruct((count, width), jnp.bfloat16),
-        compiler_params=pltpu.CompilerParams(vmem_limit_bytes=48 << 20),
+        compiler_params=pltpu.CompilerParams(vmem_limit_bytes=60 << 20),
         cost_estimate=pl.CostEstimate(
             flops=6 * count * width * hidden,
             bytes_accessed=11 << 20,
@@ -176,7 +180,7 @@
         ],
         out_specs=pl.BlockSpec((tokens, block), column),
         out_shape=jax.ShapeDtypeStruct((tokens, width), jnp.bfloat16),
-        compiler_params=pltpu.CompilerParams(vmem_limit_bytes=40 << 20),
+        compiler_params=pltpu.CompilerParams(vmem_limit_bytes=60 << 20),
         cost_estimate=pl.CostEstimate(
             flops=4 * TPAD * width * back.shape[0],
             bytes_accessed=4 << 20,
@@ -213,14 +217,16 @@
     merger = lax.all_gather(piece, ("core", "y"), axis=0, tiled=True)
     merger = merger.reshape(2, -1, half)
 
-    mine = jnp.concatenate([w_gate[0], w_up[0], w_down[0].T], axis=1)
-    mine, merger = lax.optimization_barrier((mine, merger))
-    experts = lax.all_gather(mine, ("z", "core"), axis=0, tiled=True)
-
     table, high, low = slot_tables(routes, route_weight)
     vis = tile_attention(queries, keys, values, resid, w_out)
     merged = jnp.where(live, space_to_depth(vis), jnp.zeros((), jnp.bfloat16))
     merged = jnp.pad(merged, ((0, TPAD - tokens), (0, 0)))
+
+    mine = jnp.concatenate([w_gate[0], w_up[0], w_down[0].T], axis=1)
+    mine, merger, merged, table, high, low = lax.optimization_barrier(
+        (mine, merger, merged, table, high, low)
+    )
+    experts = lax.all_gather(mine, ("z", "core"), axis=0, tiled=True)
     stream, send = merge_dispatch(merged, merger, table)
     received = lax.all_to_all(send, ("y", "x"), split_axis=0, concat_axis=0)
     width = stream.shape[1]

time: 263 us -> 247 us (0.939)
  waiting for transfers between devices: 171 us -> 93.4 us
  blocking collectives: 11.5 us -> 80.4 us
  Pallas kernels: 19.6 us -> 28.1 us
  starting transfers between devices: 14.7 us -> 6.92 us
  local copies, waits for them, and re-layouts: 16.2 us -> 8.93 us
    all_to_all x0 -> x1, blocking collectives: none -> 68.9 us  [local(): lax.all_to_all(outcome.reshape(EXPERTS, SLOT, width), ('y', 'x'), split_a...]
    all_to_all x1 -> x0, waiting for transfers between devices: 58.2 us -> none  [local(): lax.all_to_all(outcome.reshape(EXPERTS, SLOT, width), ('y', 'x'), split_a...]
    all_gather x1, waiting for transfers between devices: 53.4 us -> 34.5 us  [local(): merger = lax.all_gather(piece, ('core', 'y'), axis=0, tiled=True)]
    unnamed x26 -> x20, local copies, waits for them, and re-layouts: 9.27 us -> 1.51 us
    all_to_all x1 -> x0, starting transfers between devices: 7.74 us -> none  [local(): lax.all_to_all(outcome.reshape(EXPERTS, SLOT, width), ('y', 'x'), split_a...]
    pallas_call x1, Pallas kernels: 10.7 us -> 14.5 us  [expert_ffn(): pl.pallas_call(functools.partial(expert_body, hidden), grid=(count // blo...]
  transfers between devices with their start and end apart: 4 -> 3, of which waited for: 3 -> 2; matrix products, arithmetic and copies ran while one was open for 7% -> 8% of each run, Pallas kernels for 2% -> 3%
where the time goes in v2:
time: 247 us; the launch traced here: 246 us
  waiting for transfers between devices  93.4 us (38%)
  blocking collectives  80.4 us (33%)
  Pallas kernels  28.1 us (11%)
  between operations  14.2 us (6%)
  matrix products  12.1 us (5%)
  local copies, waits for them, and re-layouts  8.93 us (4%)
  starting transfers between devices  6.92 us (3%)
    all_to_all x1, blocking collectives, local(): lax.all_to_all(outcome.reshape(EXPERTS, SLOT, width), ('y', 'x'), split_a...  68.9 us
    all_to_all x1, waiting for transfers between devices, local(): received = lax.all_to_all(send, ('y', 'x'), split_axis=0, concat_axis=0)  58.8 us
    all_gather x1, waiting for transfers between devices, local(): merger = lax.all_gather(piece, ('core', 'y'), axis=0, tiled=True)  34.5 us
    pallas_call x1, Pallas kernels, expert_ffn(): pl.pallas_call(functools.partial(expert_body, hidden), grid=(count // blo...  14.5 us
    all_gather x1, blocking collectives, local(): piece = lax.all_gather(piece, 'x', axis=0, tiled=True)  11.5 us
    pallas_call x1, Pallas kernels, merge_dispatch(): pl.pallas_call(merge_body, grid=(width // block,), in_specs=[pl.BlockSpec...  8.36 us
    sub x1, matrix products, tile_attention(): weights = jnp.exp(scores - top)  7.18 us
    all_to_all x1, starting transfers between devices, local(): received = lax.all_to_all(send, ('y', 'x'), split_axis=0, concat_axis=0)  6.88 us
  transfers between devices with their start and end apart: 3, of which 2 were waited for; matrix products, arithmetic and copies ran while one was open for 8% of the time, Pallas kernels for 3%

profile of v2, /device:TPU:1, one launch (start us, length us, event | category | flops | bytes accessed | tf_op | source)
XLA Modules:
  0.0 246.0 jit_solution(6688700015184763072)
XLA Ops:
  6.5 0.0 copy-start
  6.5 0.0 copy-start.8
  6.5 0.0 all-gather.3.cloned.1.call-start
  6.5 1.0 dynamic-slice_bitcast_fusion
  7.5 11.5 %all_gather.9 = bf16[160,1152]{1,0:T(8,128)(2,1)} all-gather(bf16[40,1152]{1,0:T(8,128)(2,1)S(1)} %dynamic-slice_bitcast_fusion), channel_id=1, replica_groups=mesh['z'=8,'core'=2,'y'=8,'x'=4] {'x'}, dimensions={0}, use_global_device_ids=true | all-gather | bytes 460800 | tf_op jit(solution)/shard_map/all_gather | solution.py:216
  19.0 0.0 all-gather.3.cloned.1.call-update
  19.1 0.0 all-gather.5.cloned.1.call-start
  19.1 1.2 constant_dynamic-slice_fusion
  21.0 7.2 %fusion.23 = (f32[8,484]{1,0:T(8,128)S(1)}, f32[8,484,484]{1,2,0:T(8,128)}) fusion(bf16[484,8,72]{0,2,1:T(8,128)(2,1)} %bitcast.51, bf16[484,8,72]{0,2,1:T(8,128)(2,1)} %bitcast.52), kind=kOutput, calls=%fused_computation.33 | convolution fusion | flops 275485536 | bytes 8626816 | tf_op jit(solution)/shard_map/sub | solution.py:29
  28.2 0.0 copy-done.8
  28.2 0.0 copy-start.9
  28.2 4.1 %fusion.7 = bf16[8,484,72]{1,2,0:T(8,128)(2,1)S(1)} fusion(bf16[484,8,72]{0,2,1:T(8,128)(2,1)S(1)} %bitcast.53, f32[8,484,484]{1,2,0:T(8,128)} %get-tuple-element.26, f32[8,484]{1,0:T(8,128)S(1)} %get-tuple-element.25), kind=kOutput, calls=%fused_computation.9 | convolution fusion | flops 273889792 | bytes 8626816 | tf_op jit(solution)/shard_map/hqk,khd->qhd/dot_general | solution.py:31
  32.4 0.0 copy-start.6
  32.4 0.0 copy-start.7
  32.4 0.0 copy-start.2
  32.4 0.0 copy-start.3
  32.4 0.0 copy-start.4
  32.4 0.0 copy-done
  32.5 0.0 copy-done.9
  32.5 0.7 fusion.8
  33.1 0.3 copy.20
  33.5 0.8 select_n.62
  34.3 0.4 copy.21
  34.7 0.0 copy-start.5
  34.7 1.1 select_n.64
  35.9 0.1 eq.43
  36.0 0.9 pad.12.merged_ref
  36.8 0.0 copy-done.6
  36.9 0.1 fusion.9
  37.0 0.9 fusion.14.table_ref
  37.9 0.0 copy-done.7
  38.0 1.0 fusion.12
  39.0 0.0 copy-done.2
  39.0 0.0 copy-done.3
  39.0 0.0 copy-done.4
  39.0 0.9 concatenate.3
  39.9 34.5 %all-gather.3.cloned.1.call-done = bf16[2560,1152]{1,0:T(8,128)(2,1)} async-done(((bf16[160,1152]{1,0:T(8,128)(2,1)}), bf16[2560,1152]{1,0:T(8,128)(2,1)}) %all-gather.3.cloned.1.call-update) | async-done | bytes 5898256 | tf_op jit(solution)/shard_map/all_gather | solution.py:217
  74.4 0.0 all-gather.5.cloned.1.call-update
  74.5 8.4 %merge_dispatch.1 = (bf16[128,1280]{1,0:T(8,128)(2,1)}, bf16[32,32,1280]{2,1,0:T(8,128)(2,1)}) custom-call(bf16[128,2304]{1,0:T(8,128)(2,1)} %pad.12.merged_ref, bf16[2,1280,1152]{2,1,0:T(8,128)(2,1)} %bitcast.44, bf16[1024,128]{1,0:T(8,128)(2,1)} %fusion.14.table_ref), custom_call_target="tpu_custom_call" | custom-call | flops 1090519040 | bytes 10485760 | tf_op jit(solution)/shard_map/merge_dispatch/pallas_call | solution.py:87
  82.8 6.9 %all-to-all-start = ((bf16[32,32,1280]{2,1,0:T(8,128)(2,1)}), bf16[32,32,1280]{2,1,0:T(8,128)(2,1)S(1)}, u32[]{:S(2)}, u32[]{:S(2)}) async-start(bf16[32,32,1280]{2,1,0:T(8,128)(2,1)} %get-tuple-element.19), calls=%async_computation | async-start | bytes 5242880 | tf_op jit(solution)/shard_map/all_to_all | solution.py:231
  89.7 0.0 copy-done.5
  89.7 0.6 broadcast_in_dim.72.gain_ref
  90.3 58.8 %all-to-all-done = bf16[32,32,1280]{2,1,0:T(8,128)(2,1)S(1)} async-done(((bf16[32,32,1280]{2,1,0:T(8,128)(2,1)}), bf16[32,32,1280]{2,1,0:T(8,128)(2,1)S(1)}, u32[]{:S(2)}, u32[]{:S(2)}) %all-to-all-start) | async-done | bytes 2621472 | tf_op jit(solution)/shard_map/all_to_all | solution.py:231
  149.1 0.0 copy-start.1
  149.1 1.5 copy-done.1
  150.6 14.5 %expert_ffn.1 = bf16[1024,1280]{1,0:T(8,128)(2,1)} custom-call(bf16[1024,1280]{1,0:T(8,128)(2,1)} %bitcast.45, f32[1,1280]{1,0:T(1,128)} %broadcast_in_dim.72.gain_ref, bf16[1280,2112]{1,0:T(8,128)(2,1)} %all-gather.5.cloned.1.call-done.weight_ref), custom_call_target="tpu_custom_call" | custom-call | flops 5536481280 | bytes 11534336 | tf_op jit(solution)/shard_map/expert_ffn/pallas_call | solution.py:137
  165.1 68.9 %all_to_all.10 = bf16[32,32,1280]{2,1,0:T(8,128)(2,1)} all-to-all(bf16[32,32,1280]{2,1,0:T(8,128)(2,1)} %bitcast.46), channel_id=1, replica_groups=mesh['z'=8,'core'=2,'y'=8,'x'=4] {'y','x'}, dimensions={0} | all-to-all | bytes 5242880 | tf_op jit(solution)/shard_map/all_to_all | solution.py:234
  234.0 5.2 %combine.1 = bf16[121,1280]{1,0:T(8,128)(2,1)} custom-call(bf16[128,1280]{1,0:T(8,128)(2,1)} %get-tuple-element.16.stream_ref, bf16[1024,128]{1,0:T(8,128)(2,1)} %get-tuple-element.17.high_ref, bf16[1024,128]{1,0:T(8,128)(2,1)} %get-tuple-element.18.low_ref, bf16[1024,1280]{1,0:T(8,128)(2,1)} %bitcast.43), custom_call_target="tpu_custom_call" | custom-call | flops 671088640 | bytes 4194304 | tf_op jit(solution)/shard_map/combine/pallas_call | solution.py:172
  (7 shorter events, 0.1 us)
Async XLA Ops:
  6.5 25.9 %copy-start = (bf16[576,576]{1,0:T(8,128)(2,1)S(1)}, bf16[576,576]{1,0:T(8,128)(2,1)}, u32[]{:S(2)}) copy-start(bf16[576,576]{1,0:T(8,128)(2,1)} %param.17) | copy-start | bytes 1990660
  6.5 21.7 %copy-start.8 = (bf16[484,576]{0,1:T(8,128)(2,1)S(1)}, bf16[484,576]{0,1:T(8,128)(2,1)}, u32[]{:S(2)}) copy-start(bf16[484,576]{0,1:T(8,128)(2,1)} %param.15) | copy-start | bytes 1672708
  6.5 67.9 %all-gather.3.cloned.1.call-start = ((), (), s32[]{:S(2)}) async-start(), calls=%async_computation.2 | async-start | bytes 6266880 | tf_op jit(solution)/shard_map/all_gather | solution.py:217
  19.1 130.1 %all-gather.5.cloned.1.call-start = ((), (), s32[]{:S(2)}) async-start(), calls=%async_computation.3 | async-start | bytes 5918720 | tf_op jit(solution)/shard_map/all_gather | solution.py:229
  28.2 4.2 %copy-start.9 = (bf16[484,576]{0,1:T(8,128)(2,1)S(1)}, bf16[484,576]{0,1:T(8,128)(2,1)}, u32[]{:S(2)}) copy-start(bf16[484,576]{0,1:T(8,128)(2,1)} %param.16) | copy-start | bytes 1672708
  32.4 4.5 %copy-start.6 = (s32[121,6]{0,1:T(8,128)S(1)}, s32[121,6]{0,1:T(8,128)}, u32[]{:S(2)}) copy-start(s32[121,6]{0,1:T(8,128)} %param.24) | copy-start | bytes 8716
  32.4 5.5 %copy-start.7 = (f32[121,6]{0,1:T(8,128)S(1)}, f32[121,6]{0,1:T(8,128)}, u32[]{:S(2)}) copy-start(f32[121,6]{0,1:T(8,128)} %param.25) | copy-start | bytes 8716
  32.4 6.6 %copy-start.2 = (bf16[1,80,704]{2,1,0:T(8,128)(2,1)S(1)}, bf16[1,80,704]{2,1,0:T(8,128)(2,1)}, u32[]{:S(2)}) copy-start(bf16[1,80,704]{2,1,0:T(8,128)(2,1)} %param.20) | copy-start | bytes 337924
  32.4 6.5 %copy-start.3 = (bf16[1,80,704]{2,1,0:T(8,128)(2,1)S(1)}, bf16[1,80,704]{2,1,0:T(8,128)(2,1)}, u32[]{:S(2)}) copy-start(bf16[1,80,704]{2,1,0:T(8,128)(2,1)} %param.21) | copy-start | bytes 337924
  32.4 6.5 %copy-start.4 = (bf16[1,704,80]{1,2,0:T(8,128)(2,1)S(1)}, bf16[1,704,80]{1,2,0:T(8,128)(2,1)}, u32[]{:S(2)}) copy-start(bf16[1,704,80]{1,2,0:T(8,128)(2,1)} %param.22) | copy-start | bytes 337924
  34.7 55.0 %copy-start.5 = (f32[1280]{0:T(1024)S(1)}, f32[1280]{0:T(1024)}, u32[]{:S(2)}) copy-start(f32[1280]{0:T(1024)} %param.19) | copy-start | bytes 15364
  82.8 66.3 %all-to-all-start = ((bf16[32,32,1280]{2,1,0:T(8,128)(2,1)}), bf16[32,32,1280]{2,1,0:T(8,128)(2,1)S(1)}, u32[]{:S(2)}, u32[]{:S(2)}) async-start(bf16[32,32,1280]{2,1,0:T(8,128)(2,1)} %get-tuple-element.19), calls=%async_computation | async-start | bytes 5242880 | tf_op jit(solution)/shard_map/all_to_all | solution.py:231
  149.1 1.5 copy-start.1
Sparse Core Ops, SparseCore 0:
  19.2 55.2 all-gather.2
  76.6 46.2 all-gather.4

commit v3 on v2

v3 whole, which is shorter than its diff:
```python
import functools
import jax
import jax.numpy as jnp
from jax import lax
from jax.experimental import pallas as pl
from jax.experimental.pallas import tpu as pltpu
from jax.sharding import Mesh
from jax.sharding import PartitionSpec as P

HEADS = 8
TS = 22
EXPERTS = 32
TOPK = 6
MAXT = 4
SLOT = 32
TPAD = 128


def tile_attention(queries, keys, values, resid, w_out):
    patches = queries.shape[0]
    head_size = queries.shape[1] // HEADS
    q_heads = queries.reshape(patches, HEADS, head_size)
    k_heads = keys.reshape(patches, HEADS, head_size)
    v_heads = values.reshape(patches, HEADS, head_size)
    scores = jnp.einsum(
        "qhd,khd->hqk", q_heads, k_heads, preferred_element_type=jnp.float32
    ) * head_size ** (-0.5)
    top = jnp.max(scores, axis=-1, keepdims=True)
    weights = jnp.exp(scores - top)
    probs = (weights / jnp.sum(weights, axis=-1, keepdims=True)).astype(jnp.bfloat16)
    attended = jnp.einsum(
        "hqk,khd->qhd", probs, v_heads, preferred_element_type=jnp.float32
    ).astype(jnp.bfloat16)
    update = jnp.dot(attended.reshape(patches, -1), w_out, preferred_element_type=jnp.float32)
    return (resid.astype(jnp.float32) + update).astype(jnp.bfloat16)


def space_to_depth(vis):
    half = TS // 2
    width = vis.shape[1]
    grid = vis.reshape(half, 2, half, 2, width).transpose(0, 2, 1, 3, 4)
    return grid.reshape(half * half, 4 * width)


def shift(size, step):
    return [(i, (i + step) % size) for i in range(size)]


def far_shift(size):
    return [(i, (i + (2 if i % 2 == 0 else -2)) % size) for i in range(size)]


def back_again(pairs):
    return [(b, a) for a, b in pairs]


def slot_tables(info, ids):
    tiles = info.shape[0]
    hit = info[:, :TOPK, None, :].astype(jnp.int32) == ids[None, None, :, None]
    member = jnp.any(hit, axis=1)
    weight = jnp.sum(jnp.where(hit, info[:, TOPK : 2 * TOPK, None, :], 0.0), axis=1)
    earlier = jnp.triu(jnp.ones((TPAD, TPAD), jnp.bfloat16), 1)
    before = jnp.dot(
        member.astype(jnp.bfloat16), earlier, preferred_element_type=jnp.float32
    ).astype(jnp.int32)
    place = jnp.where(member, before, -1)
    table = place[:, :, None, :] == jnp.arange(SLOT, dtype=jnp.int32)[None, None, :, None]
    high = weight.astype(jnp.bfloat16)
    low = (weight - high.astype(jnp.float32)).astype(jnp.bfloat16)
    zero = jnp.zeros((), jnp.bfloat16)
    shape = (tiles, ids.shape[0] * SLOT, TPAD)
    parts = [
        jnp.where(table, part[:, :, None, :], zero).reshape(shape).swapaxes(1, 2)
        for part in (high, low)
    ]
    return table.astype(jnp.bfloat16).reshape(shape), jnp.concatenate(parts, axis=1)


def merge_body(merged_ref, weight_ref, stream_ref):
    half = weight_ref.shape[2]
    dims = (((1,), (1,)), ((), ()))
    product = lax.dot_general(
        merged_ref[:, :half], weight_ref[0], dims, preferred_element_type=jnp.float32
    ) + lax.dot_general(
        merged_ref[:, half:], weight_ref[1], dims, preferred_element_type=jnp.float32
    )
    gelu = 0.5 * product * (1.0 + lax.erf(product * (0.5**0.5)))
    stream_ref[...] = gelu.astype(jnp.bfloat16)


def merge(merged, weight):
    width = weight.shape[1]
    block = 256
    return pl.pallas_call(
        merge_body,
        grid=(width // block,),
        in_specs=[
            pl.BlockSpec(merged.shape, lambda i: (0, 0)),
            pl.BlockSpec((2, block, weight.shape[2]), lambda i: (0, i, 0)),
        ],
        out_specs=pl.BlockSpec((TPAD, block), lambda i: (0, i)),
        out_shape=jax.ShapeDtypeStruct((TPAD, width), jnp.bfloat16),
        compiler_params=pltpu.CompilerParams(vmem_limit_bytes=60 << 20),
        cost_estimate=pl.CostEstimate(
            flops=2 * TPAD * width * merged.shape[1],
            bytes_accessed=7 << 20,
            transcendentals=TPAD * width,
        ),
        name="merge",
    )(merged, weight)


def pick_body(table_ref, *refs):
    send_ref = refs[-1]
    cols, hosted, _, slot, width = send_ref.shape
    for i, tile_ref in enumerate(refs[:-1]):
        rows = jnp.dot(table_ref[i], tile_ref[...], preferred_element_type=jnp.float32)
        send_ref[:, :, i] = rows.astype(jnp.bfloat16).reshape(cols, hosted, slot, width)


def pick_rows(table, tiles, cols, hosted):
    width = tiles[0].shape[1]
    block = 256
    count = len(tiles)
    return pl.pallas_call(
        pick_body,
        grid=(width // block,),
        in_specs=[pl.BlockSpec(table.shape, lambda i: (0, 0, 0))]
        + [pl.BlockSpec((TPAD, block), lambda i: (0, i))] * count,
        out_specs=pl.BlockSpec((cols, hosted, count, SLOT, block), lambda i: (0, 0, 0, 0, i)),
        out_shape=jax.ShapeDtypeStruct((cols, hosted, count, SLOT, width), jnp.bfloat16),
        compiler_params=pltpu.CompilerParams(vmem_limit_bytes=60 << 20),
        cost_estimate=pl.CostEstimate(
            flops=2 * TPAD * width * count * table.shape[1],
            bytes_accessed=5 << 20,
            transcendentals=0,
        ),
        name="pick_rows",
    )(table, *tiles)


def expert_body(hidden, main, rows_ref, gain_ref, weight_ref, out_ref):
    width = rows_ref.shape[-1]
    wide = rows_ref[...].reshape(-1, width).astype(jnp.float32)
    scale = lax.rsqrt(jnp.mean(wide * wide, axis=-1, keepdims=True) + 1e-06)
    normed = (wide * scale * gain_ref[...]).astype(jnp.bfloat16)
    both = jnp.dot(normed, weight_ref[:, : 2 * hidden], preferred_element_type=jnp.float32)

    def gated(gate, up):
        return (gate / (1.0 + jnp.exp(-gate)) * up).astype(jnp.bfloat16)

    rest = hidden - main
    act = jnp.concatenate(
        [
            gated(both[:, :main], both[:, main : 2 * main]),
            gated(both[:, 2 * main : 2 * main + rest], both[:, 2 * main + rest :]),
        ],
        axis=1,
    )
    out_ref[...] = (
        lax.dot_general(
            act,
            weight_ref[:, 2 * hidden : 3 * hidden],
            (((1,), (1,)), ((), ())),
            preferred_element_type=jnp.float32,
        )
        .astype(jnp.bfloat16)
        .reshape(out_ref.shape)
    )


def expert_ffn(rows, gain, weight, hidden, main):
    cols, hosted, count, width = rows.shape
    place = lambda j: (0, j, 0, 0)
    return pl.pallas_call(
        functools.partial(expert_body, hidden, main),
        grid=(hosted,),
        in_specs=[
            pl.BlockSpec((cols, 1, count, width), place),
            pl.BlockSpec((1, width), lambda j: (0, 0)),
            pl.BlockSpec((width, weight.shape[1] // hosted), lambda j: (0, j)),
        ],
        out_specs=pl.BlockSpec((cols, 1, count, width), place),
        out_shape=jax.ShapeDtypeStruct(rows.shape, jnp.bfloat16),
        compiler_params=pltpu.CompilerParams(vmem_limit_bytes=60 << 20),
        cost_estimate=pl.CostEstimate(
            flops=6 * cols * hosted * count * width * hidden,
            bytes_accessed=16 << 20,
            transcendentals=cols * hosted * count * hidden,
        ),
        name="expert_ffn",
    )(rows, gain, weight)


def combine_body(base, mix_ref, back_ref, *refs):
    for i, out_ref in enumerate(refs):
        back = back_ref[:, :, base + i].reshape(mix_ref.shape[2], out_ref.shape[1])
        both = jnp.dot(mix_ref[base + i], back, preferred_element_type=jnp.float32)
        out_ref[...] = (both[:TPAD] + both[TPAD:]).astype(out_ref.dtype)


def combine(mix, back, base, count, dtype):
    cols, hosted, tiles, slot, width = back.shape
    block = 256
    return pl.pallas_call(
        functools.partial(combine_body, base),
        grid=(width // block,),
        in_specs=[
            pl.BlockSpec(mix.shape, lambda i: (0, 0, 0)),
            pl.BlockSpec((cols, hosted, tiles, slot, block), lambda i: (0, 0, 0, 0, i)),
        ],
        out_specs=[pl.BlockSpec((TPAD, block), lambda i: (0, i))] * count,
        out_shape=[jax.ShapeDtypeStruct((TPAD, width), dtype)] * count,
        compiler_params=pltpu.CompilerParams(vmem_limit_bytes=60 << 20),
        cost_estimate=pl.CostEstimate(
            flops=4 * TPAD * width * count * mix.shape[2],
            bytes_accessed=4 << 20,
            transcendentals=0,
        ),
        name="combine",
    )(mix, back)


def local(
    queries,
    keys,
    values,
    resid,
    w_out,
    w_merge,
    rms_gain,
    w_gate,
    w_up,
    w_down,
    tile_count,
    routes,
    route_weight,
):
    tokens = routes.shape[0]
    hidden = w_gate.shape[2]
    rows = lax.axis_size("y")
    cols = lax.axis_size("x")
    row = lax.axis_index("y")
    position = row * cols + lax.axis_index("x")
    page = position // MAXT
    count = lax.dynamic_index_in_dim(tile_count[0], page, keepdims=False)
    live = position % MAXT < count

    half = w_merge.shape[0] // 2
    piece = lax.dynamic_slice_in_dim(w_merge.T, lax.axis_index("core") * half, half, 1)
    piece = lax.all_gather(piece, "x", axis=0, tiled=True)

    edge = -(-3 * hidden // 128) * 128 - 3 * hidden
    main = hidden // 128 * 128
    gate, up, down = w_gate[0], w_up[0], w_down[0].T
    blank = jnp.zeros((down.shape[0], edge), down.dtype)
    own = jnp.concatenate(
        [gate[:, :main], up[:, :main], gate[:, main:], up[:, main:], down, blank], axis=1
    )
    routing = jnp.concatenate(
        [
            jnp.pad(routes, ((0, TPAD - tokens), (0, 0)), constant_values=-1).astype(jnp.float32),
            jnp.pad(route_weight, ((0, TPAD - tokens), (0, 0))),
        ],
        axis=1,
    ).T
    piece, own, routing = lax.optimization_barrier((piece, own, routing))
    merger = lax.all_gather(piece, ("core", "y"), axis=0, tiled=True)
    merger = merger.reshape(2, -1, half)
    other = lax.ppermute(own, "y", shift(rows, rows // 2))
    steps = (shift(rows, 1), shift(rows, -1), far_shift(rows))
    info = jnp.stack([routing] + [lax.ppermute(routing, "y", step) for step in steps])
    hosted = jnp.stack([row, (row + rows // 2) % rows])
    ids = (hosted[None, :] * cols + jnp.arange(cols, dtype=jnp.int32)[:, None]).reshape(-1)
    table, mix = slot_tables(info, ids)

    vis = tile_attention(queries, keys, values, resid, w_out)
    merged = jnp.where(live, space_to_depth(vis), jnp.zeros((), jnp.bfloat16))
    merged = jnp.pad(merged, ((0, TPAD - tokens), (0, 0)))

    mine = jnp.concatenate([own, other], axis=1)
    mine, merger, merged, table, mix = lax.optimization_barrier(
        (mine, merger, merged, table, mix)
    )
    experts = lax.all_gather(mine, ("z", "core"), axis=0, tiled=True)

    stream = merge(merged, merger)
    width = stream.shape[1]
    tiles = [stream] + [lax.ppermute(stream, "y", step) for step in steps]
    send = pick_rows(table, tiles, cols, 2)
    flat = (cols, send.size // cols // width, width)
    received = lax.all_to_all(send.reshape(flat), "x", split_axis=0, concat_axis=0)
    outcome = expert_ffn(
        received.reshape(cols, 2, -1, width), rms_gain[None, :], experts, hidden, main
    )
    back = lax.all_to_all(outcome.reshape(flat), "x", split_axis=0, concat_axis=0)
    back = back.reshape(send.shape)
    parts = combine(mix, back, 1, len(steps), jnp.bfloat16)
    total = combine(mix, back, 0, 1, jnp.float32)[0] + stream.astype(jnp.float32)
    for part, step in zip(parts, steps):
        total = total + lax.ppermute(part, "y", back_again(step)).astype(jnp.float32)
    return total[:tokens].astype(jnp.bfloat16)


def solution(mesh):
    inner = Mesh(mesh.devices.reshape(8, 2, 8, 4), ("z", "core", "y", "x"))
    pages = ("z", "core")
    expert = ("y", "x")
    rows = P(("z", "core", "y", "x"), None)
    return jax.shard_map(
        local,
        mesh=inner,
        in_specs=(
            rows,
            rows,
            rows,
            rows,
            P(),
            P(None, expert),
            P(),
            P(expert, pages, None),
            P(expert, pages, None),
            P(expert, None, pages),
            P(pages, None),
            rows,
            rows,
        ),
        out_specs=rows,
        check_vma=False,
    )
```

time: 247 us -> 246 us (level)
  starting transfers between devices: 6.92 us -> 40.1 us
  blocking collectives: 80.4 us -> 47.9 us
  waiting for transfers between devices: 93.4 us -> 79.4 us
  Pallas kernels: 28.1 us -> 32.5 us
  local copies, waits for them, and re-layouts: 8.93 us -> 13 us
  other arithmetic: 1.96 us -> 5.67 us
    ppermute x0 -> x10, starting transfers between devices: none -> 36.2 us  [the longest x3 11.8 us: local(): lax.ppermute(part, 'y', back_again(step)).astype(jnp.float32)]
    all_to_all x1, blocking collectives: 68.9 us -> 36.4 us  [local(): lax.all_to_all(outcome.reshape(flat), 'x', split_axis=0, concat_axis=0)]
    all_to_all x1, waiting for transfers between devices: 58.8 us -> 27.8 us  [local(): lax.all_to_all(send.reshape(flat), 'x', split_axis=0, concat_axis=0)]
    ppermute x0 -> x10, waiting for transfers between devices: none -> 13.3 us  [the longest x3 9.85 us: local(): tiles = [stream] + [lax.ppermute(stream, 'y', step) for step in steps]]
    all_gather x1, waiting for transfers between devices: 0.01 us -> 10.4 us  [local(): experts = lax.all_gather(mine, ('z', 'core'), axis=0, tiled=True)]
    all_gather x1, waiting for transfers between devices: 34.5 us -> 27.9 us  [local(): merger = lax.all_gather(piece, ('core', 'y'), axis=0, tiled=True)]
    pallas_call x3 -> x5, Pallas kernels: 28.1 us -> 32.5 us  [the longest x1 11.4 us: expert_ffn(): pl.pallas_call(functools.partial(expert_body, hidden, main), grid=(hosted...]
    slice x0 -> x4, local copies, waits for them, and re-layouts: none -> 3.34 us  [the longest x1 0.97 us: local(): gate[:, :main]]
  transfers between devices with their start and end apart: 3 -> 13, of which waited for: 2 -> 7; matrix products, arithmetic and copies ran while one was open for 8% -> 9% of each run, Pallas kernels for 3% -> 7%
where the time goes in v3:
time: 246 us; the launch traced here: 245 us
  waiting for transfers between devices  79.4 us (32%)
  blocking collectives  47.9 us (19%)
  starting transfers between devices  40.1 us (16%)
  Pallas kernels  32.5 us (13%)
  between operations  14.4 us (6%)
  local copies, waits for them, and re-layouts  13 us (5%)
  matrix products  12.1 us (5%)
  other arithmetic  5.67 us (2%)
    all_to_all x1, blocking collectives, local(): lax.all_to_all(outcome.reshape(flat), 'x', split_axis=0, concat_axis=0)  36.4 us
    all_gather x1, waiting for transfers between devices, local(): merger = lax.all_gather(piece, ('core', 'y'), axis=0, tiled=True)  27.9 us
    all_to_all x1, waiting for transfers between devices, local(): lax.all_to_all(send.reshape(flat), 'x', split_axis=0, concat_axis=0)  27.8 us
    ppermute x3, starting transfers between devices, local(): lax.ppermute(part, 'y', back_again(step)).astype(jnp.float32)  11.8 us
    ppermute x3, starting transfers between devices, local(): lax.ppermute(routing, 'y', step)  11.5 us
    all_gather x1, blocking collectives, local(): piece = lax.all_gather(piece, 'x', axis=0, tiled=True)  11.5 us
    pallas_call x1, Pallas kernels, expert_ffn(): pl.pallas_call(functools.partial(expert_body, hidden, main), grid=(hosted...  11.4 us
    all_gather x1, waiting for transfers between devices, local(): experts = lax.all_gather(mine, ('z', 'core'), axis=0, tiled=True)  10.4 us
  transfers between devices with their start and end apart: 13, of which 7 were waited for; matrix products, arithmetic and copies ran while one was open for 9% of the time, Pallas kernels for 7%

profile of v3, /device:TPU:1, one launch (start us, length us, event | category | flops | bytes accessed | tf_op | source)
XLA Modules:
  0.0 245.0 jit_solution(12525513056383094387)
XLA Ops:
  6.5 1.0 slice.29
  7.5 0.7 slice.31
  8.3 0.9 slice.30
  9.2 0.7 slice.32
  9.9 0.9 dynamic-slice_bitcast_fusion
  10.8 11.5 %all_gather.9 = bf16[160,1152]{1,0:T(8,128)(2,1)} all-gather(bf16[40,1152]{1,0:T(8,128)(2,1)S(1)} %dynamic-slice_bitcast_fusion), channel_id=1, replica_groups=mesh['z'=8,'core'=2,'y'=8,'x'=4] {'x'}, dimensions={0}, use_global_device_ids=true | all-gather | bytes 460800 | tf_op jit(solution)/shard_map/all_gather | solution.py:251
  22.3 0.8 pad_convert_fusion
  23.0 0.7 fusion.22
  23.7 1.0 concatenate.16
  24.8 5.0 %collective-permute-start.3 = (f32[12,128]{1,0:T(8,128)S(1)}, f32[12,128]{1,0:T(8,128)S(1)}, u32[]{:S(2)}, u32[]{:S(2)}) collective-permute-start(f32[12,128]{1,0:T(8,128)S(1)} %fusion.22), channel_id=1, source_target_pairs={{0,8},{4,28},{8,16},{12,4},{16,24},{20,12},{24,0},{28,20},{1,9},{5... | collective-permute-start | bytes 18440 | tf_op jit(solution)/shard_map/ppermute | solution.py:272
  29.8 4.6 %collective-permute-start.2 = (f32[12,128]{1,0:T(8,128)S(1)}, f32[12,128]{1,0:T(8,128)S(1)}, u32[]{:S(2)}, u32[]{:S(2)}) collective-permute-start(f32[12,128]{1,0:T(8,128)S(1)} %fusion.22), channel_id=1, source_target_pairs={{0,28},{4,0},{8,4},{12,8},{16,12},{20,16},{24,20},{28,24},{1,29},{... | collective-permute-start | bytes 18440 | tf_op jit(solution)/shard_map/ppermute | solution.py:272
  34.5 1.9 collective-permute-start.1
  36.4 4.4 %collective-permute-start = (bf16[80,2176]{1,0:T(8,128)(2,1)S(1)}, bf16[80,2176]{1,0:T(8,128)(2,1)S(1)}, u32[]{:S(2)}, u32[]{:S(2)}) collective-permute-start(bf16[80,2176]{1,0:T(8,128)(2,1)S(1)} %concatenate.16), channel_id=1, source_target_pairs={{0,16},{4,20},{8,24},{12,28},{16,0},{20,4},{24,8},{28,12},{1,17},{... | collective-permute-start | bytes 1044488 | tf_op jit(solution)/shard_map/ppermute | solution.py:270
  40.8 1.3 constant_dynamic-slice_fusion
  42.8 7.1 %fusion.26 = (f32[8,484]{1,0:T(8,128)S(1)}, f32[8,484,484]{1,2,0:T(8,128)}) fusion(bf16[484,8,72]{0,2,1:T(8,128)(2,1)} %bitcast.65, bf16[484,8,72]{0,2,1:T(8,128)(2,1)} %bitcast.66), kind=kOutput, calls=%fused_computation.46 | convolution fusion | flops 275485536 | bytes 8626816 | tf_op jit(solution)/shard_map/sub | solution.py:29
  49.9 4.2 %fusion.7 = bf16[8,484,72]{1,2,0:T(8,128)(2,1)S(1)} fusion(bf16[484,8,72]{0,2,1:T(8,128)(2,1)S(1)} %bitcast.67, f32[8,484,484]{1,2,0:T(8,128)} %get-tuple-element.34, f32[8,484]{1,0:T(8,128)S(1)} %get-tuple-element.33), kind=kOutput, calls=%fused_computation.9 | convolution fusion | flops 273889792 | bytes 8626816 | tf_op jit(solution)/shard_map/hqk,khd->qhd/dot_general | solution.py:31
  54.1 0.7 fusion.8
  54.8 0.3 copy.26
  55.1 0.8 select_n.66
  55.9 0.4 copy.27
  56.4 1.1 select_n.68
  57.5 0.9 pad.14.merged_ref
  59.7 0.9 pad_maximum_fusion.1.mix_ref
  60.6 0.9 pad_maximum_fusion
  61.5 27.9 %all-gather.3.cloned.1.call-done = bf16[2560,1152]{1,0:T(8,128)(2,1)} async-done(((bf16[160,1152]{1,0:T(8,128)(2,1)}), bf16[2560,1152]{1,0:T(8,128)(2,1)}) %all-gather.3.cloned.1.call-update) | async-done | bytes 5898256 | tf_op jit(solution)/shard_map/all_gather | solution.py:268
  89.4 6.3 %merge.1.refs_0_ = bf16[128,1280]{1,0:T(8,128)(2,1)} custom-call(bf16[128,2304]{1,0:T(8,128)(2,1)} %pad.14.merged_ref, bf16[2,1280,1152]{2,1,0:T(8,128)(2,1)} %bitcast.49), custom_call_target="tpu_custom_call" | custom-call | flops 754974720 | bytes 7340032 | tf_op jit(solution)/shard_map/merge/pallas_call | solution.py:94
  95.7 2.5 %collective-permute-start.4 = (bf16[128,1280]{1,0:T(8,128)(2,1)}, bf16[128,1280]{1,0:T(8,128)(2,1)S(1)}, u32[]{:S(2)}, u32[]{:S(2)}) collective-permute-start(bf16[128,1280]{1,0:T(8,128)(2,1)} %merge.1.refs_0_), channel_id=1, source_target_pairs={{0,4},{4,8},{8,12},{12,16},{16,20},{20,24},{24,28},{28,0},{1,5},{5... | collective-permute-start | bytes 983048 | tf_op jit(solution)/shard_map/ppermute | solution.py:289
  98.2 4.1 %collective-permute-start.5 = (bf16[128,1280]{1,0:T(8,128)(2,1)}, bf16[128,1280]{1,0:T(8,128)(2,1)S(1)}, u32[]{:S(2)}, u32[]{:S(2)}) collective-permute-start(bf16[128,1280]{1,0:T(8,128)(2,1)} %merge.1.refs_0_), channel_id=1, source_target_pairs={{0,28},{4,0},{8,4},{12,8},{16,12},{20,16},{24,20},{28,24},{1,29},{... | collective-permute-start | bytes 983048 | tf_op jit(solution)/shard_map/ppermute | solution.py:289
  102.3 1.9 collective-permute-start.6
  104.2 0.8 copy.31.table_ref
  105.1 3.1 %collective-permute-done.4.refs_1_ = bf16[128,1280]{1,0:T(8,128)(2,1)S(1)} collective-permute-done((bf16[128,1280]{1,0:T(8,128)(2,1)}, bf16[128,1280]{1,0:T(8,128)(2,1)S(1)}, u32[]{:S(2)}, u32[]{:S(2)}) %collective-permute-start.4) | collective-permute-done | bytes 327712 | tf_op jit(solution)/shard_map/ppermute | solution.py:289
  108.2 1.5 collective-permute-done.5.refs_2_
  109.7 5.2 %collective-permute-done.6.refs_3_ = bf16[128,1280]{1,0:T(8,128)(2,1)S(1)} collective-permute-done((bf16[128,1280]{1,0:T(8,128)(2,1)}, bf16[128,1280]{1,0:T(8,128)(2,1)S(1)}, u32[]{:S(2)}, u32[]{:S(2)}) %collective-permute-start.6) | collective-permute-done | bytes 327712 | tf_op jit(solution)/shard_map/ppermute | solution.py:289
  114.9 0.7 copy-done.5
  115.7 5.2 %pick_rows.1 = bf16[4,2,4,32,1280]{4,3,2,1,0:T(8,128)(2,1)} custom-call(bf16[4,256,128]{2,1,0:T(8,128)(2,1)} %copy.31.table_ref, bf16[128,1280]{1,0:T(8,128)(2,1)} %merge.1.refs_0_, bf16[128,1280]{1,0:T(8,128)(2,1)} %copy-done.3, bf16[128,1280]{1,0:T(8,128)(2,1)} %copy-done.4, bf16[128,1280]{1,0:T(8,128)(2,1)} %copy-done.5), custom_call_target="tpu_custom_call" | custom-call | flops 335544320 | bytes 5242880 | tf_op jit(solution)/shard_map/pick_rows/pallas_call | solution.py:125
  120.9 3.9 %all-to-all-start = ((bf16[4,256,1280]{2,1,0:T(8,128)(2,1)}), bf16[4,256,1280]{2,1,0:T(8,128)(2,1)S(1)}, u32[]{:S(2)}, u32[]{:S(2)}) async-start(bf16[4,256,1280]{2,1,0:T(8,128)(2,1)} %bitcast.48), calls=%async_computation | async-start | bytes 5242880 | tf_op jit(solution)/shard_map/all_to_all | solution.py:292
  124.8 0.6 broadcast_in_dim.77.gain_ref
  125.3 27.8 %all-to-all-done = bf16[4,256,1280]{2,1,0:T(8,128)(2,1)S(1)} async-done(((bf16[4,256,1280]{2,1,0:T(8,128)(2,1)}), bf16[4,256,1280]{2,1,0:T(8,128)(2,1)S(1)}, u32[]{:S(2)}, u32[]{:S(2)}) %all-to-all-start) | async-done | bytes 2621472 | tf_op jit(solution)/shard_map/all_to_all | solution.py:292
  153.2 10.4 %all-gather.5.cloned.1.call-done.weight_ref = bf16[1280,4352]{1,0:T(8,128)(2,1)} async-done(((bf16[80,4352]{1,0:T(8,128)(2,1)}), bf16[1280,4352]{1,0:T(8,128)(2,1)}) %all-gather.5.cloned.1.call-update) | async-done | bytes 11141136 | tf_op jit(solution)/shard_map/all_gather | solution.py:285
  163.6 11.4 %expert_ffn.1 = bf16[4,2,128,1280]{3,2,1,0:T(8,128)(2,1)} custom-call(bf16[4,2,128,1280]{3,2,1,0:T(8,128)(2,1)} %bitcast.50, f32[1,1280]{1,0:T(1,128)} %broadcast_in_dim.77.gain_ref, bf16[1280,4352]{1,0:T(8,128)(2,1)} %all-gather.5.cloned.1.call-done.weight_ref), custom_call_target="tpu_custom_call" | custom-call | flops 5536481280 | bytes 16777216 | tf_op jit(solution)/shard_map/expert_ffn/pallas_call | solution.py:175
  174.9 36.4 %all_to_all.10 = bf16[4,256,1280]{2,1,0:T(8,128)(2,1)} all-to-all(bf16[4,256,1280]{2,1,0:T(8,128)(2,1)} %bitcast.51), channel_id=1, replica_groups=mesh['z'=8,'core'=2,'y'=8,'x'=4] {'x'}, dimensions={0} | all-to-all | bytes 5242880 | tf_op jit(solution)/shard_map/all_to_all | solution.py:296
  211.3 4.9 %combine.3 = (bf16[128,1280]{1,0:T(8,128)(2,1)}, bf16[128,1280]{1,0:T(8,128)(2,1)}, bf16[128,1280]{1,0:T(8,128)(2,1)}) custom-call(bf16[4,256,256]{2,1,0:T(8,128)(2,1)} %pad_maximum_fusion.1.mix_ref, bf16[4,2,4,32,1280]{4,3,2,1,0:T(8,128)(2,1)} %bitcast.46), custom_call_target="tpu_custom_call" | custom-call | flops 503316480 | bytes 4194304 | tf_op jit(solution)/shard_map/combine/pallas_call | solution.py:205
  216.2 5.3 %collective-permute-start.9 = (bf16[128,1280]{1,0:T(8,128)(2,1)}, bf16[128,1280]{1,0:T(8,128)(2,1)S(1)}, u32[]{:S(2)}, u32[]{:S(2)}) collective-permute-start(bf16[128,1280]{1,0:T(8,128)(2,1)} %get-tuple-element.26), channel_id=1, source_target_pairs={{8,0},{28,4},{16,8},{4,12},{24,16},{12,20},{0,24},{20,28},{9,1},{2... | collective-permute-start | bytes 983048 | tf_op jit(solution)/shard_map/ppermute | solution.py:301
  221.6 1.9 collective-permute-start.8
  223.5 4.6 %collective-permute-start.7 = (bf16[128,1280]{1,0:T(8,128)(2,1)}, bf16[128,1280]{1,0:T(8,128)(2,1)S(1)}, u32[]{:S(2)}, u32[]{:S(2)}) collective-permute-start(bf16[128,1280]{1,0:T(8,128)(2,1)} %get-tuple-element.24), channel_id=1, source_target_pairs={{4,0},{8,4},{12,8},{16,12},{20,16},{24,20},{28,24},{0,28},{5,1},{9... | collective-permute-start | bytes 983048 | tf_op jit(solution)/shard_map/ppermute | solution.py:301
  228.1 4.7 %combine.2 = f32[128,1280]{1,0:T(8,128)} custom-call(bf16[4,256,256]{2,1,0:T(8,128)(2,1)} %pad_maximum_fusion.1.mix_ref, bf16[4,2,4,32,1280]{4,3,2,1,0:T(8,128)(2,1)} %bitcast.47), custom_call_target="tpu_custom_call" | custom-call | flops 167772160 | bytes 4194304 | tf_op jit(solution)/shard_map/combine/pallas_call | solution.py:205
  232.8 3.4 %collective-permute-done.8 = bf16[128,1280]{1,0:T(8,128)(2,1)S(1)} collective-permute-done((bf16[128,1280]{1,0:T(8,128)(2,1)}, bf16[128,1280]{1,0:T(8,128)(2,1)S(1)}, u32[]{:S(2)}, u32[]{:S(2)}) %collective-permute-start.8) | collective-permute-done | bytes 327712 | tf_op jit(solution)/shard_map/ppermute | solution.py:301
  236.2 2.0 fusion.15
  (48 shorter events, 1.5 us)
Async XLA Ops:
  6.5 47.5 %copy-start = (bf16[576,576]{1,0:T(8,128)(2,1)S(1)}, bf16[576,576]{1,0:T(8,128)(2,1)}, u32[]{:S(2)}) copy-start(bf16[576,576]{1,0:T(8,128)(2,1)} %param.17) | copy-start | bytes 1990660
  6.5 82.8 %all-gather.3.cloned.1.call-start = ((), (), s32[]{:S(2)}) async-start(), calls=%async_computation.2 | async-start | bytes 6266880 | tf_op jit(solution)/shard_map/all_gather | solution.py:268
  22.3 27.6 %copy-start.7 = (bf16[484,576]{0,1:T(8,128)(2,1)S(1)}, bf16[484,576]{0,1:T(8,128)(2,1)}, u32[]{:S(2)}) copy-start(bf16[484,576]{0,1:T(8,128)(2,1)} %param.15) | copy-start | bytes 1672708
  24.8 138.8 %all-gather.5.cloned.1.call-start = ((), (), s32[]{:S(2)}) async-start(), calls=%async_computation.3 | async-start | bytes 11837440 | tf_op jit(solution)/shard_map/all_gather | solution.py:285
  24.8 33.7 %collective-permute-start.3 = (f32[12,128]{1,0:T(8,128)S(1)}, f32[12,128]{1,0:T(8,128)S(1)}, u32[]{:S(2)}, u32[]{:S(2)}) collective-permute-start(f32[12,128]{1,0:T(8,128)S(1)} %fusion.22), channel_id=1, source_target_pairs={{0,8},{4,28},{8,16},{12,4},{16,24},{20,12},{24,0},{28,20},{1,9},{5... | collective-permute-start | bytes 18440 | tf_op jit(solution)/shard_map/ppermute | solution.py:272
  29.8 28.7 %collective-permute-start.2 = (f32[12,128]{1,0:T(8,128)S(1)}, f32[12,128]{1,0:T(8,128)S(1)}, u32[]{:S(2)}, u32[]{:S(2)}) collective-permute-start(f32[12,128]{1,0:T(8,128)S(1)} %fusion.22), channel_id=1, source_target_pairs={{0,28},{4,0},{8,4},{12,8},{16,12},{20,16},{24,20},{28,24},{1,29},{... | collective-permute-start | bytes 18440 | tf_op jit(solution)/shard_map/ppermute | solution.py:272
  34.5 24.1 %collective-permute-start.1 = (f32[12,128]{1,0:T(8,128)S(1)}, f32[12,128]{1,0:T(8,128)S(1)}, u32[]{:S(2)}, u32[]{:S(2)}) collective-permute-start(f32[12,128]{1,0:T(8,128)S(1)} %fusion.22), channel_id=1, source_target_pairs={{0,4},{4,8},{8,12},{12,16},{16,20},{20,24},{24,28},{28,0},{1,5},{5... | collective-permute-start | bytes 18440 | tf_op jit(solution)/shard_map/ppermute | solution.py:272
  36.4 24.2 %collective-permute-start = (bf16[80,2176]{1,0:T(8,128)(2,1)S(1)}, bf16[80,2176]{1,0:T(8,128)(2,1)S(1)}, u32[]{:S(2)}, u32[]{:S(2)}) collective-permute-start(bf16[80,2176]{1,0:T(8,128)(2,1)S(1)} %concatenate.16), channel_id=1, source_target_pairs={{0,16},{4,20},{8,24},{12,28},{16,0},{20,4},{24,8},{28,12},{1,17},{... | collective-permute-start | bytes 1044488 | tf_op jit(solution)/shard_map/ppermute | solution.py:270
  49.9 4.2 %copy-start.8 = (bf16[484,576]{0,1:T(8,128)(2,1)S(1)}, bf16[484,576]{0,1:T(8,128)(2,1)}, u32[]{:S(2)}) copy-start(bf16[484,576]{0,1:T(8,128)(2,1)} %param.16) | copy-start | bytes 1672708
  95.7 29.1 %copy-start.6 = (f32[1280]{0:T(1024)S(1)}, f32[1280]{0:T(1024)}, u32[]{:S(2)}) copy-start(f32[1280]{0:T(1024)} %param.19) | copy-start | bytes 15364
  95.7 12.5 %collective-permute-start.4 = (bf16[128,1280]{1,0:T(8,128)(2,1)}, bf16[128,1280]{1,0:T(8,128)(2,1)S(1)}, u32[]{:S(2)}, u32[]{:S(2)}) collective-permute-start(bf16[128,1280]{1,0:T(8,128)(2,1)} %merge.1.refs_0_), channel_id=1, source_target_pairs={{0,4},{4,8},{8,12},{12,16},{16,20},{20,24},{24,28},{28,0},{1,5},{5... | collective-permute-start | bytes 983048 | tf_op jit(solution)/shard_map/ppermute | solution.py:289
  98.2 11.5 %collective-permute-start.5 = (bf16[128,1280]{1,0:T(8,128)(2,1)}, bf16[128,1280]{1,0:T(8,128)(2,1)S(1)}, u32[]{:S(2)}, u32[]{:S(2)}) collective-permute-start(bf16[128,1280]{1,0:T(8,128)(2,1)} %merge.1.refs_0_), channel_id=1, source_target_pairs={{0,28},{4,0},{8,4},{12,8},{16,12},{20,16},{24,20},{28,24},{1,29},{... | collective-permute-start | bytes 983048 | tf_op jit(solution)/shard_map/ppermute | solution.py:289
  102.3 12.6 %collective-permute-start.6 = (bf16[128,1280]{1,0:T(8,128)(2,1)}, bf16[128,1280]{1,0:T(8,128)(2,1)S(1)}, u32[]{:S(2)}, u32[]{:S(2)}) collective-permute-start(bf16[128,1280]{1,0:T(8,128)(2,1)} %merge.1.refs_0_), channel_id=1, source_target_pairs={{0,8},{4,28},{8,16},{12,4},{16,24},{20,12},{24,0},{28,20},{1,9},{5... | collective-permute-start | bytes 983048 | tf_op jit(solution)/shard_map/ppermute | solution.py:289
  108.2 6.8 %copy-start.3 = (bf16[128,1280]{1,0:T(8,128)(2,1)}, bf16[128,1280]{1,0:T(8,128)(2,1)S(1)}, u32[]{:S(2)}) copy-start(bf16[128,1280]{1,0:T(8,128)(2,1)S(1)} %collective-permute-done.4.refs_1_) | copy-start | bytes 983044
  109.7 5.2 %copy-start.4 = (bf16[128,1280]{1,0:T(8,128)(2,1)}, bf16[128,1280]{1,0:T(8,128)(2,1)S(1)}, u32[]{:S(2)}) copy-start(bf16[128,1280]{1,0:T(8,128)(2,1)S(1)} %collective-permute-done.5.refs_2_) | copy-start | bytes 983044
  114.9 0.7 copy-start.5
  120.9 32.3 %all-to-all-start = ((bf16[4,256,1280]{2,1,0:T(8,128)(2,1)}), bf16[4,256,1280]{2,1,0:T(8,128)(2,1)S(1)}, u32[]{:S(2)}, u32[]{:S(2)}) async-start(bf16[4,256,1280]{2,1,0:T(8,128)(2,1)} %bitcast.48), calls=%async_computation | async-start | bytes 5242880 | tf_op jit(solution)/shard_map/all_to_all | solution.py:292
  153.2 10.4 %copy-start.2 = (bf16[4,256,1280]{2,1,0:T(8,128)(2,1)}, bf16[4,256,1280]{2,1,0:T(8,128)(2,1)S(1)}, u32[]{:S(2)}) copy-start(bf16[4,256,1280]{2,1,0:T(8,128)(2,1)S(1)} %all-to-all-done) | copy-start | bytes 7864324
  174.9 61.3 %copy-start.1 = (bf16[128,1280]{1,0:T(8,128)(2,1)S(1)}, bf16[128,1280]{1,0:T(8,128)(2,1)}, u32[]{:S(2)}) copy-start(bf16[128,1280]{1,0:T(8,128)(2,1)} %merge.1.refs_0_) | copy-start | bytes 983044
  216.2 16.5 %collective-permute-start.9 = (bf16[128,1280]{1,0:T(8,128)(2,1)}, bf16[128,1280]{1,0:T(8,128)(2,1)S(1)}, u32[]{:S(2)}, u32[]{:S(2)}) collective-permute-start(bf16[128,1280]{1,0:T(8,128)(2,1)} %get-tuple-element.26), channel_id=1, source_target_pairs={{8,0},{28,4},{16,8},{4,12},{24,16},{12,20},{0,24},{20,28},{9,1},{2... | collective-permute-start | bytes 983048 | tf_op jit(solution)/shard_map/ppermute | solution.py:301
  221.6 14.6 %collective-permute-start.8 = (bf16[128,1280]{1,0:T(8,128)(2,1)}, bf16[128,1280]{1,0:T(8,128)(2,1)S(1)}, u32[]{:S(2)}, u32[]{:S(2)}) collective-permute-start(bf16[128,1280]{1,0:T(8,128)(2,1)} %get-tuple-element.25), channel_id=1, source_target_pairs={{28,0},{0,4},{4,8},{8,12},{12,16},{16,20},{20,24},{24,28},{29,1},{... | collective-permute-start | bytes 983048 | tf_op jit(solution)/shard_map/ppermute | solution.py:301
  223.5 12.7 %collective-permute-start.7 = (bf16[128,1280]{1,0:T(8,128)(2,1)}, bf16[128,1280]{1,0:T(8,128)(2,1)S(1)}, u32[]{:S(2)}, u32[]{:S(2)}) collective-permute-start(bf16[128,1280]{1,0:T(8,128)(2,1)} %get-tuple-element.24), channel_id=1, source_target_pairs={{4,0},{8,4},{12,8},{16,12},{20,16},{24,20},{28,24},{0,28},{5,1},{9... | collective-permute-start | bytes 983048 | tf_op jit(solution)/shard_map/ppermute | solution.py:301
Sparse Core Ops, SparseCore 0:
  24.9 64.3 all-gather.2
  91.5 72.0 all-gather.4

commit v4 on v3

--- a/solution.py
+++ b/solution.py
@@ -110,78 +110,113 @@
     )(merged, weight)
 
 
-def pick_body(table_ref, *refs):
+def pick_body(table_ref, tile_ref, *refs):
     send_ref = refs[-1]
-    cols, hosted, _, slot, width = send_ref.shape
-    for i, tile_ref in enumerate(refs[:-1]):
-        rows = jnp.dot(table_ref[i], tile_ref[...], preferred_element_type=jnp.float32)
-        send_ref[:, :, i] = rows.astype(jnp.bfloat16).reshape(cols, hosted, slot, width)
-
-
-def pick_rows(table, tiles, cols, hosted):
-    width = tiles[0].shape[1]
-    block = 256
-    count = len(tiles)
+    rows = jnp.dot(table_ref[0], tile_ref[...], preferred_element_type=jnp.float32)
+    send_ref[...] = rows.astype(jnp.bfloat16).reshape(send_ref.shape)
+
+
+def pick_rows(table, index, tile, shape, send=None):
+    cols, hosted, _, slot, width = shape
+    given = [] if send is None else [send]
     return pl.pallas_call(
         pick_body,
-        grid=(width // block,),
-        in_specs=[pl.BlockSpec(table.shape, lambda i: (0, 0, 0))]
-        + [pl.BlockSpec((TPAD, block), lambda i: (0, i))] * count,
-        out_specs=pl.BlockSpec((cols, hosted, count, SLOT, block), lambda i: (0, 0, 0, 0, i)),
-        out_shape=jax.ShapeDtypeStruct((cols, hosted, count, SLOT, width), jnp.bfloat16),
+        grid=(1,),
+        in_specs=[
+            pl.BlockSpec((1,) + table.shape[1:], lambda i: (index, 0, 0)),
+            pl.BlockSpec(tile.shape, lambda i: (0, 0)),
+        ]
+        + [pl.BlockSpec(memory_space=pl.ANY)] * len(given),
+        out_specs=pl.BlockSpec((cols, hosted, 1, slot, width), lambda i: (0, 0, index, 0, 0)),
+        out_shape=jax.ShapeDtypeStruct(shape, jnp.bfloat16),
+        input_output_aliases={2: 0} if given else {},
         compiler_params=pltpu.CompilerParams(vmem_limit_bytes=60 << 20),
         cost_estimate=pl.CostEstimate(
-            flops=2 * TPAD * width * count * table.shape[1],
-            bytes_accessed=5 << 20,
+            flops=2 * TPAD * width * table.shape[1],
+            bytes_accessed=1 << 20,
             transcendentals=0,
         ),
         name="pick_rows",
-    )(table, *tiles)
-
-
-def expert_body(hidden, main, rows_ref, gain_ref, weight_ref, out_ref):
-    width = rows_ref.shape[-1]
-    wide = rows_ref[...].reshape(-1, width).astype(jnp.float32)
-    scale = lax.rsqrt(jnp.mean(wide * wide, axis=-1, keepdims=True) + 1e-06)
-    normed = (wide * scale * gain_ref[...]).astype(jnp.bfloat16)
-    both = jnp.dot(normed, weight_ref[:, : 2 * hidden], preferred_element_type=jnp.float32)
+    )(table, tile, *given)
+
+
+def expert_body(hidden, main, rows_any, gain_ref, weight_any, out_any, rows, weight, out, sems):
+    cols, hosted, count, width = rows_any.shape
+    span = weight_any.shape[1] // hosted
+    first = 2 * hidden
+    copies = []
+    for j in range(hosted):
+        copies.append(
+            [
+                pltpu.make_async_copy(rows_any.at[:, j], rows.at[j], sems.at[j, 0]),
+                pltpu.make_async_copy(
+                    weight_any.at[:, pl.ds(j * span, first)],
+                    weight.at[j, :, pl.ds(0, first)],
+                    sems.at[j, 1],
+                ),
+                pltpu.make_async_copy(
+                    weight_any.at[:, pl.ds(j * span + first, span - first)],
+                    weight.at[j, :, pl.ds(first, span - first)],
+                    sems.at[j, 2],
+                ),
+            ]
+        )
+    for group in copies:
+        for copy in group:
+            copy.start()
 
     def gated(gate, up):
         return (gate / (1.0 + jnp.exp(-gate)) * up).astype(jnp.bfloat16)
 
     rest = hidden - main
-    act = jnp.concatenate(
-        [
-            gated(both[:, :main], both[:, main : 2 * main]),
-            gated(both[:, 2 * main : 2 * main + rest], both[:, 2 * main + rest :]),
-        ],
-        axis=1,
-    )
-    out_ref[...] = (
-        lax.dot_general(
-            act,
-            weight_ref[:, 2 * hidden : 3 * hidden],
-            (((1,), (1,)), ((), ())),
-            preferred_element_type=jnp.float32,
+    results = []
+    for j in range(hosted):
+        copies[j][0].wait()
+        wide = rows[j].reshape(-1, width).astype(jnp.float32)
+        scale = lax.rsqrt(jnp.mean(wide * wide, axis=-1, keepdims=True) + 1e-06)
+        normed = (wide * scale * gain_ref[...]).astype(jnp.bfloat16)
+        copies[j][1].wait()
+        both = jnp.dot(normed, weight[j, :, :first], preferred_element_type=jnp.float32)
+        act = jnp.concatenate(
+            [
+                gated(both[:, :main], both[:, main : 2 * main]),
+                gated(both[:, 2 * main : 2 * main + rest], both[:, 2 * main + rest :]),
+            ],
+            axis=1,
         )
-        .astype(jnp.bfloat16)
-        .reshape(out_ref.shape)
-    )
+        copies[j][2].wait()
+        out[j] = (
+            lax.dot_general(
+                act,
+                weight[j, :, first : first + hidden],
+                (((1,), (1,)), ((), ())),
+                preferred_element_type=jnp.float32,
+            )
+            .astype(jnp.bfloat16)
+            .reshape(cols, count, width)
+        )
+        result = pltpu.make_async_copy(out.at[j], out_any.at[:, j], sems.at[j, 3])
+        result.start()
+        results.append(result)
+    for result in results:
+        result.wait()
 
 
 def expert_ffn(rows, gain, weight, hidden, main):
     cols, hosted, count, width = rows.shape
-    place = lambda j: (0, j, 0, 0)
+    held = (hosted, cols, count, width)
+    anywhere = pl.BlockSpec(memory_space=pl.ANY)
     return pl.pallas_call(
         functools.partial(expert_body, hidden, main),
-        grid=(hosted,),
-        in_specs=[
-            pl.BlockSpec((cols, 1, count, width), place),
-            pl.BlockSpec((1, width), lambda j: (0, 0)),
-            pl.BlockSpec((width, weight.shape[1] // hosted), lambda j: (0, j)),
+        in_specs=[anywhere, pl.BlockSpec(memory_space=pltpu.VMEM), anywhere],
+        out_specs=anywhere,
+        out_shape=jax.ShapeDtypeStruct(rows.shape, jnp.bfloat16),
+        scratch_shapes=[
+            pltpu.VMEM(held, jnp.bfloat16),
+            pltpu.VMEM((hosted, width, weight.shape[1] // hosted), jnp.bfloat16),
+            pltpu.VMEM(held, jnp.bfloat16),
+            pltpu.SemaphoreType.DMA((hosted, 4)),
         ],
-        out_specs=pl.BlockSpec((cols, 1, count, width), place),
-        out_shape=jax.ShapeDtypeStruct(rows.shape, jnp.bfloat16),
         compiler_params=pltpu.CompilerParams(vmem_limit_bytes=60 << 20),
         cost_estimate=pl.CostEstimate(
             flops=6 * cols * hosted * count * width * hidden,
@@ -192,29 +227,27 @@
     )(rows, gain, weight)
 
 
-def combine_body(base, mix_ref, back_ref, *refs):
-    for i, out_ref in enumerate(refs):
-        back = back_ref[:, :, base + i].reshape(mix_ref.shape[2], out_ref.shape[1])
-        both = jnp.dot(mix_ref[base + i], back, preferred_element_type=jnp.float32)
-        out_ref[...] = (both[:TPAD] + both[TPAD:]).astype(out_ref.dtype)
-
-
-def combine(mix, back, base, count, dtype):
-    cols, hosted, tiles, slot, width = back.shape
-    block = 256
+def combine_body(mix_ref, back_ref, out_ref):
+    back = back_ref[...].reshape(mix_ref.shape[2], out_ref.shape[1])
+    both = jnp.dot(mix_ref[0], back, preferred_element_type=jnp.float32)
+    out_ref[...] = (both[:TPAD] + both[TPAD:]).astype(out_ref.dtype)
+
+
+def combine(mix, back, index, dtype):
+    cols, hosted, _, slot, width = back.shape
     return pl.pallas_call(
-        functools.partial(combine_body, base),
-        grid=(width // block,),
+        combine_body,
+        grid=(1,),
         in_specs=[
-            pl.BlockSpec(mix.shape, lambda i: (0, 0, 0)),
-            pl.BlockSpec((cols, hosted, tiles, slot, block), lambda i: (0, 0, 0, 0, i)),
+            pl.BlockSpec((1,) + mix.shape[1:], lambda i: (index, 0, 0)),
+            pl.BlockSpec((cols, hosted, 1, slot, width), lambda i: (0, 0, index, 0, 0)),
         ],
-        out_specs=[pl.BlockSpec((TPAD, block), lambda i: (0, i))] * count,
-        out_shape=[jax.ShapeDtypeStruct((TPAD, width), dtype)] * count,
-        compiler_params=pltpu.CompilerParams(vmem_limit_bytes=60 << 20),
+        out_specs=pl.BlockSpec((TPAD, width), lambda i: (0, 0)),
+        out_shape=jax.ShapeDtypeStruct((TPAD, width), dtype),
+        compiler_params=pltpu.CompilerParams(vmem_limit_bytes=24 << 20),
         cost_estimate=pl.CostEstimate(
-            flops=4 * TPAD * width * count * mix.shape[2],
-            bytes_accessed=4 << 20,
+            flops=4 * TPAD * width * mix.shape[2],
+            bytes_accessed=1 << 20,
             transcendentals=0,
         ),
         name="combine",
@@ -248,7 +281,15 @@
 
     half = w_merge.shape[0] // 2
     piece = lax.dynamic_slice_in_dim(w_merge.T, lax.axis_index("core") * half, half, 1)
-    piece = lax.all_gather(piece, "x", axis=0, tiled=True)
+    piece = lax.all_to_all(
+        jnp.broadcast_to(piece[None], (cols,) + piece.shape), "x", split_axis=0, concat_axis=0
+    )
+    piece = piece.reshape(-1, half)
+    queries, w_gate, w_up, w_down, routes, route_weight, piece = lax.optimization_barrier(
+        (queries, w_gate, w_up, w_down, routes, route_weight, piece)
+    )
+    merger = lax.all_gather(piece, ("core", "y"), axis=0, tiled=True)
+    merger = merger.reshape(2, -1, half)
 
     edge = -(-3 * hidden // 128) * 128 - 3 * hidden
     main = hidden // 128 * 128
@@ -264,10 +305,13 @@
         ],
         axis=1,
     ).T
-    piece, own, routing = lax.optimization_barrier((piece, own, routing))
-    merger = lax.all_gather(piece, ("core", "y"), axis=0, tiled=True)
-    merger = merger.reshape(2, -1, half)
-    other = lax.ppermute(own, "y", shift(rows, rows // 2))
+    middle = own.shape[0] // 2
+    ways = []
+    for part, step in ((own[:middle], rows // 4), (own[middle:], -(rows // 4))):
+        for _ in range(2):
+            part = lax.ppermute(part, "y", shift(rows, step))
+        ways.append(part)
+    other = jnp.concatenate(ways, axis=0)
     steps = (shift(rows, 1), shift(rows, -1), far_shift(rows))
     info = jnp.stack([routing] + [lax.ppermute(routing, "y", step) for step in steps])
     hosted = jnp.stack([row, (row + rows // 2) % rows])
@@ -286,19 +330,25 @@
 
     stream = merge(merged, merger)
     width = stream.shape[1]
-    tiles = [stream] + [lax.ppermute(stream, "y", step) for step in steps]
-    send = pick_rows(table, tiles, cols, 2)
+    shape = (cols, 2, 1 + len(steps), SLOT, width)
+    arrived = [lax.ppermute(stream, "y", step) for step in steps]
+    send = pick_rows(table, 0, stream, shape)
+    for i, tile in enumerate(arrived):
+        send = pick_rows(table, i + 1, tile, shape, send)
     flat = (cols, send.size // cols // width, width)
     received = lax.all_to_all(send.reshape(flat), "x", split_axis=0, concat_axis=0)
     outcome = expert_ffn(
         received.reshape(cols, 2, -1, width), rms_gain[None, :], experts, hidden, main
     )
     back = lax.all_to_all(outcome.reshape(flat), "x", split_axis=0, concat_axis=0)
-    back = back.reshape(send.shape)
-    parts = combine(mix, back, 1, len(steps), jnp.bfloat16)
-    total = combine(mix, back, 0, 1, jnp.float32)[0] + stream.astype(jnp.float32)
-    for part, step in zip(parts, steps):
-        total = total + lax.ppermute(part, "y", back_again(step)).astype(jnp.float32)
+    back = back.reshape(shape)
+    parts = [
+        lax.ppermute(combine(mix, back, i + 1, jnp.bfloat16), "y", back_again(step))
+        for i, step in enumerate(steps)
+    ]
+    total = combine(mix, back, 0, jnp.float32) + stream.astype(jnp.float32)
+    for part in parts:
+        total = total + part.astype(jnp.float32)
     return total[:tokens].astype(jnp.bfloat16)
 
 

time: 246 us -> 236 us (0.959)
  waiting for transfers between devices: 79.4 us -> 64.5 us
  starting transfers between devices: 40.1 us -> 50.5 us
  Pallas kernels: 32.5 us -> 28.5 us
  other arithmetic: 5.67 us -> 2.8 us
  local copies, waits for them, and re-layouts: 13 us -> 15.6 us
    all_gather x1, waiting for transfers between devices: 27.9 us -> 4.44 us  [local(): merger = lax.all_gather(piece, ('core', 'y'), axis=0, tiled=True)]
    all_gather x1 -> x0, blocking collectives: 11.5 us -> none  [local(): piece = lax.all_gather(piece, 'x', axis=0, tiled=True)]
    all_to_all x0 -> x1, blocking collectives: none -> 10.8 us  [local(): lax.all_to_all(jnp.broadcast_to(piece[None], (cols,) + piece.shape), 'x',...]
    ppermute x7 -> x10, starting transfers between devices: 24.7 us -> 34.2 us  [the longest x4 13.5 us: local(): part = lax.ppermute(part, 'y', shift(rows, step))]
    ppermute x7 -> x10, waiting for transfers between devices: 13.3 us -> 20.3 us  [the longest x4 11.6 us: local(): part = lax.ppermute(part, 'y', shift(rows, step))]
    pallas_call x4 -> x9, Pallas kernels: 26.2 us -> 22.2 us  [the longest x1 12.1 us: expert_ffn(): pl.pallas_call(functools.partial(expert_body, hidden, main), in_specs=[an...]
    all_gather x1, waiting for transfers between devices: 10.4 us -> 13.5 us  [local(): experts = lax.all_gather(mine, ('z', 'core'), axis=0, tiled=True)]
  transfers between devices with their start and end apart: 13 -> 16, of which waited for: 7 -> 8; matrix products, arithmetic and copies ran while one was open for 9% -> 11% of each run, Pallas kernels for 7% -> 7%
where the time goes in v4:
time: 236 us; the launch traced here: 235 us
  waiting for transfers between devices  64.5 us (27%)
  starting transfers between devices  50.5 us (21%)
  blocking collectives  46.3 us (20%)
  Pallas kernels  28.5 us (12%)
  local copies, waits for them, and re-layouts  15.6 us (7%)
  between operations  14.5 us (6%)
  matrix products  12.1 us (5%)
  other arithmetic  2.8 us (1%)
    all_to_all x1, blocking collectives, local(): lax.all_to_all(outcome.reshape(flat), 'x', split_axis=0, concat_axis=0)  35.5 us
    all_to_all x1, waiting for transfers between devices, local(): lax.all_to_all(send.reshape(flat), 'x', split_axis=0, concat_axis=0)  26.3 us
    ppermute x4, starting transfers between devices, local(): part = lax.ppermute(part, 'y', shift(rows, step))  13.5 us
    all_gather x1, waiting for transfers between devices, local(): experts = lax.all_gather(mine, ('z', 'core'), axis=0, tiled=True)  13.5 us
    pallas_call x1, Pallas kernels, expert_ffn(): pl.pallas_call(functools.partial(expert_body, hidden, main), in_specs=[an...  12.1 us
    ppermute x3, starting transfers between devices, local(): lax.ppermute(combine(mix, back, i + 1, jnp.bfloat16), 'y', back_again(step))  11.8 us
    ppermute x3, starting transfers between devices, local(): lax.ppermute(routing, 'y', step)  11.6 us
    ppermute x4, waiting for transfers between devices, local(): part = lax.ppermute(part, 'y', shift(rows, step))  11.6 us
  transfers between devices with their start and end apart: 16, of which 8 were waited for; matrix products, arithmetic and copies ran while one was open for 11% of the time, Pallas kernels for 7%

profile of v4, /device:TPU:1, one launch (start us, length us, event | category | flops | bytes accessed | tf_op | source)
XLA Modules:
  0.0 235.0 jit_solution(12400721827843137732)
XLA Ops:
  6.5 1.0 dynamic-slice_bitcast_fusion
  7.5 10.8 %all_to_all.15 = bf16[4,40,1152]{2,1,0:T(8,128)(2,1)} all-to-all(bf16[4,40,1152]{2,1,0:T(8,128)(2,1)S(1)} %broadcast_in_dim.71), channel_id=1, replica_groups=mesh['z'=8,'core'=2,'y'=8,'x'=4] {'x'}, dimensions={0} | all-to-all | bytes 737280 | tf_op jit(solution)/shard_map/all_to_all | solution.py:284
  18.7 1.2 constant_dynamic-slice_fusion
  20.6 0.9 slice.37
  21.6 0.7 slice.39
  22.3 0.9 slice.38
  23.2 0.7 slice.40
  24.6 0.7 fusion.22
  25.3 5.0 %collective-permute-start.6 = (f32[12,128]{1,0:T(8,128)S(1)}, f32[12,128]{1,0:T(8,128)S(1)}, u32[]{:S(2)}, u32[]{:S(2)}) collective-permute-start(f32[12,128]{1,0:T(8,128)S(1)} %get-tuple-element.38), channel_id=1, source_target_pairs={{0,8},{4,28},{8,16},{12,4},{16,24},{20,12},{24,0},{28,20},{1,9},{5... | collective-permute-start | bytes 18440 | tf_op jit(solution)/shard_map/ppermute | solution.py:316
  30.3 4.6 %collective-permute-start.5 = (f32[12,128]{1,0:T(8,128)S(1)}, f32[12,128]{1,0:T(8,128)S(1)}, u32[]{:S(2)}, u32[]{:S(2)}) collective-permute-start(f32[12,128]{1,0:T(8,128)S(1)} %get-tuple-element.38), channel_id=1, source_target_pairs={{0,28},{4,0},{8,4},{12,8},{16,12},{20,16},{24,20},{28,24},{1,29},{... | collective-permute-start | bytes 18440 | tf_op jit(solution)/shard_map/ppermute | solution.py:316
  35.0 1.9 collective-permute-start.4
  36.9 1.1 concatenate.20
  38.1 3.1 %collective-permute-start.2 = (bf16[40,2176]{1,0:T(8,128)(2,1)S(1)}, bf16[40,2176]{1,0:T(8,128)(2,1)S(1)}, u32[]{:S(2)}, u32[]{:S(2)}) collective-permute-start(bf16[40,2176]{1,0:T(8,128)(2,1)S(1)} %get-tuple-element.34), channel_id=1, source_target_pairs={{0,24},{4,28},{8,0},{12,4},{16,8},{20,12},{24,16},{28,20},{1,25},{... | collective-permute-start | bytes 522248 | tf_op jit(solution)/shard_map/ppermute | solution.py:312
  41.1 3.1 %collective-permute-start = (bf16[40,2176]{1,0:T(8,128)(2,1)S(1)}, bf16[40,2176]{1,0:T(8,128)(2,1)S(1)}, u32[]{:S(2)}, u32[]{:S(2)}) collective-permute-start(bf16[40,2176]{1,0:T(8,128)(2,1)S(1)} %get-tuple-element.33), channel_id=1, source_target_pairs={{0,8},{4,12},{8,16},{12,20},{16,24},{20,28},{24,0},{28,4},{1,9},{5... | collective-permute-start | bytes 522248 | tf_op jit(solution)/shard_map/ppermute | solution.py:312
  44.3 7.1 %fusion.28 = (f32[8,484]{1,0:T(8,128)S(1)}, f32[8,484,484]{1,2,0:T(8,128)}) fusion(bf16[484,8,72]{0,2,1:T(8,128)(2,1)} %bitcast.70, bf16[484,8,72]{0,2,1:T(8,128)(2,1)} %bitcast.71), kind=kOutput, calls=%fused_computation.48 | convolution fusion | flops 275485536 | bytes 8626816 | tf_op jit(solution)/shard_map/sub | solution.py:29
  51.4 4.2 %fusion.7 = bf16[8,484,72]{1,2,0:T(8,128)(2,1)S(1)} fusion(bf16[484,8,72]{0,2,1:T(8,128)(2,1)S(1)} %bitcast.72, f32[8,484,484]{1,2,0:T(8,128)} %get-tuple-element.40, f32[8,484]{1,0:T(8,128)S(1)} %get-tuple-element.39), kind=kOutput, calls=%fused_computation.9 | convolution fusion | flops 273889792 | bytes 8626816 | tf_op jit(solution)/shard_map/hqk,khd->qhd/dot_general | solution.py:31
  56.7 0.8 select_n.66
  57.9 1.1 select_n.68
  59.0 0.9 pad.12.merged_ref
  61.0 4.3 %collective-permute-start.3 = (bf16[40,2176]{1,0:T(8,128)(2,1)S(1)}, bf16[40,2176]{1,0:T(8,128)(2,1)S(1)}, u32[]{:S(2)}, u32[]{:S(2)}) collective-permute-start(bf16[40,2176]{1,0:T(8,128)(2,1)S(1)} %collective-permute-done.2), channel_id=1, source_target_pairs={{0,24},{4,28},{8,0},{12,4},{16,8},{20,12},{24,16},{28,20},{1,25},{... | collective-permute-start | bytes 522248 | tf_op jit(solution)/shard_map/ppermute | solution.py:312
  65.3 3.0 %collective-permute-start.1 = (bf16[40,2176]{1,0:T(8,128)(2,1)S(1)}, bf16[40,2176]{1,0:T(8,128)(2,1)S(1)}, u32[]{:S(2)}, u32[]{:S(2)}) collective-permute-start(bf16[40,2176]{1,0:T(8,128)(2,1)S(1)} %collective-permute-done), channel_id=1, source_target_pairs={{0,8},{4,12},{8,16},{12,20},{16,24},{20,28},{24,0},{28,4},{1,9},{5... | collective-permute-start | bytes 522248 | tf_op jit(solution)/shard_map/ppermute | solution.py:312
  68.5 8.7 %collective-permute-done.3 = bf16[40,2176]{1,0:T(8,128)(2,1)S(1)} collective-permute-done((bf16[40,2176]{1,0:T(8,128)(2,1)S(1)}, bf16[40,2176]{1,0:T(8,128)(2,1)S(1)}, u32[]{:S(2)}, u32[]{:S(2)}) %collective-permute-start.3) | collective-permute-done | bytes 174112 | tf_op jit(solution)/shard_map/ppermute | solution.py:312
  77.2 2.8 %collective-permute-done.1 = bf16[40,2176]{1,0:T(8,128)(2,1)S(1)} collective-permute-done((bf16[40,2176]{1,0:T(8,128)(2,1)S(1)}, bf16[40,2176]{1,0:T(8,128)(2,1)S(1)}, u32[]{:S(2)}, u32[]{:S(2)}) %collective-permute-start.1) | collective-permute-done | bytes 174112 | tf_op jit(solution)/shard_map/ppermute | solution.py:312
  80.1 1.0 concatenate.22
  81.1 4.4 %all-gather.3.cloned.1.call-done = bf16[2560,1152]{1,0:T(8,128)(2,1)} async-done(((bf16[160,1152]{1,0:T(8,128)(2,1)}), bf16[2560,1152]{1,0:T(8,128)(2,1)}) %all-gather.3.cloned.1.call-update) | async-done | bytes 5898256 | tf_op jit(solution)/shard_map/all_gather | solution.py:291
  85.6 6.3 %merge.1.tile_ref = bf16[128,1280]{1,0:T(8,128)(2,1)} custom-call(bf16[128,2304]{1,0:T(8,128)(2,1)} %pad.12.merged_ref, bf16[2,1280,1152]{2,1,0:T(8,128)(2,1)} %bitcast.54), custom_call_target="tpu_custom_call" | custom-call | flops 754974720 | bytes 7340032 | tf_op jit(solution)/shard_map/merge/pallas_call | solution.py:94
  91.9 2.6 %collective-permute-start.9 = (bf16[128,1280]{1,0:T(8,128)(2,1)}, bf16[128,1280]{1,0:T(8,128)(2,1)S(1)}, u32[]{:S(2)}, u32[]{:S(2)}) collective-permute-start(bf16[128,1280]{1,0:T(8,128)(2,1)} %merge.1.tile_ref), channel_id=1, source_target_pairs={{0,4},{4,8},{8,12},{12,16},{16,20},{20,24},{24,28},{28,0},{1,5},{5... | collective-permute-start | bytes 983048 | tf_op jit(solution)/shard_map/ppermute | solution.py:334
  94.4 3.9 %collective-permute-start.8 = (bf16[128,1280]{1,0:T(8,128)(2,1)}, bf16[128,1280]{1,0:T(8,128)(2,1)S(1)}, u32[]{:S(2)}, u32[]{:S(2)}) collective-permute-start(bf16[128,1280]{1,0:T(8,128)(2,1)} %merge.1.tile_ref), channel_id=1, source_target_pairs={{0,28},{4,0},{8,4},{12,8},{16,12},{20,16},{24,20},{28,24},{1,29},{... | collective-permute-start | bytes 983048 | tf_op jit(solution)/shard_map/ppermute | solution.py:334
  98.4 2.4 %collective-permute-start.7 = (bf16[128,1280]{1,0:T(8,128)(2,1)}, bf16[128,1280]{1,0:T(8,128)(2,1)S(1)}, u32[]{:S(2)}, u32[]{:S(2)}) collective-permute-start(bf16[128,1280]{1,0:T(8,128)(2,1)} %merge.1.tile_ref), channel_id=1, source_target_pairs={{0,8},{4,28},{8,16},{12,4},{16,24},{20,12},{24,0},{28,20},{1,9},{5... | collective-permute-start | bytes 983048 | tf_op jit(solution)/shard_map/ppermute | solution.py:334
  100.8 0.8 copy.43.table_ref
  101.6 2.2 pick_rows.4.refs_0_
  104.1 0.7 copy-done.5
  104.8 2.2 pick_rows.5.refs_0_
  107.0 0.7 copy-done.4
  107.7 2.2 pick_rows.6.refs_0_
  109.9 1.0 collective-permute-done.7.tile_ref
  110.9 0.7 copy-done.3
  111.6 2.2 pick_rows.7
  113.8 4.7 %all-to-all-start.1 = ((bf16[4,256,1280]{2,1,0:T(8,128)(2,1)}), bf16[4,256,1280]{2,1,0:T(8,128)(2,1)}, u32[]{:S(2)}, u32[]{:S(2)}) async-start(bf16[4,256,1280]{2,1,0:T(8,128)(2,1)} %bitcast.53), calls=%async_computation.1 | async-start | bytes 5242880 | tf_op jit(solution)/shard_map/all_to_all | solution.py:339
  119.1 26.3 %all-to-all-done.1 = bf16[4,256,1280]{2,1,0:T(8,128)(2,1)} async-done(((bf16[4,256,1280]{2,1,0:T(8,128)(2,1)}), bf16[4,256,1280]{2,1,0:T(8,128)(2,1)}, u32[]{:S(2)}, u32[]{:S(2)}) %all-to-all-start.1) | async-done | bytes 2621472 | tf_op jit(solution)/shard_map/all_to_all | solution.py:339
  145.4 13.5 %all-gather.5.cloned.1.call-done.weight_any = bf16[1280,4352]{1,0:T(8,128)(2,1)} async-done(((bf16[80,4352]{1,0:T(8,128)(2,1)}), bf16[1280,4352]{1,0:T(8,128)(2,1)}) %all-gather.5.cloned.1.call-update) | async-done | bytes 11141136 | tf_op jit(solution)/shard_map/all_gather | solution.py:329
  158.9 12.1 %expert_ffn.1 = bf16[4,2,128,1280]{3,2,1,0:T(8,128)(2,1)} custom-call(bf16[4,2,128,1280]{3,2,1,0:T(8,128)(2,1)} %bitcast.29.rows_any, f32[1,1280]{1,0:T(1,128)} %broadcast_in_dim.84.gain_ref, bf16[1280,4352]{1,0:T(8,128)(2,1)} %all-gather.5.cloned.1.call-done.weight_any), custom_call_target="tpu_custom_call" | custom-call | flops 5536481280 | bytes 16777216 | tf_op jit(solution)/shard_map/expert_ffn/pallas_call | solution.py:209
  171.0 35.5 %all_to_all.16 = bf16[4,256,1280]{2,1,0:T(8,128)(2,1)S(1)} all-to-all(bf16[4,256,1280]{2,1,0:T(8,128)(2,1)} %bitcast.55), channel_id=1, replica_groups=mesh['z'=8,'core'=2,'y'=8,'x'=4] {'x'}, dimensions={0} | all-to-all | bytes 5242880 | tf_op jit(solution)/shard_map/all_to_all | solution.py:343
  207.6 5.3 %collective-permute-start.12 = (bf16[128,1280]{1,0:T(8,128)(2,1)S(1)}, bf16[128,1280]{1,0:T(8,128)(2,1)S(1)}, u32[]{:S(2)}, u32[]{:S(2)}) collective-permute-start(bf16[128,1280]{1,0:T(8,128)(2,1)S(1)} %combine.7), channel_id=1, source_target_pairs={{8,0},{28,4},{16,8},{4,12},{24,16},{12,20},{0,24},{20,28},{9,1},{2... | collective-permute-start | bytes 983048 | tf_op jit(solution)/shard_map/ppermute | solution.py:346
  212.9 1.9 collective-permute-start.11
  214.8 4.6 %collective-permute-start.10 = (bf16[128,1280]{1,0:T(8,128)(2,1)S(1)}, bf16[128,1280]{1,0:T(8,128)(2,1)S(1)}, u32[]{:S(2)}, u32[]{:S(2)}) collective-permute-start(bf16[128,1280]{1,0:T(8,128)(2,1)S(1)} %combine.5), channel_id=1, source_target_pairs={{4,0},{8,4},{12,8},{16,12},{20,16},{24,20},{28,24},{0,28},{5,1},{9... | collective-permute-start | bytes 983048 | tf_op jit(solution)/shard_map/ppermute | solution.py:346
  219.8 7.5 %collective-permute-done.11 = bf16[128,1280]{1,0:T(8,128)(2,1)S(1)} collective-permute-done((bf16[128,1280]{1,0:T(8,128)(2,1)S(1)}, bf16[128,1280]{1,0:T(8,128)(2,1)S(1)}, u32[]{:S(2)}, u32[]{:S(2)}) %collective-permute-start.11) | collective-permute-done | bytes 327712 | tf_op jit(solution)/shard_map/ppermute | solution.py:346
  227.2 0.9 fusion.15
  (62 shorter events, 5.9 us)
Async XLA Ops:
  6.5 49.1 %copy-start = (bf16[576,576]{1,0:T(8,128)(2,1)S(1)}, bf16[576,576]{1,0:T(8,128)(2,1)}, u32[]{:S(2)}) copy-start(bf16[576,576]{1,0:T(8,128)(2,1)} %param.17) | copy-start | bytes 1990660
  6.5 79.0 %all-gather.3.cloned.1.call-start = ((), (), s32[]{:S(2)}) async-start(), calls=%async_computation.3 | async-start | bytes 6266880 | tf_op jit(solution)/shard_map/all_gather | solution.py:291
  18.4 140.5 %all-gather.5.cloned.1.call-start = ((), (), s32[]{:S(2)}) async-start(), calls=%async_computation.4 | async-start | bytes 11837440 | tf_op jit(solution)/shard_map/all_gather | solution.py:329
  25.3 34.6 %collective-permute-start.6 = (f32[12,128]{1,0:T(8,128)S(1)}, f32[12,128]{1,0:T(8,128)S(1)}, u32[]{:S(2)}, u32[]{:S(2)}) collective-permute-start(f32[12,128]{1,0:T(8,128)S(1)} %get-tuple-element.38), channel_id=1, source_target_pairs={{0,8},{4,28},{8,16},{12,4},{16,24},{20,12},{24,0},{28,20},{1,9},{5... | collective-permute-start | bytes 18440 | tf_op jit(solution)/shard_map/ppermute | solution.py:316
  30.3 29.6 %collective-permute-start.5 = (f32[12,128]{1,0:T(8,128)S(1)}, f32[12,128]{1,0:T(8,128)S(1)}, u32[]{:S(2)}, u32[]{:S(2)}) collective-permute-start(f32[12,128]{1,0:T(8,128)S(1)} %get-tuple-element.38), channel_id=1, source_target_pairs={{0,28},{4,0},{8,4},{12,8},{16,12},{20,16},{24,20},{28,24},{1,29},{... | collective-permute-start | bytes 18440 | tf_op jit(solution)/shard_map/ppermute | solution.py:316
  35.0 24.9 %collective-permute-start.4 = (f32[12,128]{1,0:T(8,128)S(1)}, f32[12,128]{1,0:T(8,128)S(1)}, u32[]{:S(2)}, u32[]{:S(2)}) collective-permute-start(f32[12,128]{1,0:T(8,128)S(1)} %get-tuple-element.38), channel_id=1, source_target_pairs={{0,4},{4,8},{8,12},{12,16},{16,20},{20,24},{24,28},{28,0},{1,5},{5... | collective-permute-start | bytes 18440 | tf_op jit(solution)/shard_map/ppermute | solution.py:316
  36.9 14.5 %copy-start.7 = (bf16[484,576]{0,1:T(8,128)(2,1)S(1)}, bf16[484,576]{0,1:T(8,128)(2,1)}, u32[]{:S(2)}) copy-start(bf16[484,576]{0,1:T(8,128)(2,1)} %param.15) | copy-start | bytes 1672708
  38.1 22.9 %collective-permute-start.2 = (bf16[40,2176]{1,0:T(8,128)(2,1)S(1)}, bf16[40,2176]{1,0:T(8,128)(2,1)S(1)}, u32[]{:S(2)}, u32[]{:S(2)}) collective-permute-start(bf16[40,2176]{1,0:T(8,128)(2,1)S(1)} %get-tuple-element.34), channel_id=1, source_target_pairs={{0,24},{4,28},{8,0},{12,4},{16,8},{20,12},{24,16},{28,20},{1,25},{... | collective-permute-start | bytes 522248 | tf_op jit(solution)/shard_map/ppermute | solution.py:312
  41.1 24.2 %collective-permute-start = (bf16[40,2176]{1,0:T(8,128)(2,1)S(1)}, bf16[40,2176]{1,0:T(8,128)(2,1)S(1)}, u32[]{:S(2)}, u32[]{:S(2)}) collective-permute-start(bf16[40,2176]{1,0:T(8,128)(2,1)S(1)} %get-tuple-element.33), channel_id=1, source_target_pairs={{0,8},{4,12},{8,16},{12,20},{16,24},{20,28},{24,0},{28,4},{1,9},{5... | collective-permute-start | bytes 522248 | tf_op jit(solution)/shard_map/ppermute | solution.py:312
  51.4 4.2 %copy-start.8 = (bf16[484,576]{0,1:T(8,128)(2,1)S(1)}, bf16[484,576]{0,1:T(8,128)(2,1)}, u32[]{:S(2)}) copy-start(bf16[484,576]{0,1:T(8,128)(2,1)} %param.16) | copy-start | bytes 1672708
  56.6 23.4 %copy-start.2 = (bf16[1,704,80]{1,2,0:T(8,128)(2,1)S(1)}, bf16[1,704,80]{1,2,0:T(8,128)(2,1)}, u32[]{:S(2)}) copy-start(bf16[1,704,80]{1,2,0:T(8,128)(2,1)} %param.22) | copy-start | bytes 337924
  61.0 16.2 %collective-permute-start.3 = (bf16[40,2176]{1,0:T(8,128)(2,1)S(1)}, bf16[40,2176]{1,0:T(8,128)(2,1)S(1)}, u32[]{:S(2)}, u32[]{:S(2)}) collective-permute-start(bf16[40,2176]{1,0:T(8,128)(2,1)S(1)} %collective-permute-done.2), channel_id=1, source_target_pairs={{0,24},{4,28},{8,0},{12,4},{16,8},{20,12},{24,16},{28,20},{1,25},{... | collective-permute-start | bytes 522248 | tf_op jit(solution)/shard_map/ppermute | solution.py:312
  65.3 14.7 %collective-permute-start.1 = (bf16[40,2176]{1,0:T(8,128)(2,1)S(1)}, bf16[40,2176]{1,0:T(8,128)(2,1)S(1)}, u32[]{:S(2)}, u32[]{:S(2)}) collective-permute-start(bf16[40,2176]{1,0:T(8,128)(2,1)S(1)} %collective-permute-done), channel_id=1, source_target_pairs={{0,8},{4,12},{8,16},{12,20},{16,24},{20,28},{24,0},{28,4},{1,9},{5... | collective-permute-start | bytes 522248 | tf_op jit(solution)/shard_map/ppermute | solution.py:312
  91.9 12.2 %collective-permute-start.9 = (bf16[128,1280]{1,0:T(8,128)(2,1)}, bf16[128,1280]{1,0:T(8,128)(2,1)S(1)}, u32[]{:S(2)}, u32[]{:S(2)}) collective-permute-start(bf16[128,1280]{1,0:T(8,128)(2,1)} %merge.1.tile_ref), channel_id=1, source_target_pairs={{0,4},{4,8},{8,12},{12,16},{16,20},{20,24},{24,28},{28,0},{1,5},{5... | collective-permute-start | bytes 983048 | tf_op jit(solution)/shard_map/ppermute | solution.py:334
  94.4 12.6 %collective-permute-start.8 = (bf16[128,1280]{1,0:T(8,128)(2,1)}, bf16[128,1280]{1,0:T(8,128)(2,1)S(1)}, u32[]{:S(2)}, u32[]{:S(2)}) collective-permute-start(bf16[128,1280]{1,0:T(8,128)(2,1)} %merge.1.tile_ref), channel_id=1, source_target_pairs={{0,28},{4,0},{8,4},{12,8},{16,12},{20,16},{24,20},{28,24},{1,29},{... | collective-permute-start | bytes 983048 | tf_op jit(solution)/shard_map/ppermute | solution.py:334
  98.4 12.5 %collective-permute-start.7 = (bf16[128,1280]{1,0:T(8,128)(2,1)}, bf16[128,1280]{1,0:T(8,128)(2,1)S(1)}, u32[]{:S(2)}, u32[]{:S(2)}) collective-permute-start(bf16[128,1280]{1,0:T(8,128)(2,1)} %merge.1.tile_ref), channel_id=1, source_target_pairs={{0,8},{4,28},{8,16},{12,4},{16,24},{20,12},{24,0},{28,20},{1,9},{5... | collective-permute-start | bytes 983048 | tf_op jit(solution)/shard_map/ppermute | solution.py:334
  104.1 0.7 copy-start.5
  107.0 0.7 copy-start.4
  109.9 8.6 %copy-start.6 = (f32[1280]{0:T(1024)S(1)}, f32[1280]{0:T(1024)}, u32[]{:S(2)}) copy-start(f32[1280]{0:T(1024)} %param.19) | copy-start | bytes 15364
  110.9 0.7 copy-start.3
  113.8 31.6 %all-to-all-start.1 = ((bf16[4,256,1280]{2,1,0:T(8,128)(2,1)}), bf16[4,256,1280]{2,1,0:T(8,128)(2,1)}, u32[]{:S(2)}, u32[]{:S(2)}) async-start(bf16[4,256,1280]{2,1,0:T(8,128)(2,1)} %bitcast.53), calls=%async_computation.1 | async-start | bytes 5242880 | tf_op jit(solution)/shard_map/all_to_all | solution.py:339
  206.9 20.4 %copy-start.1 = (bf16[128,1280]{1,0:T(8,128)(2,1)S(1)}, bf16[128,1280]{1,0:T(8,128)(2,1)}, u32[]{:S(2)}) copy-start(bf16[128,1280]{1,0:T(8,128)(2,1)} %merge.1.tile_ref) | copy-start | bytes 983044
  207.6 12.2 %collective-permute-start.12 = (bf16[128,1280]{1,0:T(8,128)(2,1)S(1)}, bf16[128,1280]{1,0:T(8,128)(2,1)S(1)}, u32[]{:S(2)}, u32[]{:S(2)}) collective-permute-start(bf16[128,1280]{1,0:T(8,128)(2,1)S(1)} %combine.7), channel_id=1, source_target_pairs={{8,0},{28,4},{16,8},{4,12},{24,16},{12,20},{0,24},{20,28},{9,1},{2... | collective-permute-start | bytes 983048 | tf_op jit(solution)/shard_map/ppermute | solution.py:346
  212.9 14.3 %collective-permute-start.11 = (bf16[128,1280]{1,0:T(8,128)(2,1)S(1)}, bf16[128,1280]{1,0:T(8,128)(2,1)S(1)}, u32[]{:S(2)}, u32[]{:S(2)}) collective-permute-start(bf16[128,1280]{1,0:T(8,128)(2,1)S(1)} %combine.6), channel_id=1, source_target_pairs={{28,0},{0,4},{4,8},{8,12},{12,16},{16,20},{20,24},{24,28},{29,1},{... | collective-permute-start | bytes 983048 | tf_op jit(solution)/shard_map/ppermute | solution.py:346
  214.8 12.4 %collective-permute-start.10 = (bf16[128,1280]{1,0:T(8,128)(2,1)S(1)}, bf16[128,1280]{1,0:T(8,128)(2,1)S(1)}, u32[]{:S(2)}, u32[]{:S(2)}) collective-permute-start(bf16[128,1280]{1,0:T(8,128)(2,1)S(1)} %combine.5), channel_id=1, source_target_pairs={{4,0},{8,4},{12,8},{16,12},{20,16},{24,20},{28,24},{0,28},{5,1},{9... | collective-permute-start | bytes 983048 | tf_op jit(solution)/shard_map/ppermute | solution.py:346
Sparse Core Ops, SparseCore 0:
  18.5 66.9 all-gather.2
  87.7 71.1 all-gather.4

commit v5 on v4

--- a/solution.py
+++ b/solution.py
@@ -110,27 +110,34 @@
     )(merged, weight)
 
 
-def pick_body(table_ref, tile_ref, *refs):
-    send_ref = refs[-1]
-    rows = jnp.dot(table_ref[0], tile_ref[...], preferred_element_type=jnp.float32)
-    send_ref[...] = rows.astype(jnp.bfloat16).reshape(send_ref.shape)
+def pick_body(index, table_ref, tile_ref, *refs):
+    send, rows, sem = refs[-3:]
+    picked = jnp.dot(table_ref[0], tile_ref[...], preferred_element_type=jnp.float32)
+    rows[...] = picked.astype(jnp.bfloat16).reshape(rows.shape)
+    copy = pltpu.make_async_copy(rows, send.at[:, :, index], sem)
+    copy.start()
+    copy.wait()
 
 
 def pick_rows(table, index, tile, shape, send=None):
     cols, hosted, _, slot, width = shape
     given = [] if send is None else [send]
     return pl.pallas_call(
-        pick_body,
+        functools.partial(pick_body, index),
         grid=(1,),
         in_specs=[
             pl.BlockSpec((1,) + table.shape[1:], lambda i: (index, 0, 0)),
             pl.BlockSpec(tile.shape, lambda i: (0, 0)),
         ]
-        + [pl.BlockSpec(memory_space=pl.ANY)] * len(given),
-        out_specs=pl.BlockSpec((cols, hosted, 1, slot, width), lambda i: (0, 0, index, 0, 0)),
+        + [pl.BlockSpec(memory_space=pltpu.HBM)] * len(given),
+        out_specs=pl.BlockSpec(memory_space=pltpu.HBM),
         out_shape=jax.ShapeDtypeStruct(shape, jnp.bfloat16),
+        scratch_shapes=[
+            pltpu.VMEM((cols, hosted, slot, width), jnp.bfloat16),
+            pltpu.SemaphoreType.DMA,
+        ],
         input_output_aliases={2: 0} if given else {},
-        compiler_params=pltpu.CompilerParams(vmem_limit_bytes=60 << 20),
+        compiler_params=pltpu.CompilerParams(vmem_limit_bytes=24 << 20),
         cost_estimate=pl.CostEstimate(
             flops=2 * TPAD * width * table.shape[1],
             bytes_accessed=1 << 20,
@@ -140,51 +147,45 @@
     )(table, tile, *given)
 
 
-def expert_body(hidden, main, rows_any, gain_ref, weight_any, out_any, rows, weight, out, sems):
-    cols, hosted, count, width = rows_any.shape
-    span = weight_any.shape[1] // hosted
+def expert_body(hidden, rows_hbm, gain_ref, weight_hbm, out_hbm, rows, weight, out, sems):
+    cols, hosted, count, width = rows_hbm.shape
+    span = weight_hbm.shape[1] // hosted
     first = 2 * hidden
-    copies = []
-    for j in range(hosted):
-        copies.append(
-            [
-                pltpu.make_async_copy(rows_any.at[:, j], rows.at[j], sems.at[j, 0]),
-                pltpu.make_async_copy(
-                    weight_any.at[:, pl.ds(j * span, first)],
-                    weight.at[j, :, pl.ds(0, first)],
-                    sems.at[j, 1],
-                ),
-                pltpu.make_async_copy(
-                    weight_any.at[:, pl.ds(j * span + first, span - first)],
-                    weight.at[j, :, pl.ds(first, span - first)],
-                    sems.at[j, 2],
-                ),
-            ]
-        )
-    for group in copies:
-        for copy in group:
+
+    def load(j):
+        copies = [
+            pltpu.make_async_copy(rows_hbm.at[:, j], rows.at[j], sems.at[j, 0]),
+            pltpu.make_async_copy(
+                weight_hbm.at[:, pl.ds(j * span, first)],
+                weight.at[j, :, pl.ds(0, first)],
+                sems.at[j, 1],
+            ),
+            pltpu.make_async_copy(
+                weight_hbm.at[:, pl.ds(j * span + first, span - first)],
+                weight.at[j, :, pl.ds(first, span - first)],
+                sems.at[j, 2],
+            ),
+        ]
+        for copy in copies:
             copy.start()
-
-    def gated(gate, up):
-        return (gate / (1.0 + jnp.exp(-gate)) * up).astype(jnp.bfloat16)
-
-    rest = hidden - main
+        return copies
+
+    pending = load(0)
     results = []
     for j in range(hosted):
-        copies[j][0].wait()
+        current = pending
+        current[0].wait()
         wide = rows[j].reshape(-1, width).astype(jnp.float32)
         scale = lax.rsqrt(jnp.mean(wide * wide, axis=-1, keepdims=True) + 1e-06)
         normed = (wide * scale * gain_ref[...]).astype(jnp.bfloat16)
-        copies[j][1].wait()
+        current[1].wait()
+        if j + 1 < hosted:
+            pending = load(j + 1)
         both = jnp.dot(normed, weight[j, :, :first], preferred_element_type=jnp.float32)
-        act = jnp.concatenate(
-            [
-                gated(both[:, :main], both[:, main : 2 * main]),
-                gated(both[:, 2 * main : 2 * main + rest], both[:, 2 * main + rest :]),
-            ],
-            axis=1,
-        )
-        copies[j][2].wait()
+        gate = both[:, :hidden]
+        up = both[:, hidden:]
+        act = (gate / (1.0 + jnp.exp(-gate)) * up).astype(jnp.bfloat16)
+        current[2].wait()
         out[j] = (
             lax.dot_general(
                 act,
@@ -195,21 +196,21 @@
             .astype(jnp.bfloat16)
             .reshape(cols, count, width)
         )
-        result = pltpu.make_async_copy(out.at[j], out_any.at[:, j], sems.at[j, 3])
+        result = pltpu.make_async_copy(out.at[j], out_hbm.at[:, j], sems.at[j, 3])
         result.start()
         results.append(result)
     for result in results:
         result.wait()
 
 
-def expert_ffn(rows, gain, weight, hidden, main):
+def expert_ffn(rows, gain, weight, hidden):
     cols, hosted, count, width = rows.shape
     held = (hosted, cols, count, width)
-    anywhere = pl.BlockSpec(memory_space=pl.ANY)
+    hbm = pl.BlockSpec(memory_space=pltpu.HBM)
     return pl.pallas_call(
-        functools.partial(expert_body, hidden, main),
-        in_specs=[anywhere, pl.BlockSpec(memory_space=pltpu.VMEM), anywhere],
-        out_specs=anywhere,
+        functools.partial(expert_body, hidden),
+        in_specs=[hbm, pl.BlockSpec(memory_space=pltpu.VMEM), hbm],
+        out_specs=hbm,
         out_shape=jax.ShapeDtypeStruct(rows.shape, jnp.bfloat16),
         scratch_shapes=[
             pltpu.VMEM(held, jnp.bfloat16),
@@ -281,23 +282,21 @@
 
     half = w_merge.shape[0] // 2
     piece = lax.dynamic_slice_in_dim(w_merge.T, lax.axis_index("core") * half, half, 1)
+    down = w_down[0].T
+    blank = jnp.zeros((down.shape[0], -(-3 * hidden // 128) * 128 - 3 * hidden), down.dtype)
+    own = jnp.concatenate([w_gate[0], w_up[0], down, blank], axis=1)
+    own, piece = lax.optimization_barrier((own, piece))
+    other = lax.ppermute(own, "y", shift(rows, rows // 2))
     piece = lax.all_to_all(
         jnp.broadcast_to(piece[None], (cols,) + piece.shape), "x", split_axis=0, concat_axis=0
     )
     piece = piece.reshape(-1, half)
-    queries, w_gate, w_up, w_down, routes, route_weight, piece = lax.optimization_barrier(
-        (queries, w_gate, w_up, w_down, routes, route_weight, piece)
+    queries, routes, route_weight, piece, own, other = lax.optimization_barrier(
+        (queries, routes, route_weight, piece, own, other)
     )
     merger = lax.all_gather(piece, ("core", "y"), axis=0, tiled=True)
     merger = merger.reshape(2, -1, half)
 
-    edge = -(-3 * hidden // 128) * 128 - 3 * hidden
-    main = hidden // 128 * 128
-    gate, up, down = w_gate[0], w_up[0], w_down[0].T
-    blank = jnp.zeros((down.shape[0], edge), down.dtype)
-    own = jnp.concatenate(
-        [gate[:, :main], up[:, :main], gate[:, main:], up[:, main:], down, blank], axis=1
-    )
     routing = jnp.concatenate(
         [
             jnp.pad(routes, ((0, TPAD - tokens), (0, 0)), constant_values=-1).astype(jnp.float32),
@@ -305,13 +304,6 @@
         ],
         axis=1,
     ).T
-    middle = own.shape[0] // 2
-    ways = []
-    for part, step in ((own[:middle], rows // 4), (own[middle:], -(rows // 4))):
-        for _ in range(2):
-            part = lax.ppermute(part, "y", shift(rows, step))
-        ways.append(part)
-    other = jnp.concatenate(ways, axis=0)
     steps = (shift(rows, 1), shift(rows, -1), far_shift(rows))
     info = jnp.stack([routing] + [lax.ppermute(routing, "y", step) for step in steps])
     hosted = jnp.stack([row, (row + rows // 2) % rows])
@@ -338,7 +330,10 @@
     flat = (cols, send.size // cols // width, width)
     received = lax.all_to_all(send.reshape(flat), "x", split_axis=0, concat_axis=0)
     outcome = expert_ffn(
-        received.reshape(cols, 2, -1, width), rms_gain[None, :], experts, hidden, main
+        received.reshape(cols, 2, -1, width),
+        rms_gain[None, :],
+        experts,
+        hidden,
     )
     back = lax.all_to_all(outcome.reshape(flat), "x", split_axis=0, concat_axis=0)
     back = back.reshape(shape)

time: 236 us -> 236 us (level)
  waiting for transfers between devices: 64.5 us -> 77.8 us
  local copies, waits for them, and re-layouts: 15.6 us -> 9.53 us
  starting transfers between devices: 50.5 us -> 46.8 us
  Pallas kernels: 28.5 us -> 24.8 us
    all_gather x1, waiting for transfers between devices: 4.44 us -> 21.6 us  [local(): merger = lax.all_gather(piece, ('core', 'y'), axis=0, tiled=True)]
    ppermute x4 -> x1, waiting for transfers between devices: 11.6 us -> 1.56 us  [local(): other = lax.ppermute(own, 'y', shift(rows, rows // 2))]
    ppermute x4 -> x1, starting transfers between devices: 13.5 us -> 8.28 us  [local(): other = lax.ppermute(own, 'y', shift(rows, rows // 2))]
    ppermute x3, waiting for transfers between devices: 1.24 us -> 5.73 us  [local(): arrived = [lax.ppermute(stream, 'y', step) for step in steps]]
    pallas_call x5, Pallas kernels: 20.9 us -> 17.1 us  [the longest x1 12.4 us: expert_ffn(): pl.pallas_call(functools.partial(expert_body, hidden), in_specs=[hbm, pl....]
    slice x5 -> x0, local copies, waits for them, and re-layouts: 3.3 us -> none  [the longest x1 0.91 us: local(): gate[:, :main]]
  transfers between devices with their start and end apart: 16 -> 13, of which waited for: 8 -> 8; matrix products, arithmetic and copies ran while one was open for 11% -> 9% of each run, Pallas kernels for 7% -> 5%
where the time goes in v5:
time: 236 us; the launch traced here: 235 us
  waiting for transfers between devices  77.8 us (33%)
  starting transfers between devices  46.8 us (20%)
  blocking collectives  45.9 us (19%)
  Pallas kernels  24.8 us (11%)
  between operations  14.5 us (6%)
  matrix products  12.2 us (5%)
  local copies, waits for them, and re-layouts  9.53 us (4%)
  other arithmetic  3.7 us (2%)
    all_to_all x1, blocking collectives, local(): lax.all_to_all(outcome.reshape(flat), 'x', split_axis=0, concat_axis=0)  35.5 us
    all_to_all x1, waiting for transfers between devices, local(): lax.all_to_all(send.reshape(flat), 'x', split_axis=0, concat_axis=0)  27.4 us
    all_gather x1, waiting for transfers between devices, local(): merger = lax.all_gather(piece, ('core', 'y'), axis=0, tiled=True)  21.6 us
    all_gather x1, waiting for transfers between devices, local(): experts = lax.all_gather(mine, ('z', 'core'), axis=0, tiled=True)  14.1 us
    ppermute x3, starting transfers between devices, local(): lax.ppermute(routing, 'y', step)  13.3 us
    pallas_call x1, Pallas kernels, expert_ffn(): pl.pallas_call(functools.partial(expert_body, hidden), in_specs=[hbm, pl....  12.4 us
    ppermute x3, starting transfers between devices, local(): lax.ppermute(combine(mix, back, i + 1, jnp.bfloat16), 'y', back_again(step))  11.8 us
    all_to_all x1, blocking collectives, local(): lax.all_to_all(jnp.broadcast_to(piece[None], (cols,) + piece.shape), 'x',...  10.4 us
  transfers between devices with their start and end apart: 13, of which 8 were waited for; matrix products, arithmetic and copies ran while one was open for 9% of the time, Pallas kernels for 5%

profile of v5, /device:TPU:1, one launch (start us, length us, event | category | flops | bytes accessed | tf_op | source)
XLA Modules:
  0.0 235.2 jit_solution(2006729960441759893)
XLA Ops:
  6.5 1.0 dynamic-slice_bitcast_fusion
  7.5 1.2 concatenate.16
  8.7 8.3 %collective-permute-start = (bf16[80,2176]{1,0:T(8,128)(2,1)S(1)}, bf16[80,2176]{1,0:T(8,128)(2,1)S(1)}, u32[]{:S(2)}, u32[]{:S(2)}) collective-permute-start(bf16[80,2176]{1,0:T(8,128)(2,1)S(1)} %concatenate.16), channel_id=1, source_target_pairs={{0,16},{4,20},{8,24},{12,28},{16,0},{20,4},{24,8},{28,12},{1,17},{... | collective-permute-start | bytes 1044488 | tf_op jit(solution)/shard_map/ppermute | solution.py:289
  17.0 10.4 %all_to_all.15 = bf16[4,40,1152]{2,1,0:T(8,128)(2,1)} all-to-all(bf16[4,40,1152]{2,1,0:T(8,128)(2,1)S(1)} %broadcast_in_dim.72), channel_id=1, replica_groups=mesh['z'=8,'core'=2,'y'=8,'x'=4] {'x'}, dimensions={0} | all-to-all | bytes 737280 | tf_op jit(solution)/shard_map/all_to_all | solution.py:290
  27.5 1.6 collective-permute-done
  29.4 1.2 constant_dynamic-slice_fusion
  31.3 0.7 pad_convert_fusion
  32.0 0.7 fusion.22
  32.7 8.0 %collective-permute-start.3 = (f32[12,128]{1,0:T(8,128)S(1)}, f32[12,128]{1,0:T(8,128)S(1)}, u32[]{:S(2)}, u32[]{:S(2)}) collective-permute-start(f32[12,128]{1,0:T(8,128)S(1)} %get-tuple-element.38), channel_id=1, source_target_pairs={{0,8},{4,28},{8,16},{12,4},{16,24},{20,12},{24,0},{28,20},{1,9},{5... | collective-permute-start | bytes 18440 | tf_op jit(solution)/shard_map/ppermute | solution.py:308
  40.7 2.0 collective-permute-start.2
  42.7 3.2 %collective-permute-start.1 = (f32[12,128]{1,0:T(8,128)S(1)}, f32[12,128]{1,0:T(8,128)S(1)}, u32[]{:S(2)}, u32[]{:S(2)}) collective-permute-start(f32[12,128]{1,0:T(8,128)S(1)} %get-tuple-element.38), channel_id=1, source_target_pairs={{0,4},{4,8},{8,12},{12,16},{16,20},{20,24},{24,28},{28,0},{1,5},{5... | collective-permute-start | bytes 18440 | tf_op jit(solution)/shard_map/ppermute | solution.py:308
  46.0 7.1 %fusion.27 = (f32[8,484]{1,0:T(8,128)S(1)}, f32[8,484,484]{1,2,0:T(8,128)}) fusion(bf16[484,8,72]{0,2,1:T(8,128)(2,1)} %bitcast.66, bf16[484,8,72]{0,2,1:T(8,128)(2,1)} %bitcast.67), kind=kOutput, calls=%fused_computation.47 | convolution fusion | flops 275485536 | bytes 8626816 | tf_op jit(solution)/shard_map/sub | solution.py:29
  53.1 0.9 pad_maximum_fusion
  54.0 4.2 %fusion.7 = bf16[8,484,72]{1,2,0:T(8,128)(2,1)S(1)} fusion(bf16[484,8,72]{0,2,1:T(8,128)(2,1)S(1)} %bitcast.68, f32[8,484,484]{1,2,0:T(8,128)} %get-tuple-element.40, f32[8,484]{1,0:T(8,128)S(1)} %get-tuple-element.39), kind=kOutput, calls=%fused_computation.9 | convolution fusion | flops 273889792 | bytes 8626816 | tf_op jit(solution)/shard_map/hqk,khd->qhd/dot_general | solution.py:31
  58.3 0.7 fusion.8
  59.0 0.3 copy.35
  59.3 0.8 select_n.66
  60.1 0.4 copy.36
  60.6 1.1 select_n.68
  61.7 0.9 pad.12.merged_ref
  63.2 0.2 copy.37
  63.8 21.6 %all-gather.3.cloned.1.call-done = bf16[2560,1152]{1,0:T(8,128)(2,1)} async-done(((bf16[160,1152]{1,0:T(8,128)(2,1)}), bf16[2560,1152]{1,0:T(8,128)(2,1)}) %all-gather.3.cloned.1.call-update) | async-done | bytes 5898256 | tf_op jit(solution)/shard_map/all_gather | solution.py:297
  85.4 6.3 %merge.1.tile_ref = bf16[128,1280]{1,0:T(8,128)(2,1)} custom-call(bf16[128,2304]{1,0:T(8,128)(2,1)} %pad.12.merged_ref, bf16[2,1280,1152]{2,1,0:T(8,128)(2,1)} %bitcast.53), custom_call_target="tpu_custom_call" | custom-call | flops 754974720 | bytes 7340032 | tf_op jit(solution)/shard_map/merge/pallas_call | solution.py:94
  91.7 2.8 %collective-permute-start.6 = (bf16[128,1280]{1,0:T(8,128)(2,1)}, bf16[128,1280]{1,0:T(8,128)(2,1)S(1)}, u32[]{:S(2)}, u32[]{:S(2)}) collective-permute-start(bf16[128,1280]{1,0:T(8,128)(2,1)} %merge.1.tile_ref), channel_id=1, source_target_pairs={{0,4},{4,8},{8,12},{12,16},{16,20},{20,24},{24,28},{28,0},{1,5},{5... | collective-permute-start | bytes 983048 | tf_op jit(solution)/shard_map/ppermute | solution.py:326
  94.5 3.7 %collective-permute-start.5 = (bf16[128,1280]{1,0:T(8,128)(2,1)}, bf16[128,1280]{1,0:T(8,128)(2,1)S(1)}, u32[]{:S(2)}, u32[]{:S(2)}) collective-permute-start(bf16[128,1280]{1,0:T(8,128)(2,1)} %merge.1.tile_ref), channel_id=1, source_target_pairs={{0,28},{4,0},{8,4},{12,8},{16,12},{20,16},{24,20},{28,24},{1,29},{... | collective-permute-start | bytes 983048 | tf_op jit(solution)/shard_map/ppermute | solution.py:326
  98.2 2.1 collective-permute-start.4
  100.6 1.0 copy-done.1
  101.5 1.2 pick_rows.4.refs_0_
  102.7 1.3 collective-permute-done.6.tile_ref
  104.1 1.2 pick_rows.5.refs_0_
  105.4 1.2 pick_rows.6.refs_0_
  106.7 4.2 %collective-permute-done.4.tile_ref = bf16[128,1280]{1,0:T(8,128)(2,1)S(1)} collective-permute-done((bf16[128,1280]{1,0:T(8,128)(2,1)}, bf16[128,1280]{1,0:T(8,128)(2,1)S(1)}, u32[]{:S(2)}, u32[]{:S(2)}) %collective-permute-start.4) | collective-permute-done | bytes 327712 | tf_op jit(solution)/shard_map/ppermute | solution.py:326
  110.8 1.2 pick_rows.7
  112.0 4.7 %all-to-all-start.1 = ((bf16[4,256,1280]{2,1,0:T(8,128)(2,1)}), bf16[4,256,1280]{2,1,0:T(8,128)(2,1)}, u32[]{:S(2)}, u32[]{:S(2)}) async-start(bf16[4,256,1280]{2,1,0:T(8,128)(2,1)} %bitcast.27), calls=%async_computation.1 | async-start | bytes 5242880 | tf_op jit(solution)/shard_map/all_to_all | solution.py:331
  116.8 0.6 broadcast_in_dim.84.gain_ref
  117.4 27.4 %all-to-all-done.1 = bf16[4,256,1280]{2,1,0:T(8,128)(2,1)} async-done(((bf16[4,256,1280]{2,1,0:T(8,128)(2,1)}), bf16[4,256,1280]{2,1,0:T(8,128)(2,1)}, u32[]{:S(2)}, u32[]{:S(2)}) %all-to-all-start.1) | async-done | bytes 2621472 | tf_op jit(solution)/shard_map/all_to_all | solution.py:331
  144.7 14.1 %all-gather.5.cloned.1.call-done.weight_hbm = bf16[1280,4352]{1,0:T(8,128)(2,1)} async-done(((bf16[80,4352]{1,0:T(8,128)(2,1)}), bf16[1280,4352]{1,0:T(8,128)(2,1)}) %all-gather.5.cloned.1.call-update) | async-done | bytes 11141136 | tf_op jit(solution)/shard_map/all_gather | solution.py:321
  158.8 12.4 %expert_ffn.1 = bf16[4,2,128,1280]{3,2,1,0:T(8,128)(2,1)} custom-call(bf16[4,2,128,1280]{3,2,1,0:T(8,128)(2,1)} %bitcast.28.rows_hbm, f32[1,1280]{1,0:T(1,128)} %broadcast_in_dim.84.gain_ref, bf16[1280,4352]{1,0:T(8,128)(2,1)} %all-gather.5.cloned.1.call-done.weight_hbm), custom_call_target="tpu_custom_call" | custom-call | flops 5536481280 | bytes 16777216 | tf_op jit(solution)/shard_map/expert_ffn/pallas_call | solution.py:210
  171.2 35.5 %all_to_all.16 = bf16[4,256,1280]{2,1,0:T(8,128)(2,1)S(1)} all-to-all(bf16[4,256,1280]{2,1,0:T(8,128)(2,1)} %bitcast.54), channel_id=1, replica_groups=mesh['z'=8,'core'=2,'y'=8,'x'=4] {'x'}, dimensions={0} | all-to-all | bytes 5242880 | tf_op jit(solution)/shard_map/all_to_all | solution.py:338
  206.7 0.3 combine.7
  207.0 0.3 combine.6
  207.4 0.3 combine.5
  207.8 5.3 %collective-permute-start.9 = (bf16[128,1280]{1,0:T(8,128)(2,1)S(1)}, bf16[128,1280]{1,0:T(8,128)(2,1)S(1)}, u32[]{:S(2)}, u32[]{:S(2)}) collective-permute-start(bf16[128,1280]{1,0:T(8,128)(2,1)S(1)} %combine.7), channel_id=1, source_target_pairs={{8,0},{28,4},{16,8},{4,12},{24,16},{12,20},{0,24},{20,28},{9,1},{2... | collective-permute-start | bytes 983048 | tf_op jit(solution)/shard_map/ppermute | solution.py:341
  213.1 1.9 collective-permute-start.8
  215.0 4.6 %collective-permute-start.7 = (bf16[128,1280]{1,0:T(8,128)(2,1)S(1)}, bf16[128,1280]{1,0:T(8,128)(2,1)S(1)}, u32[]{:S(2)}, u32[]{:S(2)}) collective-permute-start(bf16[128,1280]{1,0:T(8,128)(2,1)S(1)} %combine.5), channel_id=1, source_target_pairs={{4,0},{8,4},{12,8},{16,12},{20,16},{24,20},{28,24},{0,28},{5,1},{9... | collective-permute-start | bytes 983048 | tf_op jit(solution)/shard_map/ppermute | solution.py:341
  219.6 0.3 combine.4
  220.0 7.5 %collective-permute-done.8 = bf16[128,1280]{1,0:T(8,128)(2,1)S(1)} collective-permute-done((bf16[128,1280]{1,0:T(8,128)(2,1)S(1)}, bf16[128,1280]{1,0:T(8,128)(2,1)S(1)}, u32[]{:S(2)}, u32[]{:S(2)}) %collective-permute-start.8) | collective-permute-done | bytes 327712 | tf_op jit(solution)/shard_map/ppermute | solution.py:341
  227.4 0.9 fusion.15
  (44 shorter events, 1.7 us)
Async XLA Ops:
  6.5 51.7 %copy-start = (bf16[576,576]{1,0:T(8,128)(2,1)S(1)}, bf16[576,576]{1,0:T(8,128)(2,1)}, u32[]{:S(2)}) copy-start(bf16[576,576]{1,0:T(8,128)(2,1)} %param.17) | copy-start | bytes 1990660
  6.5 78.9 %all-gather.3.cloned.1.call-start = ((), (), s32[]{:S(2)}) async-start(), calls=%async_computation.3 | async-start | bytes 6266880 | tf_op jit(solution)/shard_map/all_gather | solution.py:297
  8.7 20.3 %collective-permute-start = (bf16[80,2176]{1,0:T(8,128)(2,1)S(1)}, bf16[80,2176]{1,0:T(8,128)(2,1)S(1)}, u32[]{:S(2)}, u32[]{:S(2)}) collective-permute-start(bf16[80,2176]{1,0:T(8,128)(2,1)S(1)} %concatenate.16), channel_id=1, source_target_pairs={{0,16},{4,20},{8,24},{12,28},{16,0},{20,4},{24,8},{28,12},{1,17},{... | collective-permute-start | bytes 1044488 | tf_op jit(solution)/shard_map/ppermute | solution.py:289
  29.0 129.8 %all-gather.5.cloned.1.call-start = ((), (), s32[]{:S(2)}) async-start(), calls=%async_computation.4 | async-start | bytes 11837440 | tf_op jit(solution)/shard_map/all_gather | solution.py:321
  32.7 29.9 %collective-permute-start.3 = (f32[12,128]{1,0:T(8,128)S(1)}, f32[12,128]{1,0:T(8,128)S(1)}, u32[]{:S(2)}, u32[]{:S(2)}) collective-permute-start(f32[12,128]{1,0:T(8,128)S(1)} %get-tuple-element.38), channel_id=1, source_target_pairs={{0,8},{4,28},{8,16},{12,4},{16,24},{20,12},{24,0},{28,20},{1,9},{5... | collective-permute-start | bytes 18440 | tf_op jit(solution)/shard_map/ppermute | solution.py:308
  40.7 21.9 %collective-permute-start.2 = (f32[12,128]{1,0:T(8,128)S(1)}, f32[12,128]{1,0:T(8,128)S(1)}, u32[]{:S(2)}, u32[]{:S(2)}) collective-permute-start(f32[12,128]{1,0:T(8,128)S(1)} %get-tuple-element.38), channel_id=1, source_target_pairs={{0,28},{4,0},{8,4},{12,8},{16,12},{20,16},{24,20},{28,24},{1,29},{... | collective-permute-start | bytes 18440 | tf_op jit(solution)/shard_map/ppermute | solution.py:308
  42.7 19.8 %collective-permute-start.1 = (f32[12,128]{1,0:T(8,128)S(1)}, f32[12,128]{1,0:T(8,128)S(1)}, u32[]{:S(2)}, u32[]{:S(2)}) collective-permute-start(f32[12,128]{1,0:T(8,128)S(1)} %get-tuple-element.38), channel_id=1, source_target_pairs={{0,4},{4,8},{8,12},{12,16},{16,20},{20,24},{24,28},{28,0},{1,5},{5... | collective-permute-start | bytes 18440 | tf_op jit(solution)/shard_map/ppermute | solution.py:308
  46.0 8.1 %copy-start.4 = (bf16[484,576]{0,1:T(8,128)(2,1)S(1)}, bf16[484,576]{0,1:T(8,128)(2,1)}, u32[]{:S(2)}) copy-start(bf16[484,576]{0,1:T(8,128)(2,1)} %param.15) | copy-start | bytes 1672708
  54.0 4.2 %copy-start.5 = (bf16[484,576]{0,1:T(8,128)(2,1)S(1)}, bf16[484,576]{0,1:T(8,128)(2,1)}, u32[]{:S(2)}) copy-start(bf16[484,576]{0,1:T(8,128)(2,1)} %param.16) | copy-start | bytes 1672708
  91.7 12.4 %collective-permute-start.6 = (bf16[128,1280]{1,0:T(8,128)(2,1)}, bf16[128,1280]{1,0:T(8,128)(2,1)S(1)}, u32[]{:S(2)}, u32[]{:S(2)}) collective-permute-start(bf16[128,1280]{1,0:T(8,128)(2,1)} %merge.1.tile_ref), channel_id=1, source_target_pairs={{0,4},{4,8},{8,12},{12,16},{16,20},{20,24},{24,28},{28,0},{1,5},{5... | collective-permute-start | bytes 983048 | tf_op jit(solution)/shard_map/ppermute | solution.py:326
  94.5 10.9 %collective-permute-start.5 = (bf16[128,1280]{1,0:T(8,128)(2,1)}, bf16[128,1280]{1,0:T(8,128)(2,1)S(1)}, u32[]{:S(2)}, u32[]{:S(2)}) collective-permute-start(bf16[128,1280]{1,0:T(8,128)(2,1)} %merge.1.tile_ref), channel_id=1, source_target_pairs={{0,28},{4,0},{8,4},{12,8},{16,12},{20,16},{24,20},{28,24},{1,29},{... | collective-permute-start | bytes 983048 | tf_op jit(solution)/shard_map/ppermute | solution.py:326
  98.2 12.6 %collective-permute-start.4 = (bf16[128,1280]{1,0:T(8,128)(2,1)}, bf16[128,1280]{1,0:T(8,128)(2,1)S(1)}, u32[]{:S(2)}, u32[]{:S(2)}) collective-permute-start(bf16[128,1280]{1,0:T(8,128)(2,1)} %merge.1.tile_ref), channel_id=1, source_target_pairs={{0,8},{4,28},{8,16},{12,4},{16,24},{20,12},{24,0},{28,20},{1,9},{5... | collective-permute-start | bytes 983048 | tf_op jit(solution)/shard_map/ppermute | solution.py:326
  100.5 1.0 copy-start.1
  112.0 4.7 %copy-start.3 = (f32[1280]{0:T(1024)S(1)}, f32[1280]{0:T(1024)}, u32[]{:S(2)}) copy-start(f32[1280]{0:T(1024)} %param.19) | copy-start | bytes 15364
  112.0 32.7 %all-to-all-start.1 = ((bf16[4,256,1280]{2,1,0:T(8,128)(2,1)}), bf16[4,256,1280]{2,1,0:T(8,128)(2,1)}, u32[]{:S(2)}, u32[]{:S(2)}) async-start(bf16[4,256,1280]{2,1,0:T(8,128)(2,1)} %bitcast.27), calls=%async_computation.1 | async-start | bytes 5242880 | tf_op jit(solution)/shard_map/all_to_all | solution.py:331
  207.4 20.0 %copy-start.2 = (bf16[128,1280]{1,0:T(8,128)(2,1)S(1)}, bf16[128,1280]{1,0:T(8,128)(2,1)}, u32[]{:S(2)}) copy-start(bf16[128,1280]{1,0:T(8,128)(2,1)} %merge.1.tile_ref) | copy-start | bytes 983044
  207.8 12.2 %collective-permute-start.9 = (bf16[128,1280]{1,0:T(8,128)(2,1)S(1)}, bf16[128,1280]{1,0:T(8,128)(2,1)S(1)}, u32[]{:S(2)}, u32[]{:S(2)}) collective-permute-start(bf16[128,1280]{1,0:T(8,128)(2,1)S(1)} %combine.7), channel_id=1, source_target_pairs={{8,0},{28,4},{16,8},{4,12},{24,16},{12,20},{0,24},{20,28},{9,1},{2... | collective-permute-start | bytes 983048 | tf_op jit(solution)/shard_map/ppermute | solution.py:341
  213.1 14.3 %collective-permute-start.8 = (bf16[128,1280]{1,0:T(8,128)(2,1)S(1)}, bf16[128,1280]{1,0:T(8,128)(2,1)S(1)}, u32[]{:S(2)}, u32[]{:S(2)}) collective-permute-start(bf16[128,1280]{1,0:T(8,128)(2,1)S(1)} %combine.6), channel_id=1, source_target_pairs={{28,0},{0,4},{4,8},{8,12},{12,16},{16,20},{20,24},{24,28},{29,1},{... | collective-permute-start | bytes 983048 | tf_op jit(solution)/shard_map/ppermute | solution.py:341
  215.0 12.4 %collective-permute-start.7 = (bf16[128,1280]{1,0:T(8,128)(2,1)S(1)}, bf16[128,1280]{1,0:T(8,128)(2,1)S(1)}, u32[]{:S(2)}, u32[]{:S(2)}) collective-permute-start(bf16[128,1280]{1,0:T(8,128)(2,1)S(1)} %combine.5), channel_id=1, source_target_pairs={{4,0},{8,4},{12,8},{16,12},{20,16},{24,20},{28,24},{0,28},{5,1},{9... | collective-permute-start | bytes 983048 | tf_op jit(solution)/shard_map/ppermute | solution.py:341
Sparse Core Ops, SparseCore 0:
  29.2 56.1 all-gather.2
  87.5 71.2 all-gather.4

commit v6 on v5

--- a/solution.py
+++ b/solution.py
@@ -174,28 +174,28 @@
     results = []
     for j in range(hosted):
         current = pending
-        current[0].wait()
-        wide = rows[j].reshape(-1, width).astype(jnp.float32)
-        scale = lax.rsqrt(jnp.mean(wide * wide, axis=-1, keepdims=True) + 1e-06)
-        normed = (wide * scale * gain_ref[...]).astype(jnp.bfloat16)
-        current[1].wait()
+        for copy in current:
+            copy.wait()
         if j + 1 < hosted:
             pending = load(j + 1)
-        both = jnp.dot(normed, weight[j, :, :first], preferred_element_type=jnp.float32)
-        gate = both[:, :hidden]
-        up = both[:, hidden:]
-        act = (gate / (1.0 + jnp.exp(-gate)) * up).astype(jnp.bfloat16)
-        current[2].wait()
-        out[j] = (
-            lax.dot_general(
-                act,
-                weight[j, :, first : first + hidden],
-                (((1,), (1,)), ((), ())),
-                preferred_element_type=jnp.float32,
+        for i in range(0, cols, 2):
+            wide = rows[j, i : i + 2].reshape(-1, width).astype(jnp.float32)
+            scale = lax.rsqrt(jnp.mean(wide * wide, axis=-1, keepdims=True) + 1e-06)
+            normed = (wide * scale * gain_ref[...]).astype(jnp.bfloat16)
+            both = jnp.dot(normed, weight[j, :, :first], preferred_element_type=jnp.float32)
+            gate = both[:, :hidden]
+            up = both[:, hidden:]
+            act = (gate / (1.0 + jnp.exp(-gate)) * up).astype(jnp.bfloat16)
+            out[j, i : i + 2] = (
+                lax.dot_general(
+                    act,
+                    weight[j, :, first : first + hidden],
+                    (((1,), (1,)), ((), ())),
+                    preferred_element_type=jnp.float32,
+                )
+                .astype(jnp.bfloat16)
+                .reshape(2, count, width)
             )
-            .astype(jnp.bfloat16)
-            .reshape(cols, count, width)
-        )
         result = pltpu.make_async_copy(out.at[j], out_hbm.at[:, j], sems.at[j, 3])
         result.start()
         results.append(result)
@@ -282,21 +282,20 @@
 
     half = w_merge.shape[0] // 2
     piece = lax.dynamic_slice_in_dim(w_merge.T, lax.axis_index("core") * half, half, 1)
+    piece = lax.all_to_all(
+        jnp.broadcast_to(piece[None], (cols,) + piece.shape), "x", split_axis=0, concat_axis=0
+    )
+    piece = piece.reshape(-1, half)
+    queries, w_gate, w_up, w_down, routes, route_weight, piece = lax.optimization_barrier(
+        (queries, w_gate, w_up, w_down, routes, route_weight, piece)
+    )
+    merger = lax.all_gather(piece, ("core", "y"), axis=0, tiled=True)
+    merger = merger.reshape(2, -1, half)
+
     down = w_down[0].T
     blank = jnp.zeros((down.shape[0], -(-3 * hidden // 128) * 128 - 3 * hidden), down.dtype)
     own = jnp.concatenate([w_gate[0], w_up[0], down, blank], axis=1)
-    own, piece = lax.optimization_barrier((own, piece))
     other = lax.ppermute(own, "y", shift(rows, rows // 2))
-    piece = lax.all_to_all(
-        jnp.broadcast_to(piece[None], (cols,) + piece.shape), "x", split_axis=0, concat_axis=0
-    )
-    piece = piece.reshape(-1, half)
-    queries, routes, route_weight, piece, own, other = lax.optimization_barrier(
-        (queries, routes, route_weight, piece, own, other)
-    )
-    merger = lax.all_gather(piece, ("core", "y"), axis=0, tiled=True)
-    merger = merger.reshape(2, -1, half)
-
     routing = jnp.concatenate(
         [
             jnp.pad(routes, ((0, TPAD - tokens), (0, 0)), constant_values=-1).astype(jnp.float32),
@@ -314,12 +313,9 @@
     merged = jnp.where(live, space_to_depth(vis), jnp.zeros((), jnp.bfloat16))
     merged = jnp.pad(merged, ((0, TPAD - tokens), (0, 0)))
 
+    own, other, merged, table, mix = lax.optimization_barrier((own, other, merged, table, mix))
     mine = jnp.concatenate([own, other], axis=1)
-    mine, merger, merged, table, mix = lax.optimization_barrier(
-        (mine, merger, merged, table, mix)
-    )
     experts = lax.all_gather(mine, ("z", "core"), axis=0, tiled=True)
-
     stream = merge(merged, merger)
     width = stream.shape[1]
     shape = (cols, 2, 1 + len(steps), SLOT, width)

time: 236 us -> 236 us (level)
  waiting for transfers between devices: 77.8 us -> 83.2 us
  starting transfers between devices: 46.8 us -> 41.4 us
    ppermute x1, waiting for transfers between devices: 1.56 us -> 6.66 us  [local(): other = lax.ppermute(own, 'y', shift(rows, rows // 2))]
    ppermute x1, starting transfers between devices: 8.28 us -> 4.38 us  [local(): other = lax.ppermute(own, 'y', shift(rows, rows // 2))]
  transfers between devices with their start and end apart: 13 -> 13, of which waited for: 8 -> 8; matrix products, arithmetic and copies ran while one was open for 9% -> 10% of each run, Pallas kernels for 5% -> 5%
where the time goes in v6:
time: 236 us; the launch traced here: 235 us
  waiting for transfers between devices  83.2 us (35%)
  blocking collectives  46.4 us (20%)
  starting transfers between devices  41.4 us (18%)
  Pallas kernels  24.4 us (10%)
  between operations  14.5 us (6%)
  matrix products  12.2 us (5%)
  local copies, waits for them, and re-layouts  9.52 us (4%)
  other arithmetic  3.7 us (2%)
    all_to_all x1, blocking collectives, local(): lax.all_to_all(outcome.reshape(flat), 'x', split_axis=0, concat_axis=0)  35.5 us
    all_to_all x1, waiting for transfers between devices, local(): lax.all_to_all(send.reshape(flat), 'x', split_axis=0, concat_axis=0)  28.2 us
    all_gather x1, waiting for transfers between devices, local(): merger = lax.all_gather(piece, ('core', 'y'), axis=0, tiled=True)  22 us
    all_gather x1, waiting for transfers between devices, local(): experts = lax.all_gather(mine, ('z', 'core'), axis=0, tiled=True)  13.3 us
    pallas_call x1, Pallas kernels, expert_ffn(): pl.pallas_call(functools.partial(expert_body, hidden), in_specs=[hbm, pl....  12.1 us
    ppermute x3, starting transfers between devices, local(): lax.ppermute(combine(mix, back, i + 1, jnp.bfloat16), 'y', back_again(step))  11.8 us
    ppermute x3, starting transfers between devices, local(): lax.ppermute(routing, 'y', step)  11.6 us
    all_to_all x1, blocking collectives, local(): lax.all_to_all(jnp.broadcast_to(piece[None], (cols,) + piece.shape), 'x',...  10.8 us
  transfers between devices with their start and end apart: 13, of which 8 were waited for; matrix products, arithmetic and copies ran while one was open for 10% of the time, Pallas kernels for 5%

profile of v6, /device:TPU:1, one launch (start us, length us, event | category | flops | bytes accessed | tf_op | source)
XLA Modules:
  0.0 235.3 jit_solution(2186995957152421721)
XLA Ops:
  6.5 1.0 dynamic-slice_bitcast_fusion
  7.5 10.8 %all_to_all.15 = bf16[4,40,1152]{2,1,0:T(8,128)(2,1)} all-to-all(bf16[4,40,1152]{2,1,0:T(8,128)(2,1)S(1)} %broadcast_in_dim.71), channel_id=1, replica_groups=mesh['z'=8,'core'=2,'y'=8,'x'=4] {'x'}, dimensions={0} | all-to-all | bytes 737280 | tf_op jit(solution)/shard_map/all_to_all | solution.py:285
  18.7 1.2 constant_dynamic-slice_fusion
  20.6 0.7 pad_convert_fusion
  21.3 0.7 fusion.22
  22.0 5.0 %collective-permute-start.3 = (f32[12,128]{1,0:T(8,128)S(1)}, f32[12,128]{1,0:T(8,128)S(1)}, u32[]{:S(2)}, u32[]{:S(2)}) collective-permute-start(f32[12,128]{1,0:T(8,128)S(1)} %get-tuple-element.36), channel_id=1, source_target_pairs={{0,8},{4,28},{8,16},{12,4},{16,24},{20,12},{24,0},{28,20},{1,9},{5... | collective-permute-start | bytes 18440 | tf_op jit(solution)/shard_map/ppermute | solution.py:307
  27.0 4.6 %collective-permute-start.2 = (f32[12,128]{1,0:T(8,128)S(1)}, f32[12,128]{1,0:T(8,128)S(1)}, u32[]{:S(2)}, u32[]{:S(2)}) collective-permute-start(f32[12,128]{1,0:T(8,128)S(1)} %get-tuple-element.36), channel_id=1, source_target_pairs={{0,28},{4,0},{8,4},{12,8},{16,12},{20,16},{24,20},{28,24},{1,29},{... | collective-permute-start | bytes 18440 | tf_op jit(solution)/shard_map/ppermute | solution.py:307
  31.7 1.9 collective-permute-start.1
  33.6 1.2 concatenate.16
  34.8 4.4 %collective-permute-start = (bf16[80,2176]{1,0:T(8,128)(2,1)S(1)}, bf16[80,2176]{1,0:T(8,128)(2,1)S(1)}, u32[]{:S(2)}, u32[]{:S(2)}) collective-permute-start(bf16[80,2176]{1,0:T(8,128)(2,1)S(1)} %concatenate.16), channel_id=1, source_target_pairs={{0,16},{4,20},{8,24},{12,28},{16,0},{20,4},{24,8},{28,12},{1,17},{... | collective-permute-start | bytes 1044488 | tf_op jit(solution)/shard_map/ppermute | solution.py:298
  39.2 7.2 %fusion.27 = (f32[8,484]{1,0:T(8,128)S(1)}, f32[8,484,484]{1,2,0:T(8,128)}) fusion(bf16[484,8,72]{0,2,1:T(8,128)(2,1)} %bitcast.66, bf16[484,8,72]{0,2,1:T(8,128)(2,1)} %bitcast.67), kind=kOutput, calls=%fused_computation.47 | convolution fusion | flops 275485536 | bytes 8626816 | tf_op jit(solution)/shard_map/sub | solution.py:29
  46.4 4.2 %fusion.7 = bf16[8,484,72]{1,2,0:T(8,128)(2,1)S(1)} fusion(bf16[484,8,72]{0,2,1:T(8,128)(2,1)S(1)} %bitcast.68, f32[8,484,484]{1,2,0:T(8,128)} %get-tuple-element.38, f32[8,484]{1,0:T(8,128)S(1)} %get-tuple-element.37), kind=kOutput, calls=%fused_computation.9 | convolution fusion | flops 273889792 | bytes 8626816 | tf_op jit(solution)/shard_map/hqk,khd->qhd/dot_general | solution.py:31
  50.6 0.7 fusion.8
  51.3 0.3 copy.35
  51.6 0.8 select_n.66
  52.4 0.4 copy.36
  52.9 1.1 select_n.68
  54.0 0.9 pad.12.merged_ref
  56.1 6.7 %collective-permute-done = bf16[80,2176]{1,0:T(8,128)(2,1)S(1)} collective-permute-done((bf16[80,2176]{1,0:T(8,128)(2,1)S(1)}, bf16[80,2176]{1,0:T(8,128)(2,1)S(1)}, u32[]{:S(2)}, u32[]{:S(2)}) %collective-permute-start) | collective-permute-done | bytes 348192 | tf_op jit(solution)/shard_map/ppermute | solution.py:298
  62.8 0.9 pad_maximum_fusion
  63.7 22.0 %all-gather.3.cloned.1.call-done = bf16[2560,1152]{1,0:T(8,128)(2,1)} async-done(((bf16[160,1152]{1,0:T(8,128)(2,1)}), bf16[2560,1152]{1,0:T(8,128)(2,1)}) %all-gather.3.cloned.1.call-update) | async-done | bytes 5898256 | tf_op jit(solution)/shard_map/all_gather | solution.py:292
  85.7 6.3 %merge.1.tile_ref = bf16[128,1280]{1,0:T(8,128)(2,1)} custom-call(bf16[128,2304]{1,0:T(8,128)(2,1)} %pad.12.merged_ref, bf16[2,1280,1152]{2,1,0:T(8,128)(2,1)} %bitcast.53), custom_call_target="tpu_custom_call" | custom-call | flops 754974720 | bytes 7340032 | tf_op jit(solution)/shard_map/merge/pallas_call | solution.py:94
  92.0 3.2 %collective-permute-start.6 = (bf16[128,1280]{1,0:T(8,128)(2,1)}, bf16[128,1280]{1,0:T(8,128)(2,1)S(1)}, u32[]{:S(2)}, u32[]{:S(2)}) collective-permute-start(bf16[128,1280]{1,0:T(8,128)(2,1)} %merge.1.tile_ref), channel_id=1, source_target_pairs={{0,4},{4,8},{8,12},{12,16},{16,20},{20,24},{24,28},{28,0},{1,5},{5... | collective-permute-start | bytes 983048 | tf_op jit(solution)/shard_map/ppermute | solution.py:322
  95.2 3.3 %collective-permute-start.5 = (bf16[128,1280]{1,0:T(8,128)(2,1)}, bf16[128,1280]{1,0:T(8,128)(2,1)S(1)}, u32[]{:S(2)}, u32[]{:S(2)}) collective-permute-start(bf16[128,1280]{1,0:T(8,128)(2,1)} %merge.1.tile_ref), channel_id=1, source_target_pairs={{0,28},{4,0},{8,4},{12,8},{16,12},{20,16},{24,20},{28,24},{1,29},{... | collective-permute-start | bytes 983048 | tf_op jit(solution)/shard_map/ppermute | solution.py:322
  98.5 2.4 %collective-permute-start.4 = (bf16[128,1280]{1,0:T(8,128)(2,1)}, bf16[128,1280]{1,0:T(8,128)(2,1)S(1)}, u32[]{:S(2)}, u32[]{:S(2)}) collective-permute-start(bf16[128,1280]{1,0:T(8,128)(2,1)} %merge.1.tile_ref), channel_id=1, source_target_pairs={{0,8},{4,28},{8,16},{12,4},{16,24},{20,12},{24,0},{28,20},{1,9},{5... | collective-permute-start | bytes 983048 | tf_op jit(solution)/shard_map/ppermute | solution.py:322
  101.1 1.0 copy-done.1
  102.0 1.2 pick_rows.4.refs_0_
  103.3 1.1 collective-permute-done.6.tile_ref
  104.4 1.2 pick_rows.5.refs_0_
  105.5 0.6 collective-permute-done.5.tile_ref
  106.1 1.2 pick_rows.6.refs_0_
  107.3 3.9 %collective-permute-done.4.tile_ref = bf16[128,1280]{1,0:T(8,128)(2,1)S(1)} collective-permute-done((bf16[128,1280]{1,0:T(8,128)(2,1)}, bf16[128,1280]{1,0:T(8,128)(2,1)S(1)}, u32[]{:S(2)}, u32[]{:S(2)}) %collective-permute-start.4) | collective-permute-done | bytes 327712 | tf_op jit(solution)/shard_map/ppermute | solution.py:322
  111.2 1.2 pick_rows.7
  112.4 4.7 %all-to-all-start.1 = ((bf16[4,256,1280]{2,1,0:T(8,128)(2,1)}), bf16[4,256,1280]{2,1,0:T(8,128)(2,1)}, u32[]{:S(2)}, u32[]{:S(2)}) async-start(bf16[4,256,1280]{2,1,0:T(8,128)(2,1)} %bitcast.27), calls=%async_computation.1 | async-start | bytes 5242880 | tf_op jit(solution)/shard_map/all_to_all | solution.py:327
  117.1 0.6 broadcast_in_dim.84.gain_ref
  117.7 28.2 %all-to-all-done.1 = bf16[4,256,1280]{2,1,0:T(8,128)(2,1)} async-done(((bf16[4,256,1280]{2,1,0:T(8,128)(2,1)}), bf16[4,256,1280]{2,1,0:T(8,128)(2,1)}, u32[]{:S(2)}, u32[]{:S(2)}) %all-to-all-start.1) | async-done | bytes 2621472 | tf_op jit(solution)/shard_map/all_to_all | solution.py:327
  146.0 13.3 %all-gather.5.cloned.1.call-done.weight_hbm = bf16[1280,4352]{1,0:T(8,128)(2,1)} async-done(((bf16[80,4352]{1,0:T(8,128)(2,1)}), bf16[1280,4352]{1,0:T(8,128)(2,1)}) %all-gather.5.cloned.1.call-update) | async-done | bytes 11141136 | tf_op jit(solution)/shard_map/all_gather | solution.py:318
  159.2 12.1 %expert_ffn.1 = bf16[4,2,128,1280]{3,2,1,0:T(8,128)(2,1)} custom-call(bf16[4,2,128,1280]{3,2,1,0:T(8,128)(2,1)} %bitcast.28.rows_hbm, f32[1,1280]{1,0:T(1,128)} %broadcast_in_dim.84.gain_ref, bf16[1280,4352]{1,0:T(8,128)(2,1)} %all-gather.5.cloned.1.call-done.weight_hbm), custom_call_target="tpu_custom_call" | custom-call | flops 5536481280 | bytes 16777216 | tf_op jit(solution)/shard_map/expert_ffn/pallas_call | solution.py:210
  171.3 35.5 %all_to_all.16 = bf16[4,256,1280]{2,1,0:T(8,128)(2,1)S(1)} all-to-all(bf16[4,256,1280]{2,1,0:T(8,128)(2,1)} %bitcast.54), channel_id=1, replica_groups=mesh['z'=8,'core'=2,'y'=8,'x'=4] {'x'}, dimensions={0} | all-to-all | bytes 5242880 | tf_op jit(solution)/shard_map/all_to_all | solution.py:334
  206.8 0.3 combine.7
  207.2 0.3 combine.6
  207.6 0.3 combine.5
  207.9 5.3 %collective-permute-start.9 = (bf16[128,1280]{1,0:T(8,128)(2,1)S(1)}, bf16[128,1280]{1,0:T(8,128)(2,1)S(1)}, u32[]{:S(2)}, u32[]{:S(2)}) collective-permute-start(bf16[128,1280]{1,0:T(8,128)(2,1)S(1)} %combine.7), channel_id=1, source_target_pairs={{8,0},{28,4},{16,8},{4,12},{24,16},{12,20},{0,24},{20,28},{9,1},{2... | collective-permute-start | bytes 983048 | tf_op jit(solution)/shard_map/ppermute | solution.py:337
  213.2 1.9 collective-permute-start.8
  215.2 4.6 %collective-permute-start.7 = (bf16[128,1280]{1,0:T(8,128)(2,1)S(1)}, bf16[128,1280]{1,0:T(8,128)(2,1)S(1)}, u32[]{:S(2)}, u32[]{:S(2)}) collective-permute-start(bf16[128,1280]{1,0:T(8,128)(2,1)S(1)} %combine.5), channel_id=1, source_target_pairs={{4,0},{8,4},{12,8},{16,12},{20,16},{24,20},{28,24},{0,28},{5,1},{9... | collective-permute-start | bytes 983048 | tf_op jit(solution)/shard_map/ppermute | solution.py:337
  219.8 0.3 combine.4
  220.1 7.4 %collective-permute-done.8 = bf16[128,1280]{1,0:T(8,128)(2,1)S(1)} collective-permute-done((bf16[128,1280]{1,0:T(8,128)(2,1)S(1)}, bf16[128,1280]{1,0:T(8,128)(2,1)S(1)}, u32[]{:S(2)}, u32[]{:S(2)}) %collective-permute-start.8) | collective-permute-done | bytes 327712 | tf_op jit(solution)/shard_map/ppermute | solution.py:337
  227.5 0.9 fusion.15
  (44 shorter events, 1.7 us)
Async XLA Ops:
  6.5 44.0 %copy-start = (bf16[576,576]{1,0:T(8,128)(2,1)S(1)}, bf16[576,576]{1,0:T(8,128)(2,1)}, u32[]{:S(2)}) copy-start(bf16[576,576]{1,0:T(8,128)(2,1)} %param.17) | copy-start | bytes 1990660
  6.5 79.2 %all-gather.3.cloned.1.call-start = ((), (), s32[]{:S(2)}) async-start(), calls=%async_computation.3 | async-start | bytes 6266880 | tf_op jit(solution)/shard_map/all_gather | solution.py:292
  18.4 140.8 %all-gather.5.cloned.1.call-start = ((), (), s32[]{:S(2)}) async-start(), calls=%async_computation.4 | async-start | bytes 11837440 | tf_op jit(solution)/shard_map/all_gather | solution.py:318
  22.0 32.8 %collective-permute-start.3 = (f32[12,128]{1,0:T(8,128)S(1)}, f32[12,128]{1,0:T(8,128)S(1)}, u32[]{:S(2)}, u32[]{:S(2)}) collective-permute-start(f32[12,128]{1,0:T(8,128)S(1)} %get-tuple-element.36), channel_id=1, source_target_pairs={{0,8},{4,28},{8,16},{12,4},{16,24},{20,12},{24,0},{28,20},{1,9},{5... | collective-permute-start | bytes 18440 | tf_op jit(solution)/shard_map/ppermute | solution.py:307
  27.0 27.8 %collective-permute-start.2 = (f32[12,128]{1,0:T(8,128)S(1)}, f32[12,128]{1,0:T(8,128)S(1)}, u32[]{:S(2)}, u32[]{:S(2)}) collective-permute-start(f32[12,128]{1,0:T(8,128)S(1)} %get-tuple-element.36), channel_id=1, source_target_pairs={{0,28},{4,0},{8,4},{12,8},{16,12},{20,16},{24,20},{28,24},{1,29},{... | collective-permute-start | bytes 18440 | tf_op jit(solution)/shard_map/ppermute | solution.py:307
  31.7 23.2 %collective-permute-start.1 = (f32[12,128]{1,0:T(8,128)S(1)}, f32[12,128]{1,0:T(8,128)S(1)}, u32[]{:S(2)}, u32[]{:S(2)}) collective-permute-start(f32[12,128]{1,0:T(8,128)S(1)} %get-tuple-element.36), channel_id=1, source_target_pairs={{0,4},{4,8},{8,12},{12,16},{16,20},{20,24},{24,28},{28,0},{1,5},{5... | collective-permute-start | bytes 18440 | tf_op jit(solution)/shard_map/ppermute | solution.py:307
  34.8 28.0 %collective-permute-start = (bf16[80,2176]{1,0:T(8,128)(2,1)S(1)}, bf16[80,2176]{1,0:T(8,128)(2,1)S(1)}, u32[]{:S(2)}, u32[]{:S(2)}) collective-permute-start(bf16[80,2176]{1,0:T(8,128)(2,1)S(1)} %concatenate.16), channel_id=1, source_target_pairs={{0,16},{4,20},{8,24},{12,28},{16,0},{20,4},{24,8},{28,12},{1,17},{... | collective-permute-start | bytes 1044488 | tf_op jit(solution)/shard_map/ppermute | solution.py:298
  39.2 7.2 %copy-start.4 = (bf16[484,576]{0,1:T(8,128)(2,1)S(1)}, bf16[484,576]{0,1:T(8,128)(2,1)}, u32[]{:S(2)}) copy-start(bf16[484,576]{0,1:T(8,128)(2,1)} %param.15) | copy-start | bytes 1672708
  46.4 4.2 %copy-start.5 = (bf16[484,576]{0,1:T(8,128)(2,1)S(1)}, bf16[484,576]{0,1:T(8,128)(2,1)}, u32[]{:S(2)}) copy-start(bf16[484,576]{0,1:T(8,128)(2,1)} %param.16) | copy-start | bytes 1672708
  92.0 12.4 %collective-permute-start.6 = (bf16[128,1280]{1,0:T(8,128)(2,1)}, bf16[128,1280]{1,0:T(8,128)(2,1)S(1)}, u32[]{:S(2)}, u32[]{:S(2)}) collective-permute-start(bf16[128,1280]{1,0:T(8,128)(2,1)} %merge.1.tile_ref), channel_id=1, source_target_pairs={{0,4},{4,8},{8,12},{12,16},{16,20},{20,24},{24,28},{28,0},{1,5},{5... | collective-permute-start | bytes 983048 | tf_op jit(solution)/shard_map/ppermute | solution.py:322
  95.2 10.9 %collective-permute-start.5 = (bf16[128,1280]{1,0:T(8,128)(2,1)}, bf16[128,1280]{1,0:T(8,128)(2,1)S(1)}, u32[]{:S(2)}, u32[]{:S(2)}) collective-permute-start(bf16[128,1280]{1,0:T(8,128)(2,1)} %merge.1.tile_ref), channel_id=1, source_target_pairs={{0,28},{4,0},{8,4},{12,8},{16,12},{20,16},{24,20},{28,24},{1,29},{... | collective-permute-start | bytes 983048 | tf_op jit(solution)/shard_map/ppermute | solution.py:322
  98.5 12.7 %collective-permute-start.4 = (bf16[128,1280]{1,0:T(8,128)(2,1)}, bf16[128,1280]{1,0:T(8,128)(2,1)S(1)}, u32[]{:S(2)}, u32[]{:S(2)}) collective-permute-start(bf16[128,1280]{1,0:T(8,128)(2,1)} %merge.1.tile_ref), channel_id=1, source_target_pairs={{0,8},{4,28},{8,16},{12,4},{16,24},{20,12},{24,0},{28,20},{1,9},{5... | collective-permute-start | bytes 983048 | tf_op jit(solution)/shard_map/ppermute | solution.py:322
  101.1 1.0 copy-start.1
  112.4 4.7 %copy-start.3 = (f32[1280]{0:T(1024)S(1)}, f32[1280]{0:T(1024)}, u32[]{:S(2)}) copy-start(f32[1280]{0:T(1024)} %param.19) | copy-start | bytes 15364
  112.4 33.6 %all-to-all-start.1 = ((bf16[4,256,1280]{2,1,0:T(8,128)(2,1)}), bf16[4,256,1280]{2,1,0:T(8,128)(2,1)}, u32[]{:S(2)}, u32[]{:S(2)}) async-start(bf16[4,256,1280]{2,1,0:T(8,128)(2,1)} %bitcast.27), calls=%async_computation.1 | async-start | bytes 5242880 | tf_op jit(solution)/shard_map/all_to_all | solution.py:327
  207.5 20.0 %copy-start.2 = (bf16[128,1280]{1,0:T(8,128)(2,1)S(1)}, bf16[128,1280]{1,0:T(8,128)(2,1)}, u32[]{:S(2)}) copy-start(bf16[128,1280]{1,0:T(8,128)(2,1)} %merge.1.tile_ref) | copy-start | bytes 983044
  207.9 12.2 %collective-permute-start.9 = (bf16[128,1280]{1,0:T(8,128)(2,1)S(1)}, bf16[128,1280]{1,0:T(8,128)(2,1)S(1)}, u32[]{:S(2)}, u32[]{:S(2)}) collective-permute-start(bf16[128,1280]{1,0:T(8,128)(2,1)S(1)} %combine.7), channel_id=1, source_target_pairs={{8,0},{28,4},{16,8},{4,12},{24,16},{12,20},{0,24},{20,28},{9,1},{2... | collective-permute-start | bytes 983048 | tf_op jit(solution)/shard_map/ppermute | solution.py:337
  213.2 14.3 %collective-permute-start.8 = (bf16[128,1280]{1,0:T(8,128)(2,1)S(1)}, bf16[128,1280]{1,0:T(8,128)(2,1)S(1)}, u32[]{:S(2)}, u32[]{:S(2)}) collective-permute-start(bf16[128,1280]{1,0:T(8,128)(2,1)S(1)} %combine.6), channel_id=1, source_target_pairs={{28,0},{0,4},{4,8},{8,12},{12,16},{16,20},{20,24},{24,28},{29,1},{... | collective-permute-start | bytes 983048 | tf_op jit(solution)/shard_map/ppermute | solution.py:337
  215.2 12.4 %collective-permute-start.7 = (bf16[128,1280]{1,0:T(8,128)(2,1)S(1)}, bf16[128,1280]{1,0:T(8,128)(2,1)S(1)}, u32[]{:S(2)}, u32[]{:S(2)}) collective-permute-start(bf16[128,1280]{1,0:T(8,128)(2,1)S(1)} %combine.5), channel_id=1, source_target_pairs={{4,0},{8,4},{12,8},{16,12},{20,16},{24,20},{28,24},{0,28},{5,1},{9... | collective-permute-start | bytes 983048 | tf_op jit(solution)/shard_map/ppermute | solution.py:337
Sparse Core Ops, SparseCore 0:
  18.5 67.1 all-gather.2
  87.8 71.3 all-gather.4

commit v7 on v6

--- a/solution.py
+++ b/solution.py
@@ -147,78 +147,82 @@
     )(table, tile, *given)
 
 
-def expert_body(hidden, rows_hbm, gain_ref, weight_hbm, out_hbm, rows, weight, out, sems):
-    cols, hosted, count, width = rows_hbm.shape
-    span = weight_hbm.shape[1] // hosted
+def expert_body(hidden, rows, gain_ref, weight_hbm, out_hbm, weight, out, load_sems, store_sems):
+    cols, hosted, count, width = rows.shape
     first = 2 * hidden
-
-    def load(j):
-        copies = [
-            pltpu.make_async_copy(rows_hbm.at[:, j], rows.at[j], sems.at[j, 0]),
-            pltpu.make_async_copy(
-                weight_hbm.at[:, pl.ds(j * span, first)],
-                weight.at[j, :, pl.ds(0, first)],
-                sems.at[j, 1],
-            ),
-            pltpu.make_async_copy(
-                weight_hbm.at[:, pl.ds(j * span + first, span - first)],
-                weight.at[j, :, pl.ds(first, span - first)],
-                sems.at[j, 2],
-            ),
-        ]
-        for copy in copies:
-            copy.start()
-        return copies
-
-    pending = load(0)
-    results = []
+    downs = hosted * first
+    cut = -(-(downs + hidden) // 128) * 128
+    spans = ((0, first), (downs, cut)), ((first, downs), (cut, weight.shape[1]))
+
+    def load(j, part):
+        start, stop = spans[j][part]
+        lanes = pl.ds(start, stop - start)
+        copy = pltpu.make_async_copy(
+            weight_hbm.at[:, lanes], weight.at[:, lanes], load_sems.at[j, part]
+        )
+        copy.start()
+        return copy
+
+    pending = [load(0, 0), load(0, 1)]
+    stores = []
     for j in range(hosted):
-        current = pending
-        for copy in current:
-            copy.wait()
-        if j + 1 < hosted:
-            pending = load(j + 1)
-        for i in range(0, cols, 2):
-            wide = rows[j, i : i + 2].reshape(-1, width).astype(jnp.float32)
+        last = j + 1 == hosted
+        chunks = range(0, cols, 2)
+        current, acts = pending, []
+        current[0].wait()
+        pending = [] if last else [load(j + 1, 0)]
+        for i in chunks:
+            wide = rows[i : i + 2, j].reshape(-1, width).astype(jnp.float32)
             scale = lax.rsqrt(jnp.mean(wide * wide, axis=-1, keepdims=True) + 1e-06)
             normed = (wide * scale * gain_ref[...]).astype(jnp.bfloat16)
-            both = jnp.dot(normed, weight[j, :, :first], preferred_element_type=jnp.float32)
+            both = jnp.dot(normed, weight[:, j * first : (j + 1) * first], preferred_element_type=jnp.float32)
             gate = both[:, :hidden]
             up = both[:, hidden:]
-            act = (gate / (1.0 + jnp.exp(-gate)) * up).astype(jnp.bfloat16)
+            acts.append((gate / (1.0 + jnp.exp(-gate)) * up).astype(jnp.bfloat16))
+        current[1].wait()
+        if not last:
+            pending.append(load(j + 1, 1))
+        lead = (downs + j * hidden) % 128
+        start = downs + j * hidden - lead
+        for i, act in zip(chunks, acts):
+            if lead:
+                blank = jnp.zeros((act.shape[0], lead), act.dtype)
+                act = jnp.concatenate([blank, act], axis=1)
             out[j, i : i + 2] = (
                 lax.dot_general(
                     act,
-                    weight[j, :, first : first + hidden],
+                    weight[:, start : start + lead + hidden],
                     (((1,), (1,)), ((), ())),
                     preferred_element_type=jnp.float32,
                 )
                 .astype(jnp.bfloat16)
                 .reshape(2, count, width)
             )
-        result = pltpu.make_async_copy(out.at[j], out_hbm.at[:, j], sems.at[j, 3])
-        result.start()
-        results.append(result)
-    for result in results:
-        result.wait()
+            store = pltpu.make_async_copy(
+                out.at[j, pl.ds(i, 2)], out_hbm.at[pl.ds(i, 2), j], store_sems.at[j, i // 2]
+            )
+            store.start()
+            stores.append(store)
+    for store in stores:
+        store.wait()
 
 
 def expert_ffn(rows, gain, weight, hidden):
     cols, hosted, count, width = rows.shape
-    held = (hosted, cols, count, width)
+    vmem = pl.BlockSpec(memory_space=pltpu.VMEM)
     hbm = pl.BlockSpec(memory_space=pltpu.HBM)
     return pl.pallas_call(
         functools.partial(expert_body, hidden),
-        in_specs=[hbm, pl.BlockSpec(memory_space=pltpu.VMEM), hbm],
+        in_specs=[vmem, vmem, hbm],
         out_specs=hbm,
         out_shape=jax.ShapeDtypeStruct(rows.shape, jnp.bfloat16),
         scratch_shapes=[
-            pltpu.VMEM(held, jnp.bfloat16),
-            pltpu.VMEM((hosted, width, weight.shape[1] // hosted), jnp.bfloat16),
-            pltpu.VMEM(held, jnp.bfloat16),
-            pltpu.SemaphoreType.DMA((hosted, 4)),
-        ],
-        compiler_params=pltpu.CompilerParams(vmem_limit_bytes=60 << 20),
+            pltpu.VMEM(weight.shape, jnp.bfloat16),
+            pltpu.VMEM((hosted, cols, count, width), jnp.bfloat16),
+            pltpu.SemaphoreType.DMA((hosted, 2)),
+            pltpu.SemaphoreType.DMA((hosted, cols // 2)),
+        ],
+        compiler_params=pltpu.CompilerParams(vmem_limit_bytes=40 << 20),
         cost_estimate=pl.CostEstimate(
             flops=6 * cols * hosted * count * width * hidden,
             bytes_accessed=16 << 20,
@@ -292,9 +296,7 @@
     merger = lax.all_gather(piece, ("core", "y"), axis=0, tiled=True)
     merger = merger.reshape(2, -1, half)
 
-    down = w_down[0].T
-    blank = jnp.zeros((down.shape[0], -(-3 * hidden // 128) * 128 - 3 * hidden), down.dtype)
-    own = jnp.concatenate([w_gate[0], w_up[0], down, blank], axis=1)
+    own = jnp.concatenate([w_gate[0], w_up[0], w_down[0].T], axis=1)
     other = lax.ppermute(own, "y", shift(rows, rows // 2))
     routing = jnp.concatenate(
         [
@@ -314,7 +316,10 @@
     merged = jnp.pad(merged, ((0, TPAD - tokens), (0, 0)))
 
     own, other, merged, table, mix = lax.optimization_barrier((own, other, merged, table, mix))
-    mine = jnp.concatenate([own, other], axis=1)
+    first = 2 * hidden
+    mine = jnp.concatenate(
+        [own[:, :first], other[:, :first], own[:, first:], other[:, first:]], axis=1
+    )
     experts = lax.all_gather(mine, ("z", "core"), axis=0, tiled=True)
     stream = merge(merged, merger)
     width = stream.shape[1]

time: 236 us -> 235 us (level)
  transfers between devices with their start and end apart: 13 -> 13, of which waited for: 8 -> 8; matrix products, arithmetic and copies ran while one was open for 10% -> 9% of each run, Pallas kernels for 5% -> 5%
where the time goes in v7:
time: 235 us; the launch traced here: 234 us
  waiting for transfers between devices  82.1 us (35%)
  blocking collectives  46.1 us (20%)
  starting transfers between devices  41.5 us (18%)
  Pallas kernels  24.9 us (11%)
  between operations  14.5 us (6%)
  matrix products  12.1 us (5%)
  local copies, waits for them, and re-layouts  9.98 us (4%)
  other arithmetic  2.8 us (1%)
    all_to_all x1, blocking collectives, local(): lax.all_to_all(outcome.reshape(flat), 'x', split_axis=0, concat_axis=0)  35.3 us
    all_to_all x1, waiting for transfers between devices, local(): lax.all_to_all(send.reshape(flat), 'x', split_axis=0, concat_axis=0)  28.9 us
    all_gather x1, waiting for transfers between devices, local(): merger = lax.all_gather(piece, ('core', 'y'), axis=0, tiled=True)  21.9 us
    pallas_call x1, Pallas kernels, expert_ffn(): pl.pallas_call(functools.partial(expert_body, hidden), in_specs=[vmem, vm...  12.5 us
    ppermute x3, starting transfers between devices, local(): lax.ppermute(combine(mix, back, i + 1, jnp.bfloat16), 'y', back_again(step))  11.8 us
    ppermute x3, starting transfers between devices, local(): lax.ppermute(routing, 'y', step)  11.6 us
    all_gather x1, waiting for transfers between devices, local(): experts = lax.all_gather(mine, ('z', 'core'), axis=0, tiled=True)  11.5 us
    all_to_all x1, blocking collectives, local(): lax.all_to_all(jnp.broadcast_to(piece[None], (cols,) + piece.shape), 'x',...  10.8 us
  transfers between devices with their start and end apart: 13, of which 8 were waited for; matrix products, arithmetic and copies ran while one was open for 9% of the time, Pallas kernels for 5%

profile of v7, /device:TPU:1, one launch (start us, length us, event | category | flops | bytes accessed | tf_op | source)
XLA Modules:
  0.0 234.0 jit_solution(17793523784122323694)
XLA Ops:
  6.5 1.0 dynamic-slice_bitcast_fusion
  7.5 10.8 %all_to_all.15 = bf16[4,40,1152]{2,1,0:T(8,128)(2,1)} all-to-all(bf16[4,40,1152]{2,1,0:T(8,128)(2,1)S(1)} %broadcast_in_dim.68), channel_id=1, replica_groups=mesh['z'=8,'core'=2,'y'=8,'x'=4] {'x'}, dimensions={0} | all-to-all | bytes 737280 | tf_op jit(solution)/shard_map/all_to_all | solution.py:289
  18.8 1.2 constant_dynamic-slice_fusion
  20.6 0.7 pad_convert_fusion
  21.3 0.7 fusion.22
  22.0 5.0 %collective-permute-start.3 = (f32[12,128]{1,0:T(8,128)S(1)}, f32[12,128]{1,0:T(8,128)S(1)}, u32[]{:S(2)}, u32[]{:S(2)}) collective-permute-start(f32[12,128]{1,0:T(8,128)S(1)} %get-tuple-element.36), channel_id=1, source_target_pairs={{0,8},{4,28},{8,16},{12,4},{16,24},{20,12},{24,0},{28,20},{1,9},{5... | collective-permute-start | bytes 18440 | tf_op jit(solution)/shard_map/ppermute | solution.py:309
  27.0 4.6 %collective-permute-start.2 = (f32[12,128]{1,0:T(8,128)S(1)}, f32[12,128]{1,0:T(8,128)S(1)}, u32[]{:S(2)}, u32[]{:S(2)}) collective-permute-start(f32[12,128]{1,0:T(8,128)S(1)} %get-tuple-element.36), channel_id=1, source_target_pairs={{0,28},{4,0},{8,4},{12,8},{16,12},{20,16},{24,20},{28,24},{1,29},{... | collective-permute-start | bytes 18440 | tf_op jit(solution)/shard_map/ppermute | solution.py:309
  31.7 1.9 collective-permute-start.1
  33.6 1.2 concatenate.16
  34.8 4.4 %collective-permute-start = (bf16[80,2112]{1,0:T(8,128)(2,1)S(1)}, bf16[80,2112]{1,0:T(8,128)(2,1)S(1)}, u32[]{:S(2)}, u32[]{:S(2)}) collective-permute-start(bf16[80,2112]{1,0:T(8,128)(2,1)S(1)} %concatenate.16), channel_id=1, source_target_pairs={{0,16},{4,20},{8,24},{12,28},{16,0},{20,4},{24,8},{28,12},{1,17},{... | collective-permute-start | bytes 1013768 | tf_op jit(solution)/shard_map/ppermute | solution.py:300
  39.2 7.1 %fusion.27 = (f32[8,484]{1,0:T(8,128)S(1)}, f32[8,484,484]{1,2,0:T(8,128)}) fusion(bf16[484,8,72]{0,2,1:T(8,128)(2,1)} %bitcast.66, bf16[484,8,72]{0,2,1:T(8,128)(2,1)} %bitcast.67), kind=kOutput, calls=%fused_computation.46 | convolution fusion | flops 275485536 | bytes 8626816 | tf_op jit(solution)/shard_map/sub | solution.py:29
  46.3 4.2 %fusion.7 = bf16[8,484,72]{1,2,0:T(8,128)(2,1)S(1)} fusion(bf16[484,8,72]{0,2,1:T(8,128)(2,1)S(1)} %bitcast.68, f32[8,484,484]{1,2,0:T(8,128)} %get-tuple-element.38, f32[8,484]{1,0:T(8,128)S(1)} %get-tuple-element.37), kind=kOutput, calls=%fused_computation.9 | convolution fusion | flops 273889792 | bytes 8626816 | tf_op jit(solution)/shard_map/hqk,khd->qhd/dot_general | solution.py:31
  50.5 0.7 fusion.8
  51.2 0.3 copy.35
  51.5 0.8 select_n.66
  52.3 0.4 copy.36
  52.8 1.1 select_n.68
  53.9 0.9 pad.12.merged_ref
  55.4 0.2 copy.37
  56.0 6.6 %collective-permute-done = bf16[80,2112]{1,0:T(8,128)(2,1)S(1)} collective-permute-done((bf16[80,2112]{1,0:T(8,128)(2,1)S(1)}, bf16[80,2112]{1,0:T(8,128)(2,1)S(1)}, u32[]{:S(2)}, u32[]{:S(2)}) %collective-permute-start) | collective-permute-done | bytes 337952 | tf_op jit(solution)/shard_map/ppermute | solution.py:300
  62.7 1.0 concatenate.19
  63.8 21.9 %all-gather.3.cloned.1.call-done = bf16[2560,1152]{1,0:T(8,128)(2,1)} async-done(((bf16[160,1152]{1,0:T(8,128)(2,1)}), bf16[2560,1152]{1,0:T(8,128)(2,1)}) %all-gather.3.cloned.1.call-update) | async-done | bytes 5898256 | tf_op jit(solution)/shard_map/all_gather | solution.py:296
  85.7 6.3 %merge.1.tile_ref = bf16[128,1280]{1,0:T(8,128)(2,1)} custom-call(bf16[128,2304]{1,0:T(8,128)(2,1)} %pad.12.merged_ref, bf16[2,1280,1152]{2,1,0:T(8,128)(2,1)} %bitcast.54), custom_call_target="tpu_custom_call" | custom-call | flops 754974720 | bytes 7340032 | tf_op jit(solution)/shard_map/merge/pallas_call | solution.py:94
  92.0 3.2 %collective-permute-start.6 = (bf16[128,1280]{1,0:T(8,128)(2,1)}, bf16[128,1280]{1,0:T(8,128)(2,1)S(1)}, u32[]{:S(2)}, u32[]{:S(2)}) collective-permute-start(bf16[128,1280]{1,0:T(8,128)(2,1)} %merge.1.tile_ref), channel_id=1, source_target_pairs={{0,4},{4,8},{8,12},{12,16},{16,20},{20,24},{24,28},{28,0},{1,5},{5... | collective-permute-start | bytes 983048 | tf_op jit(solution)/shard_map/ppermute | solution.py:327
  95.2 3.3 %collective-permute-start.5 = (bf16[128,1280]{1,0:T(8,128)(2,1)}, bf16[128,1280]{1,0:T(8,128)(2,1)S(1)}, u32[]{:S(2)}, u32[]{:S(2)}) collective-permute-start(bf16[128,1280]{1,0:T(8,128)(2,1)} %merge.1.tile_ref), channel_id=1, source_target_pairs={{0,28},{4,0},{8,4},{12,8},{16,12},{20,16},{24,20},{28,24},{1,29},{... | collective-permute-start | bytes 983048 | tf_op jit(solution)/shard_map/ppermute | solution.py:327
  98.5 2.4 %collective-permute-start.4 = (bf16[128,1280]{1,0:T(8,128)(2,1)}, bf16[128,1280]{1,0:T(8,128)(2,1)S(1)}, u32[]{:S(2)}, u32[]{:S(2)}) collective-permute-start(bf16[128,1280]{1,0:T(8,128)(2,1)} %merge.1.tile_ref), channel_id=1, source_target_pairs={{0,8},{4,28},{8,16},{12,4},{16,24},{20,12},{24,0},{28,20},{1,9},{5... | collective-permute-start | bytes 983048 | tf_op jit(solution)/shard_map/ppermute | solution.py:327
  101.1 1.0 copy-done.1
  102.1 1.2 pick_rows.4.refs_0_
  103.2 1.1 collective-permute-done.6.tile_ref
  104.4 1.2 pick_rows.5.refs_0_
  105.5 0.6 collective-permute-done.5.tile_ref
  106.1 1.2 pick_rows.6.refs_0_
  107.4 3.9 %collective-permute-done.4.tile_ref = bf16[128,1280]{1,0:T(8,128)(2,1)S(1)} collective-permute-done((bf16[128,1280]{1,0:T(8,128)(2,1)}, bf16[128,1280]{1,0:T(8,128)(2,1)S(1)}, u32[]{:S(2)}, u32[]{:S(2)}) %collective-permute-start.4) | collective-permute-done | bytes 327712 | tf_op jit(solution)/shard_map/ppermute | solution.py:327
  111.2 1.2 pick_rows.7
  112.4 4.8 %all-to-all-start.1 = ((bf16[4,256,1280]{2,1,0:T(8,128)(2,1)}), bf16[4,256,1280]{2,1,0:T(8,128)(2,1)}, u32[]{:S(2)}, u32[]{:S(2)}) async-start(bf16[4,256,1280]{2,1,0:T(8,128)(2,1)} %bitcast.27), calls=%async_computation.1 | async-start | bytes 5242880 | tf_op jit(solution)/shard_map/all_to_all | solution.py:332
  117.2 28.9 %all-to-all-done.1 = bf16[4,256,1280]{2,1,0:T(8,128)(2,1)} async-done(((bf16[4,256,1280]{2,1,0:T(8,128)(2,1)}), bf16[4,256,1280]{2,1,0:T(8,128)(2,1)}, u32[]{:S(2)}, u32[]{:S(2)}) %all-to-all-start.1) | async-done | bytes 2621472 | tf_op jit(solution)/shard_map/all_to_all | solution.py:332
  146.2 11.5 %all-gather.5.cloned.1.call-done.weight_hbm = bf16[1280,4224]{1,0:T(8,128)(2,1)} async-done(((bf16[80,4224]{1,0:T(8,128)(2,1)}), bf16[1280,4224]{1,0:T(8,128)(2,1)}) %all-gather.5.cloned.1.call-update) | async-done | bytes 10813456 | tf_op jit(solution)/shard_map/all_gather | solution.py:323
  157.7 12.5 %expert_ffn.1 = bf16[4,2,128,1280]{3,2,1,0:T(8,128)(2,1)S(1)} custom-call(bf16[4,2,128,1280]{3,2,1,0:T(8,128)(2,1)} %bitcast.28.rows, f32[1,1280]{1,0:T(1,128)S(1)} %broadcast_in_dim.80.gain_ref, bf16[1280,4224]{1,0:T(8,128)(2,1)} %all-gather.5.cloned.1.call-done.weight_hbm), custom_call_target="tpu_custom_call" | custom-call | flops 5536481280 | bytes 16777216 | tf_op jit(solution)/shard_map/expert_ffn/pallas_call | solution.py:214
  170.2 35.3 %all_to_all.16 = bf16[4,256,1280]{2,1,0:T(8,128)(2,1)S(1)} all-to-all(bf16[4,256,1280]{2,1,0:T(8,128)(2,1)S(1)} %bitcast.53), channel_id=1, replica_groups=mesh['z'=8,'core'=2,'y'=8,'x'=4] {'x'}, dimensions={0} | all-to-all | bytes 5242880 | tf_op jit(solution)/shard_map/all_to_all | solution.py:339
  205.5 0.3 combine.7
  205.9 0.3 combine.6
  206.2 0.3 combine.5
  206.6 5.3 %collective-permute-start.9 = (bf16[128,1280]{1,0:T(8,128)(2,1)S(1)}, bf16[128,1280]{1,0:T(8,128)(2,1)S(1)}, u32[]{:S(2)}, u32[]{:S(2)}) collective-permute-start(bf16[128,1280]{1,0:T(8,128)(2,1)S(1)} %combine.7), channel_id=1, source_target_pairs={{8,0},{28,4},{16,8},{4,12},{24,16},{12,20},{0,24},{20,28},{9,1},{2... | collective-permute-start | bytes 983048 | tf_op jit(solution)/shard_map/ppermute | solution.py:342
  211.9 1.9 collective-permute-start.8
  213.8 4.6 %collective-permute-start.7 = (bf16[128,1280]{1,0:T(8,128)(2,1)S(1)}, bf16[128,1280]{1,0:T(8,128)(2,1)S(1)}, u32[]{:S(2)}, u32[]{:S(2)}) collective-permute-start(bf16[128,1280]{1,0:T(8,128)(2,1)S(1)} %combine.5), channel_id=1, source_target_pairs={{4,0},{8,4},{12,8},{16,12},{20,16},{24,20},{28,24},{0,28},{5,1},{9... | collective-permute-start | bytes 983048 | tf_op jit(solution)/shard_map/ppermute | solution.py:342
  218.4 0.3 combine.4
  218.8 7.5 %collective-permute-done.8 = bf16[128,1280]{1,0:T(8,128)(2,1)S(1)} collective-permute-done((bf16[128,1280]{1,0:T(8,128)(2,1)S(1)}, bf16[128,1280]{1,0:T(8,128)(2,1)S(1)}, u32[]{:S(2)}, u32[]{:S(2)}) %collective-permute-start.8) | collective-permute-done | bytes 327712 | tf_op jit(solution)/shard_map/ppermute | solution.py:342
  226.3 0.9 fusion.15
  (47 shorter events, 1.6 us)
Async XLA Ops:
  6.5 44.0 %copy-start = (bf16[576,576]{1,0:T(8,128)(2,1)S(1)}, bf16[576,576]{1,0:T(8,128)(2,1)}, u32[]{:S(2)}) copy-start(bf16[576,576]{1,0:T(8,128)(2,1)} %param.17) | copy-start | bytes 1990660
  6.5 79.2 %all-gather.3.cloned.1.call-start = ((), (), s32[]{:S(2)}) async-start(), calls=%async_computation.3 | async-start | bytes 6266880 | tf_op jit(solution)/shard_map/all_gather | solution.py:296
  18.4 27.9 %copy-start.4 = (bf16[484,576]{0,1:T(8,128)(2,1)S(1)}, bf16[484,576]{0,1:T(8,128)(2,1)}, u32[]{:S(2)}) copy-start(bf16[484,576]{0,1:T(8,128)(2,1)} %param.15) | copy-start | bytes 1672708
  18.4 139.3 %all-gather.5.cloned.1.call-start = ((), (), s32[]{:S(2)}) async-start(), calls=%async_computation.4 | async-start | bytes 11489280 | tf_op jit(solution)/shard_map/all_gather | solution.py:323
  22.0 32.7 %collective-permute-start.3 = (f32[12,128]{1,0:T(8,128)S(1)}, f32[12,128]{1,0:T(8,128)S(1)}, u32[]{:S(2)}, u32[]{:S(2)}) collective-permute-start(f32[12,128]{1,0:T(8,128)S(1)} %get-tuple-element.36), channel_id=1, source_target_pairs={{0,8},{4,28},{8,16},{12,4},{16,24},{20,12},{24,0},{28,20},{1,9},{5... | collective-permute-start | bytes 18440 | tf_op jit(solution)/shard_map/ppermute | solution.py:309
  27.0 27.7 %collective-permute-start.2 = (f32[12,128]{1,0:T(8,128)S(1)}, f32[12,128]{1,0:T(8,128)S(1)}, u32[]{:S(2)}, u32[]{:S(2)}) collective-permute-start(f32[12,128]{1,0:T(8,128)S(1)} %get-tuple-element.36), channel_id=1, source_target_pairs={{0,28},{4,0},{8,4},{12,8},{16,12},{20,16},{24,20},{28,24},{1,29},{... | collective-permute-start | bytes 18440 | tf_op jit(solution)/shard_map/ppermute | solution.py:309
  31.7 23.1 %collective-permute-start.1 = (f32[12,128]{1,0:T(8,128)S(1)}, f32[12,128]{1,0:T(8,128)S(1)}, u32[]{:S(2)}, u32[]{:S(2)}) collective-permute-start(f32[12,128]{1,0:T(8,128)S(1)} %get-tuple-element.36), channel_id=1, source_target_pairs={{0,4},{4,8},{8,12},{12,16},{16,20},{20,24},{24,28},{28,0},{1,5},{5... | collective-permute-start | bytes 18440 | tf_op jit(solution)/shard_map/ppermute | solution.py:309
  34.8 27.8 %collective-permute-start = (bf16[80,2112]{1,0:T(8,128)(2,1)S(1)}, bf16[80,2112]{1,0:T(8,128)(2,1)S(1)}, u32[]{:S(2)}, u32[]{:S(2)}) collective-permute-start(bf16[80,2112]{1,0:T(8,128)(2,1)S(1)} %concatenate.16), channel_id=1, source_target_pairs={{0,16},{4,20},{8,24},{12,28},{16,0},{20,4},{24,8},{28,12},{1,17},{... | collective-permute-start | bytes 1013768 | tf_op jit(solution)/shard_map/ppermute | solution.py:300
  46.3 4.2 %copy-start.5 = (bf16[484,576]{0,1:T(8,128)(2,1)S(1)}, bf16[484,576]{0,1:T(8,128)(2,1)}, u32[]{:S(2)}) copy-start(bf16[484,576]{0,1:T(8,128)(2,1)} %param.16) | copy-start | bytes 1672708
  92.0 12.4 %collective-permute-start.6 = (bf16[128,1280]{1,0:T(8,128)(2,1)}, bf16[128,1280]{1,0:T(8,128)(2,1)S(1)}, u32[]{:S(2)}, u32[]{:S(2)}) collective-permute-start(bf16[128,1280]{1,0:T(8,128)(2,1)} %merge.1.tile_ref), channel_id=1, source_target_pairs={{0,4},{4,8},{8,12},{12,16},{16,20},{20,24},{24,28},{28,0},{1,5},{5... | collective-permute-start | bytes 983048 | tf_op jit(solution)/shard_map/ppermute | solution.py:327
  95.2 10.9 %collective-permute-start.5 = (bf16[128,1280]{1,0:T(8,128)(2,1)}, bf16[128,1280]{1,0:T(8,128)(2,1)S(1)}, u32[]{:S(2)}, u32[]{:S(2)}) collective-permute-start(bf16[128,1280]{1,0:T(8,128)(2,1)} %merge.1.tile_ref), channel_id=1, source_target_pairs={{0,28},{4,0},{8,4},{12,8},{16,12},{20,16},{24,20},{28,24},{1,29},{... | collective-permute-start | bytes 983048 | tf_op jit(solution)/shard_map/ppermute | solution.py:327
  98.5 12.7 %collective-permute-start.4 = (bf16[128,1280]{1,0:T(8,128)(2,1)}, bf16[128,1280]{1,0:T(8,128)(2,1)S(1)}, u32[]{:S(2)}, u32[]{:S(2)}) collective-permute-start(bf16[128,1280]{1,0:T(8,128)(2,1)} %merge.1.tile_ref), channel_id=1, source_target_pairs={{0,8},{4,28},{8,16},{12,4},{16,24},{20,12},{24,0},{28,20},{1,9},{5... | collective-permute-start | bytes 983048 | tf_op jit(solution)/shard_map/ppermute | solution.py:327
  101.1 1.0 copy-start.1
  107.4 9.9 %copy-start.3 = (f32[1280]{0:T(1024)S(1)}, f32[1280]{0:T(1024)}, u32[]{:S(2)}) copy-start(f32[1280]{0:T(1024)} %param.19) | copy-start | bytes 15364
  112.4 33.7 %all-to-all-start.1 = ((bf16[4,256,1280]{2,1,0:T(8,128)(2,1)}), bf16[4,256,1280]{2,1,0:T(8,128)(2,1)}, u32[]{:S(2)}, u32[]{:S(2)}) async-start(bf16[4,256,1280]{2,1,0:T(8,128)(2,1)} %bitcast.27), calls=%async_computation.1 | async-start | bytes 5242880 | tf_op jit(solution)/shard_map/all_to_all | solution.py:332
  205.8 20.4 %copy-start.2 = (bf16[128,1280]{1,0:T(8,128)(2,1)S(1)}, bf16[128,1280]{1,0:T(8,128)(2,1)}, u32[]{:S(2)}) copy-start(bf16[128,1280]{1,0:T(8,128)(2,1)} %merge.1.tile_ref) | copy-start | bytes 983044
  206.6 12.2 %collective-permute-start.9 = (bf16[128,1280]{1,0:T(8,128)(2,1)S(1)}, bf16[128,1280]{1,0:T(8,128)(2,1)S(1)}, u32[]{:S(2)}, u32[]{:S(2)}) collective-permute-start(bf16[128,1280]{1,0:T(8,128)(2,1)S(1)} %combine.7), channel_id=1, source_target_pairs={{8,0},{28,4},{16,8},{4,12},{24,16},{12,20},{0,24},{20,28},{9,1},{2... | collective-permute-start | bytes 983048 | tf_op jit(solution)/shard_map/ppermute | solution.py:342
  211.9 14.3 %collective-permute-start.8 = (bf16[128,1280]{1,0:T(8,128)(2,1)S(1)}, bf16[128,1280]{1,0:T(8,128)(2,1)S(1)}, u32[]{:S(2)}, u32[]{:S(2)}) collective-permute-start(bf16[128,1280]{1,0:T(8,128)(2,1)S(1)} %combine.6), channel_id=1, source_target_pairs={{28,0},{0,4},{4,8},{8,12},{12,16},{16,20},{20,24},{24,28},{29,1},{... | collective-permute-start | bytes 983048 | tf_op jit(solution)/shard_map/ppermute | solution.py:342
  213.8 12.4 %collective-permute-start.7 = (bf16[128,1280]{1,0:T(8,128)(2,1)S(1)}, bf16[128,1280]{1,0:T(8,128)(2,1)S(1)}, u32[]{:S(2)}, u32[]{:S(2)}) collective-permute-start(bf16[128,1280]{1,0:T(8,128)(2,1)S(1)} %combine.5), channel_id=1, source_target_pairs={{4,0},{8,4},{12,8},{16,12},{20,16},{24,20},{28,24},{0,28},{5,1},{9... | collective-permute-start | bytes 983048 | tf_op jit(solution)/shard_map/ppermute | solution.py:342
Sparse Core Ops, SparseCore 0:
  18.5 67.1 all-gather.2
  87.8 69.8 all-gather.4
